TPU v7x, 32 devices: a whole 2x2x4 slice. The times are simulated.
32 devices in a mesh: groups: 2 (over y), xt: 4 (over z), yt: 2 (over x), sg: 2 (over core).
Axes of the slice: x: 2, y: 2, z: 4, core: 2. Of those that a mesh axis runs over, the one named last changes fastest.
Arguments:
- field: float32 [2, 2048, 512], P(None, ('groups', 'xt'), 'yt'), parts along dimension 1, may hold values from -6 to 6
- probe: bfloat16 [8, 2, 256, 256], P('groups'), parts along dimension 0, may hold values from -3 to 3
- amplitudes: bfloat16 [8, 2, 6, 256, 256], P(('groups', 'xt'), 'yt', 'sg'), parts along dimension 0, may hold values from 0.25 to 2.5
- offsets: int32 [8, 2, 6, 2], P(('groups', 'xt'), 'yt', 'sg'), parts along dimension 0, may hold values from 0 to 256, as said below
- counts: int32 [8, 2], P(('groups', 'xt'), 'yt'), parts along dimension 0, may hold values from 1 to 6, as said below
Outputs:
- new_field: float32 [2, 2048, 512], P(None, ('groups', 'xt', 'sg'), 'yt'), parts along dimension 1
- new_probe: float32 [8, 2, 256, 256], P('groups'), parts along dimension 0
There are 2 independent parts, one for each index of `groups`. A program takes and returns all parts, laid end to end along the dimension named above; each array names one. Nothing has to cross between parts.
Inputs may be any that keep to these rules, and one draw needn't show every extreme that they name: `offsets`: each scan window lies within the tile extended by 128 pixels on every side. `counts`: the live scans of a tile are its first slots.
All inputs are finite; a program needn't handle non-finite values.
Results may differ from a plain program's by a relative error of at most 0.0077.
Values sent between devices are 32-bit elements; how exact they have to be, the bound alone decides.
No kernel may reach another device: no remote copies, remote signals or barrier semaphores. Data moves between devices by JAX's collectives and lax.ppermute only.
A program may use at most 64 MiB of HBM per device.

v0:
```python
import math

import jax
import jax.numpy as jnp
from jax import lax
from jax.sharding import PartitionSpec as P

floor_term = 0.5
field_rate = 0.25
probe_rate = 0.1


def with_halo(block, sides, width):
    for axis, dim in sides:
        count = lax.axis_size(axis)
        forward = [(i, i + 1) for i in range(count - 1)]
        backward = [(target, source) for source, target in forward]
        low = lax.ppermute(
            lax.slice_in_dim(block, block.shape[dim] - width, None, axis=dim), axis, forward
        )
        high = lax.ppermute(lax.slice_in_dim(block, 0, width, axis=dim), axis, backward)
        block = jnp.concatenate([low, block, high], axis=dim)
    return block


def swapped(block, axis, stride):
    count = lax.axis_size(axis)
    route = []
    for low in range(count):
        high = low | 1 << stride
        if high != low and high < count:
            route += [(low, high), (high, low)]
    return lax.ppermute(block, axis, route)


def dft_tables(width):
    index = jnp.arange(width, dtype=jnp.int32)
    phase = index[:, None] * index[None, :] % width
    angle = phase.astype(jnp.float32) * (2.0 * math.pi / width)
    return (jnp.cos(angle).astype(jnp.bfloat16), jnp.sin(angle).astype(jnp.bfloat16))


def on_left(table, values):
    return jnp.einsum("kn,mnj->mkj", table, values, preferred_element_type=jnp.float32)


def on_right(values, table):
    return jnp.einsum("mkn,nj->mkj", values, table, preferred_element_type=jnp.float32)


def scan_terms(probe_real, probe_imag, patch, amplitude, cosine, sine, width):
    patch_real = patch[0]
    patch_imag = patch[1]
    psi_real = (probe_real * patch_real - probe_imag * patch_imag).astype(jnp.bfloat16)
    psi_imag = (probe_real * patch_imag + probe_imag * patch_real).astype(jnp.bfloat16)
    left_real = (on_left(cosine, psi_real) + on_left(sine, psi_imag)).astype(jnp.bfloat16)
    left_imag = (on_left(cosine, psi_imag) - on_left(sine, psi_real)).astype(jnp.bfloat16)
    far_real = (on_right(left_real, cosine) + on_right(left_imag, sine)) / width
    far_imag = (on_right(left_imag, cosine) - on_right(left_real, sine)) / width
    inten = jnp.sum(far_real * far_real + far_imag * far_imag, axis=0)
    factor = 1.0 - amplitude / jnp.sqrt(inten + floor_term)
    chi_real = (far_real * factor).astype(jnp.bfloat16)
    chi_imag = (far_imag * factor).astype(jnp.bfloat16)
    back_real = (on_left(cosine, chi_real) - on_left(sine, chi_imag)).astype(jnp.bfloat16)
    back_imag = (on_left(cosine, chi_imag) + on_left(sine, chi_real)).astype(jnp.bfloat16)
    grad_real = (on_right(back_real, cosine) - on_right(back_imag, sine)) / width
    grad_imag = (on_right(back_imag, cosine) + on_right(back_real, sine)) / width
    patch_grad = jnp.stack(
        [
            jnp.sum(probe_real * grad_real + probe_imag * grad_imag, axis=0),
            jnp.sum(probe_real * grad_imag - probe_imag * grad_real, axis=0),
        ]
    )
    probe_term = jnp.stack(
        [
            patch_real * grad_real + patch_imag * grad_imag,
            patch_real * grad_imag - patch_imag * grad_real,
        ],
        axis=1,
    )
    return (patch_grad, probe_term)


def fold_back(grad_pad, tile, half):
    row_strips = jnp.concatenate([grad_pad[:, :half], grad_pad[:, tile + half :]], axis=1)
    row_wider = with_halo(row_strips, (("xt", 1),), half)
    middle = grad_pad[:, half : tile + half]
    middle = middle.at[:, :half].add(row_wider[:, :half])
    middle = middle.at[:, tile - half :].add(row_wider[:, 3 * half :])
    col_strips = jnp.concatenate([middle[:, :, :half], middle[:, :, tile + half :]], axis=2)
    col_wider = with_halo(col_strips, (("yt", 2),), half)
    inner = middle[:, :, half : tile + half]
    inner = inner.at[:, :, :half].add(col_wider[:, :, :half])
    inner = inner.at[:, :, tile - half :].add(col_wider[:, :, 3 * half :])
    return inner


def shards(field, probe, amplitudes, offsets, counts):
    width = probe.shape[-1]
    half = width // 2
    tile = field.shape[1]
    per_device = amplitudes.shape[2]
    padded = with_halo(field, (("xt", 1), ("yt", 2)), half)
    cosine, sine = dft_tables(width)
    probe_real = probe[:, 0]
    probe_imag = probe[:, 1]
    group_index = lax.axis_index("sg")
    first_slot = group_index * per_device
    live = jnp.clip(counts[0, 0] - first_slot, 0, per_device)
    zero_index = jnp.zeros((), jnp.int32)
    own_amplitudes = amplitudes[0, 0]
    own_offsets = offsets[0, 0]

    def visit(slot, carry):
        grad_pad, probe_grad = carry
        anchor_row = own_offsets[slot, 0]
        anchor_col = own_offsets[slot, 1]
        patch = lax.dynamic_slice(padded, (zero_index, anchor_row, anchor_col), (2, width, width))
        amplitude = lax.dynamic_index_in_dim(own_amplitudes, slot, 0, keepdims=False)
        patch_grad, probe_term = scan_terms(
            probe_real, probe_imag, patch, amplitude, cosine, sine, width
        )
        current = lax.dynamic_slice(
            grad_pad, (zero_index, anchor_row, anchor_col), (2, width, width)
        )
        grad_pad = lax.dynamic_update_slice(
            grad_pad, current + patch_grad, (zero_index, anchor_row, anchor_col)
        )
        return (grad_pad, probe_grad + probe_term)

    start = (jnp.zeros(padded.shape, jnp.float32), jnp.zeros(probe.shape, jnp.float32))
    grad_pad, probe_grad = lax.fori_loop(0, live, visit, start)
    grad_pad = grad_pad + swapped(grad_pad, "sg", 0)
    field_grad = fold_back(grad_pad, tile, half)
    probe_total = lax.psum(probe_grad, ("xt", "yt", "sg"))
    share = tile // lax.axis_size("sg")
    row_start = group_index * share
    own_field = lax.dynamic_slice_in_dim(field, row_start, share, 1)
    own_grad = lax.dynamic_slice_in_dim(field_grad, row_start, share, 1)
    new_field = own_field - field_rate * own_grad
    new_probe = probe.astype(jnp.float32) - probe_rate * probe_total
    return (new_field, new_probe)


def solution(mesh):
    in_specs = (
        P(None, ("groups", "xt"), "yt"),
        P("groups", None, None, None),
        P(("groups", "xt"), "yt", "sg", None, None),
        P(("groups", "xt"), "yt", "sg", None),
        P(("groups", "xt"), "yt"),
    )
    out_specs = (P(None, ("groups", "xt", "sg"), "yt"), P("groups", None, None, None))
    return jax.shard_map(shards, mesh=mesh, in_specs=in_specs, out_specs=out_specs, check_vma=False)
```

profile of v0, /device:TPU:0, one launch (start us, length us, event | category | flops | bytes accessed | tf_op | source)
XLA Modules:
  0.0 291.4 jit_solution(5719988131149152508)
XLA Ops:
  8.3 4.9 %collective-permute-start = (f32[2,128,256]{2,1,0:T(8,128)S(1)}, f32[2,128,256]{2,1,0:T(8,128)S(1)}, u32[]{:S(2)}, u32[]{:S(2)}) collective-permute-start(f32[2,128,256]{2,1,0:T(8,128)S(1)} %get-tuple-element.260), channel_id=1, source_target_pairs={{0,4},{4,8},{8,12},{1,5},{5,9},{9,13},{2,6},{6,10},{10,14},{3,7},{... | collective-permute-start | bytes 786440 | tf_op jit(solution)/shard_map/ppermute | solution.py:18
  13.2 1.4 collective-permute-start.1
  14.7 4.1 %collective-permute-done = f32[2,128,256]{2,1,0:T(8,128)S(1)} collective-permute-done((f32[2,128,256]{2,1,0:T(8,128)S(1)}, f32[2,128,256]{2,1,0:T(8,128)S(1)}, u32[]{:S(2)}, u32[]{:S(2)}) %collective-permute-start) | collective-permute-done | bytes 262176 | tf_op jit(solution)/shard_map/ppermute | solution.py:18
  19.9 3.2 %collective-permute-done.1 = f32[2,128,256]{2,1,0:T(8,128)S(1)} collective-permute-done((f32[2,128,256]{2,1,0:T(8,128)S(1)}, f32[2,128,256]{2,1,0:T(8,128)S(1)}, u32[]{:S(2)}, u32[]{:S(2)}) %collective-permute-start.1) | collective-permute-done | bytes 262176 | tf_op jit(solution)/shard_map/ppermute | solution.py:21
  24.1 4.2 %collective-permute-start.2 = (f32[2,512,128]{2,1,0:T(8,128)}, f32[2,512,128]{2,1,0:T(8,128)}, u32[]{:S(2)}, u32[]{:S(2)}) collective-permute-start(f32[2,512,128]{2,1,0:T(8,128)} %get-tuple-element.257), channel_id=1, source_target_pairs={{0,2},{1,3},{4,6},{5,7},{8,10},{9,11},{12,14},{13,15},{16,18},{17,... | collective-permute-start | bytes 1572872 | tf_op jit(solution)/shard_map/ppermute | solution.py:18
  30.4 7.5 %collective-permute-done.2 = f32[2,512,128]{2,1,0:T(8,128)} collective-permute-done((f32[2,512,128]{2,1,0:T(8,128)}, f32[2,512,128]{2,1,0:T(8,128)}, u32[]{:S(2)}, u32[]{:S(2)}) %collective-permute-start.2) | collective-permute-done | bytes 524320 | tf_op jit(solution)/shard_map/ppermute | solution.py:18
  37.8 4.9 %collective-permute-done.3 = f32[2,512,128]{2,1,0:T(8,128)} collective-permute-done((f32[2,512,128]{2,1,0:T(8,128)}, f32[2,512,128]{2,1,0:T(8,128)}, u32[]{:S(2)}, u32[]{:S(2)}) %collective-permute-start.3) | collective-permute-done | bytes 524320 | tf_op jit(solution)/shard_map/ppermute | solution.py:21
  42.7 2.7 pad_maximum_fusion
  45.5 1.5 broadcast_in_dim.5
  47.0 1.6 broadcast_in_dim.4
  48.6 39.8 %while.18 = (s32[]{:T(128)}, f32[2,512,512]{2,1,0:T(8,128)}, f32[4,2,256,256]{3,2,0,1:T(8,128)}, s32[]{:T(128)}, s32[3,2]{0,1:T(2,128)S(1)}, /*index=5*/bf16[4,2...) while((s32[]{:T(128)}, f32[2,512,512]{2,1,0:T(8,128)}, ...), condition=%wide.region_4.5_spmd.clone.clone, body=%wide.region_0.4_spmd.clone.clone.sunk | while | flops 2182610944 | bytes 55443756 | solution.py:132
  74.7 1.8 add_bitcast_fusion.2
  76.6 2.2 maximum_add_fusion.4
  78.7 6.4 %dynamic_update_slice.6 = f32[2,512,512]{2,1,0:T(8,128)} dynamic-update-slice(f32[2,512,512]{2,1,0:T(8,128)} %get-tuple-element.356, f32[2,256,256]{2,1,0:T(8,128)} %maximum_add_fusion.4, s32[]{:T(128)} %constant.151.clone.1..sunk, s32[]{:T(128)S(6)} %select_n.138, s32[]{:T(128)S(6)} %select_n.139) | dynamic-update-slice | bytes 1048580 | tf_op jit(solution)/shard_map/while/body/dynamic_update_slice | solution.py:126
  85.2 3.2 %maximum_add_fusion.5 = f32[4,2,256,256]{3,2,0,1:T(8,128)} fusion(f32[4,2,256,256]{3,2,0,1:T(8,128)} %get-tuple-element.357, f32[4,1,256,256]{3,2,0,1:T(8,128)S(1)} %get-tuple-element.339, f32[4,1,256,256]{3,2,0,1:T(8,128)S(1)} %get-tuple-element.340), kind=kLoop, calls=%fused_computation.2.clone.1 | loop fusion | flops 1048576 | bytes 6291456 | tf_op jit(solution)/shard_map/while/body/add | solution.py:129
  88.4 4.4 %collective-permute-done.4 = f32[2,512,512]{2,1,0:T(8,128)S(1)} collective-permute-done((f32[2,512,512]{2,1,0:T(8,128)}, f32[2,512,512]{2,1,0:T(8,128)S(1)}, u32[]{:S(2)}, u32[]{:S(2)}) %collective-permute-start.4) | collective-permute-done | bytes 2097184 | tf_op jit(solution)/shard_map/ppermute | solution.py:33
  92.7 2.1 add.137
  95.9 84.0 %collective-permute-start.5 = (f32[2,128,512]{2,1,0:T(8,128)}, f32[2,128,512]{2,1,0:T(8,128)}, u32[]{:S(2)}, u32[]{:S(2)}) collective-permute-start(f32[2,128,512]{2,1,0:T(8,128)} %get-tuple-element.252), channel_id=1, source_target_pairs={{0,4},{4,8},{8,12},{1,5},{5,9},{9,13},{2,6},{6,10},{10,14},{3,7},{... | collective-permute-start | bytes 1572872 | tf_op jit(solution)/shard_map/ppermute | solution.py:18
  179.9 1.5 copy.25
  182.7 14.1 %collective-permute-done.5 = f32[2,128,512]{2,1,0:T(8,128)} collective-permute-done((f32[2,128,512]{2,1,0:T(8,128)}, f32[2,128,512]{2,1,0:T(8,128)}, u32[]{:S(2)}, u32[]{:S(2)}) %collective-permute-start.5) | collective-permute-done | bytes 524320 | tf_op jit(solution)/shard_map/ppermute | solution.py:18
  198.0 9.8 %collective-permute-done.6 = f32[2,128,512]{2,1,0:T(8,128)} collective-permute-done((f32[2,128,512]{2,1,0:T(8,128)}, f32[2,128,512]{2,1,0:T(8,128)}, u32[]{:S(2)}, u32[]{:S(2)}) %collective-permute-start.6) | collective-permute-done | bytes 524320 | tf_op jit(solution)/shard_map/ppermute | solution.py:21
  210.3 4.6 %collective-permute-start.7 = (f32[2,256,128]{2,1,0:T(8,128)S(1)}, f32[2,256,128]{2,1,0:T(8,128)S(1)}, u32[]{:S(2)}, u32[]{:S(2)}) collective-permute-start(f32[2,256,128]{2,1,0:T(8,128)S(1)} %get-tuple-element.254), channel_id=1, source_target_pairs={{0,2},{1,3},{4,6},{5,7},{8,10},{9,11},{12,14},{13,15},{16,18},{17,... | collective-permute-start | bytes 786440 | tf_op jit(solution)/shard_map/ppermute | solution.py:18
  214.9 64.4 %all-reduce.2.cloned.1.call-done = f32[4,2,256,256]{3,2,1,0:T(8,128)} async-done(((f32[4,2,256,256]{3,2,1,0:T(8,128)}), f32[4,2,256,256]{3,2,1,0:T(8,128)}) %all-reduce.2.cloned.1.call-update) | async-done | bytes 2097168 | tf_op jit(solution)/shard_map/psum | solution.py:135
  279.3 3.4 %multiply_subtract_fusion = f32[4,2,256,256]{3,2,1,0:T(8,128)} fusion(f32[4,2,256,256]{3,2,1,0:T(8,128)} %all-reduce.2.cloned.1.call-done, bf16[4,2,256,256]{3,2,1,0:T(8,128)(2,1)} %param.16), kind=kLoop, calls=%fused_computation.137 | loop fusion | flops 1572864 | bytes 5242880 | tf_op jit(solution)/shard_map/sub | solution.py:141
  (49 shorter events, 34.7 us)
Async XLA Ops:
  7.2 272.1 %all-reduce.2.cloned.1.call-start = ((), (), s32[]{:S(2)}) async-start(), calls=%async_computation | async-start | bytes 4194304 | tf_op jit(solution)/shard_map/psum | solution.py:135
  8.3 10.5 %collective-permute-start = (f32[2,128,256]{2,1,0:T(8,128)S(1)}, f32[2,128,256]{2,1,0:T(8,128)S(1)}, u32[]{:S(2)}, u32[]{:S(2)}) collective-permute-start(f32[2,128,256]{2,1,0:T(8,128)S(1)} %get-tuple-element.260), channel_id=1, source_target_pairs={{0,4},{4,8},{8,12},{1,5},{5,9},{9,13},{2,6},{6,10},{10,14},{3,7},{... | collective-permute-start | bytes 786440 | tf_op jit(solution)/shard_map/ppermute | solution.py:18
  13.2 17.0 %copy-start.1 = (bf16[4,2,256,256]{3,2,1,0:T(8,128)(2,1)S(1)}, bf16[4,2,256,256]{3,2,1,0:T(8,128)(2,1)}, u32[]{:S(2)}) copy-start(bf16[4,2,256,256]{3,2,1,0:T(8,128)(2,1)} %param.16) | copy-start | bytes 3145732
  13.2 9.8 %collective-permute-start.1 = (f32[2,128,256]{2,1,0:T(8,128)S(1)}, f32[2,128,256]{2,1,0:T(8,128)S(1)}, u32[]{:S(2)}, u32[]{:S(2)}) collective-permute-start(f32[2,128,256]{2,1,0:T(8,128)S(1)} %get-tuple-element.259), channel_id=1, source_target_pairs={{4,0},{8,4},{12,8},{5,1},{9,5},{13,9},{6,2},{10,6},{14,10},{7,3},{... | collective-permute-start | bytes 786440 | tf_op jit(solution)/shard_map/ppermute | solution.py:21
  24.1 13.7 %collective-permute-start.2 = (f32[2,512,128]{2,1,0:T(8,128)}, f32[2,512,128]{2,1,0:T(8,128)}, u32[]{:S(2)}, u32[]{:S(2)}) collective-permute-start(f32[2,512,128]{2,1,0:T(8,128)} %get-tuple-element.257), channel_id=1, source_target_pairs={{0,2},{1,3},{4,6},{5,7},{8,10},{9,11},{12,14},{13,15},{16,18},{17,... | collective-permute-start | bytes 1572872 | tf_op jit(solution)/shard_map/ppermute | solution.py:18
  28.3 14.4 %collective-permute-start.3 = (f32[2,512,128]{2,1,0:T(8,128)}, f32[2,512,128]{2,1,0:T(8,128)}, u32[]{:S(2)}, u32[]{:S(2)}) collective-permute-start(f32[2,512,128]{2,1,0:T(8,128)} %get-tuple-element.258), channel_id=1, source_target_pairs={{2,0},{3,1},{6,4},{7,5},{10,8},{11,9},{14,12},{15,13},{18,16},{19,... | collective-permute-start | bytes 1572872 | tf_op jit(solution)/shard_map/ppermute | solution.py:21
  45.5 3.1 %copy-start.3 = (s32[1,1,3,2]{2,3,1,0:T(2,128)S(1)}, s32[1,1,3,2]{2,3,1,0:T(2,128)}, u32[]{:S(2)}) copy-start(s32[1,1,3,2]{2,3,1,0:T(2,128)} %param.18) | copy-start | bytes 76
  88.4 4.4 %collective-permute-start.4 = (f32[2,512,512]{2,1,0:T(8,128)}, f32[2,512,512]{2,1,0:T(8,128)S(1)}, u32[]{:S(2)}, u32[]{:S(2)}) collective-permute-start(f32[2,512,512]{2,1,0:T(8,128)} %get-tuple-element.151), channel_id=1, source_target_pairs={{0,1},{1,0},{2,3},{3,2},{4,5},{5,4},{6,7},{7,6},{8,9},{9,8},{10,11... | collective-permute-start | bytes 6291464 | tf_op jit(solution)/shard_map/ppermute | solution.py:33
  94.8 85.0 %copy-start = (f32[4,2,256,256]{3,2,0,1:T(8,128)S(1)}, f32[4,2,256,256]{3,2,0,1:T(8,128)}, u32[]{:S(2)}) copy-start(f32[4,2,256,256]{3,2,0,1:T(8,128)} %get-tuple-element.152) | copy-start | bytes 6291460
  95.9 101.0 %collective-permute-start.5 = (f32[2,128,512]{2,1,0:T(8,128)}, f32[2,128,512]{2,1,0:T(8,128)}, u32[]{:S(2)}, u32[]{:S(2)}) collective-permute-start(f32[2,128,512]{2,1,0:T(8,128)} %get-tuple-element.252), channel_id=1, source_target_pairs={{0,4},{4,8},{8,12},{1,5},{5,9},{9,13},{2,6},{6,10},{10,14},{3,7},{... | collective-permute-start | bytes 1572872 | tf_op jit(solution)/shard_map/ppermute | solution.py:18
  181.3 26.5 %collective-permute-start.6 = (f32[2,128,512]{2,1,0:T(8,128)}, f32[2,128,512]{2,1,0:T(8,128)}, u32[]{:S(2)}, u32[]{:S(2)}) collective-permute-start(f32[2,128,512]{2,1,0:T(8,128)} %get-tuple-element.251), channel_id=1, source_target_pairs={{4,0},{8,4},{12,8},{5,1},{9,5},{13,9},{6,2},{10,6},{14,10},{7,3},{... | collective-permute-start | bytes 1572872 | tf_op jit(solution)/shard_map/ppermute | solution.py:21
  209.0 73.8 %collective-permute-start.8 = (f32[2,256,128]{2,1,0:T(8,128)S(1)}, f32[2,256,128]{2,1,0:T(8,128)S(1)}, u32[]{:S(2)}, u32[]{:S(2)}) collective-permute-start(f32[2,256,128]{2,1,0:T(8,128)S(1)} %get-tuple-element.253), channel_id=1, source_target_pairs={{2,0},{3,1},{6,4},{7,5},{10,8},{11,9},{14,12},{15,13},{18,16},{19,... | collective-permute-start | bytes 786440 | tf_op jit(solution)/shard_map/ppermute | solution.py:21
  210.3 72.4 %collective-permute-start.7 = (f32[2,256,128]{2,1,0:T(8,128)S(1)}, f32[2,256,128]{2,1,0:T(8,128)S(1)}, u32[]{:S(2)}, u32[]{:S(2)}) collective-permute-start(f32[2,256,128]{2,1,0:T(8,128)S(1)} %get-tuple-element.254), channel_id=1, source_target_pairs={{0,2},{1,3},{4,6},{5,7},{8,10},{9,11},{12,14},{13,15},{16,18},{17,... | collective-permute-start | bytes 786440 | tf_op jit(solution)/shard_map/ppermute | solution.py:18
  282.7 1.0 copy-start.2
Sparse Core Ops, SparseCore 0:
  181.5 97.7 all-reduce.1
where the time goes:
time: 294 us; the launch traced here: 291 us
  waiting for transfers between devices  112 us (38%)
  starting transfers between devices  103 us (35%)
  matrix products  21.1 us (7%)
  other arithmetic  19.1 us (6%)
  local copies, waits for them, and re-layouts  17.1 us (6%)
  between operations  14.8 us (5%)
  loops' own time  3.88 us (1%)
    ppermute x4, starting transfers between devices, with_halo(): lax.ppermute(lax.slice_in_dim(block, block.shape[dim] - width, None, axis...  97.7 us
    psum x1, waiting for transfers between devices, shards(): probe_total = lax.psum(probe_grad, ('xt', 'yt', 'sg'))  64.4 us
    ppermute x4, waiting for transfers between devices, with_halo(): lax.ppermute(lax.slice_in_dim(block, block.shape[dim] - width, None, axis...  25.7 us
    ppermute x4, waiting for transfers between devices, with_halo(): lax.ppermute(lax.slice_in_dim(block, 0, width, axis=dim), axis, backward)  17.9 us
    dot_general x8, matrix products, on_right(): jnp.einsum('mkn,nj->mkj', values, table, preferred_element_type=jnp.float32)  10.7 us
    dot_general x8, matrix products, on_left(): jnp.einsum('kn,mnj->mkj', table, values, preferred_element_type=jnp.float32)  10.5 us
    dynamic_update_slice x1, local copies, waits for them, and re-layouts, visit(): lax.dynamic_update_slice(grad_pad, current + patch_grad, (zero_index, anc...  6.43 us
  transfers between devices with their start and end apart: 10, of which 8 were waited for; matrix products, arithmetic and copies ran while one was open for 3% of the time, Pallas kernels for 0%

commit v1 on v0

v1 whole, which is shorter than its diff:
```python
import math

import numpy as np
import ml_dtypes
import jax
import jax.numpy as jnp
from jax import lax
from jax.experimental import pallas as pl
from jax.experimental.pallas import tpu as pltpu
from jax.sharding import PartitionSpec as P

floor_term = 0.5
field_rate = 0.25
probe_rate = 0.1
grid_axes = ("xt", "yt", "sg")


def half_spectrum_order(width):
    half = width // 2
    return np.concatenate([np.arange(half), [half], np.arange(width - 1, half, -1)])


def real_tables(width):
    half = width // 2
    index = np.arange(width)
    angle = (index[:, None] * index[None, :] % width) * (2.0 * math.pi / width)
    cosine, sine = np.cos(angle), np.sin(angle)
    cosine[np.abs(cosine) < 1e-9] = 0.0
    rows = np.concatenate([cosine[: half + 1], sine[1:half]], axis=0)
    select = np.eye(width)[half_spectrum_order(width)]
    return [np.asarray(x, dtype=ml_dtypes.bfloat16) for x in (rows, rows.T, select, select.T)]


def dot(a, b):
    return jnp.dot(a, b, preferred_element_type=jnp.float32)


def scan_kernel(meta_ref, offs_ref, tile_ref, mine_ref, other_ref, probe_ref, amp_ref, rows_ref, cols_ref,
                sel_ref, selt_ref, keep_grad_ref, send_grad_ref, keep_probe_ref, send_probe_ref,
                pad_ref, grad_ref, pg_ref, patch_ref, far_ref, acc_ref, fac_ref):
    modes = probe_ref.shape[0]
    width = probe_ref.shape[-1]
    half = width // 2
    bf16 = jnp.bfloat16
    grad_ref[...] = jnp.zeros_like(grad_ref)
    core = meta_ref[1]
    side = meta_ref[2]
    middle = 1 - core
    for j in range(2):
        for i in range(2):
            pad_ref[:, 1 + j, (1 + i) * half : (2 + i) * half] = tile_ref[:, i * half : (i + 1) * half, j * half : (j + 1) * half]
    for source, at in ((mine_ref, core), (other_ref, middle)):
        margin = pl.ds(pl.multiple_of(at * 3 * half, half), half)
        strip = pl.ds(pl.multiple_of((at + 1) * half, half), half)
        pad_ref[:, 1, margin] = source[:, :, :half]
        pad_ref[:, 2, margin] = source[:, :, half:width]
        for step in range(2):
            block = side if step == 0 else 3 - side
            start = width + step * width
            if start < source.shape[-1]:
                pad_ref[:, block, strip] = source[:, :, start : start + half]
                pad_ref[:, block, margin] = source[:, :, start + half : start + width]
            else:
                pad_ref[:, block, strip] = jnp.zeros((2, half, half), jnp.float32)
                pad_ref[:, block, margin] = jnp.zeros((2, half, half), jnp.float32)
    pg_ref[...] = jnp.zeros_like(pg_ref)
    row_zero = lax.broadcasted_iota(jnp.int32, (half, width), 0) == 0
    col_zero = lax.broadcasted_iota(jnp.int32, (width, half), 1) == 0

    def split(re, im, axis):
        zero = row_zero if axis == 0 else col_zero
        cut = (lambda x: (x[:half], x[half:])) if axis == 0 else (lambda x: (x[:, :half], x[:, half:]))
        ar, br = cut(re)
        ai, bi = cut(im)
        bi0 = jnp.where(zero, 0.0, bi)
        br0 = jnp.where(zero, 0.0, br)
        lr, li = ar + bi0, ai - br0
        hr = jnp.where(zero, br, ar - bi)
        hi = jnp.where(zero, bi, ai + br)
        return jnp.concatenate([lr, hr], axis), jnp.concatenate([li, hi], axis)

    def fold(re, im, axis):
        zero = row_zero if axis == 0 else col_zero
        cut = (lambda x: (x[:half], x[half:])) if axis == 0 else (lambda x: (x[:, :half], x[:, half:]))
        r1, r2 = cut(re)
        i1, i2 = cut(im)
        lr = r1 + jnp.where(zero, 0.0, r2)
        li = i1 + jnp.where(zero, 0.0, i2)
        hr = jnp.where(zero, r2, i2 - i1)
        hi = jnp.where(zero, i2, r1 - r2)
        return (jnp.concatenate([lr, hr], axis).astype(bf16), jnp.concatenate([li, hi], axis).astype(bf16))

    def visit(s, carry):
        row = offs_ref[s, 0]
        col = offs_ref[s, 1]
        base = jnp.where(col >= half, 1, 0)
        shift = col - base * half
        for comp in range(2):
            win = jnp.concatenate([pad_ref[comp, base + j, pl.ds(row, width), :] for j in range(3)], axis=1)
            win = pltpu.roll(win, lax.rem(width + half - shift, width + half), 1)
            patch_ref[comp] = win[:, :width]
        amp = dot(dot(sel_ref[...], amp_ref[s]).astype(bf16), selt_ref[...])
        fac_ref[...] = jnp.zeros_like(fac_ref)

        def forward(m, carry):
            qr = probe_ref[m, 0].astype(jnp.float32)
            qi = probe_ref[m, 1].astype(jnp.float32)
            pr = patch_ref[0]
            pi = patch_ref[1]
            psi_r = (qr * pr - qi * pi).astype(bf16)
            psi_i = (qr * pi + qi * pr).astype(bf16)
            yr, yi = split(dot(rows_ref[...], psi_r), dot(rows_ref[...], psi_i), 0)
            fr, fi = split(dot(yr.astype(bf16), cols_ref[...]), dot(yi.astype(bf16), cols_ref[...]), 1)
            far_ref[m, 0] = fr
            far_ref[m, 1] = fi
            fac_ref[...] += fr * fr + fi * fi
            return carry

        lax.fori_loop(0, modes, forward, 0, unroll=True)
        scale = 1.0 / (width * width)
        fac_ref[...] = (scale - amp * scale * lax.rsqrt(fac_ref[...] * scale + floor_term))
        acc_ref[...] = jnp.zeros_like(acc_ref)

        def backward(m, carry):
            f = fac_ref[...]
            ur, ui = fold(far_ref[m, 0] * f, far_ref[m, 1] * f, 0)
            vr, vi = fold(dot(cols_ref[...], ur), dot(cols_ref[...], ui), 1)
            gr = dot(vr, rows_ref[...])
            gi = dot(vi, rows_ref[...])
            qr = probe_ref[m, 0].astype(jnp.float32)
            qi = probe_ref[m, 1].astype(jnp.float32)
            pr = patch_ref[0]
            pi = patch_ref[1]
            acc_ref[0] += qr * gr + qi * gi
            acc_ref[1] += qr * gi - qi * gr
            pg_ref[m, 0] += pr * gr + pi * gi
            pg_ref[m, 1] += pr * gi - pi * gr
            return carry

        lax.fori_loop(0, modes, backward, 0, unroll=True)
        for comp in range(2):
            wide = jnp.concatenate([acc_ref[comp], jnp.zeros((width, half), jnp.float32)], axis=1)
            wide = pltpu.roll(wide, shift, 1)
            for j in range(3):
                at = (comp, base + j, pl.ds(row, width), slice(None))
                grad_ref[at] = grad_ref[at] + wide[:, j * half : (j + 1) * half]
        return carry

    lax.fori_loop(0, meta_ref[0], visit, 0)
    for target, at in ((keep_grad_ref, core), (send_grad_ref, middle)):
        main = pl.ds(pl.multiple_of((at + 1) * half, half), half)
        margin = pl.ds(pl.multiple_of((1 - at) * 3 * half, half), half)
        target[0] = grad_ref[:, :, main]
        target[1] = grad_ref[:, :, margin]
    share = modes // 2
    keep_probe_ref[...] = pg_ref[pl.ds(core * share, share)]
    send_probe_ref[...] = pg_ref[pl.ds(middle * share, share)]


def scans(meta, offs, tile, mine, other, probe, amp):
    modes, _, width, _ = probe.shape
    half = width // 2
    tables = [jnp.asarray(t) for t in real_tables(width)]
    smem = pl.BlockSpec(memory_space=pltpu.SMEM)
    vmem = pl.BlockSpec(memory_space=pltpu.VMEM)
    grad = jax.ShapeDtypeStruct((2, 2, 4, half, half), jnp.float32)
    share = jax.ShapeDtypeStruct((modes // 2, 2, width, width), jnp.float32)
    return pl.pallas_call(
        scan_kernel,
        out_shape=(grad, grad, share, share),
        in_specs=[smem, smem] + [vmem] * 9,
        out_specs=(vmem,) * 4,
        scratch_shapes=[
            pltpu.VMEM((2, 4, 2 * width, half), jnp.float32),
            pltpu.VMEM((2, 4, 2 * width, half), jnp.float32),
            pltpu.VMEM((modes, 2, width, width), jnp.float32),
            pltpu.VMEM((2, width, width), jnp.float32),
            pltpu.VMEM((modes, 2, width, width), jnp.float32),
            pltpu.VMEM((2, width, width), jnp.float32),
            pltpu.VMEM((width, width), jnp.float32),
        ],
        compiler_params=pltpu.CompilerParams(vmem_limit_bytes=40 * 2**20),
        cost_estimate=pl.CostEstimate(flops=4 * 10**9, bytes_accessed=8 * 2**20, transcendentals=0),
    )(meta, offs, tile, mine, other, probe, amp, *tables)


def route(target):
    rows, cols, cores = (lax.axis_size(a) for a in grid_axes)
    pairs = []
    for z in range(rows):
        for x in range(cols):
            for c in range(cores):
                to = target(z, x, c)
                if to is not None and 0 <= to[0] < rows and 0 <= to[1] < cols:
                    pairs.append(((z * cols + x) * cores + c, (to[0] * cols + to[1]) * cores + to[2]))
    return pairs


def move(block, target):
    return lax.ppermute(block, grid_axes, route(target))


def across(x, step):
    return x + 1 if x % 2 == step else x - 1


def down(z, c):
    return z + 1 if c == 0 else z - 1


def swap_cores(block):
    return move(block, lambda z, x, c: (z, x, 1 - c))


def axis_bits(axis):
    return [(axis, b) for b in range(lax.axis_size(axis).bit_length() - 1)]


def reduce_orders():
    first, second = axis_bits("yt"), axis_bits("xt")
    a, b = [], []
    for i in range(max(len(first), len(second))):
        pair = first[i : i + 1] + second[i : i + 1]
        a += pair
        b += pair[::-1]
    return list(zip(a, b))


def flip(order):
    def target(z, x, c):
        axis, bit = order[c]
        return (z ^ (1 << bit), x, c) if axis == "xt" else (z, x ^ (1 << bit), c)

    return target


def bit_of(order, core):
    bits = [(lax.axis_index(axis) >> bit) & 1 for axis, bit in order]
    return jnp.where(core == 0, bits[0], bits[1])


def pick(block, index):
    return lax.dynamic_index_in_dim(block, index, 0, keepdims=False)


def joined(own, other, bit):
    return jnp.where(bit == 0, jnp.concatenate([own, other], 0), jnp.concatenate([other, own], 0))


def new_probe_share(part, probe_part, core):
    orders = reduce_orders()
    shape = part.shape
    part = part.reshape(-1, shape[-1])
    probe_part = probe_part.reshape(-1, shape[-1])
    for order in orders[:-1]:
        bit = bit_of(order, core)
        part = part.reshape(2, -1, shape[-1])
        got = move(pick(part, 1 - bit), flip(order))
        part = pick(part, bit) + got
        probe_part = pick(probe_part.reshape(2, -1, shape[-1]), bit)
    for order in orders[-1:]:
        part = part + move(part, flip(order))
    part = probe_part.astype(jnp.float32) - probe_rate * part
    for order in orders[:-1][::-1]:
        part = joined(part, move(part, flip(order)), bit_of(order, core))
    return part.reshape(shape)


def shards(field, probe, amplitudes, offsets, counts):
    modes, _, width, _ = probe.shape
    half = width // 2
    per_device = amplitudes.shape[2]
    core = lax.axis_index("sg")
    odd = lax.axis_index("yt") % 2
    steps = min(2, lax.axis_size("yt") - 1)
    live = jnp.clip(counts[0, 0] - core * per_device, 0, per_device)
    side = jnp.where(odd == 0, 3, 0)
    meta = jnp.stack([live, core, side]).astype(jnp.int32)

    outer = lax.dynamic_slice_in_dim(field, (1 - core) * half, half, 1)
    inner = lax.dynamic_slice_in_dim(field, core * half, half, 1)
    parts = [move(outer, lambda z, x, c: (down(z, c), x, c))]
    for step in range(steps):
        start = jnp.where(odd == step, half, 0)
        parts.append(move(lax.dynamic_slice_in_dim(inner, start, half, 2), lambda z, x, c: (z, across(x, step), c)))
        parts.append(move(lax.dynamic_slice_in_dim(outer, start, half, 2), lambda z, x, c: (down(z, c), across(x, step), c)))
    mine = jnp.concatenate(parts, axis=2)
    other = swap_cores(mine)

    keep_grad, send_grad, keep_probe, send_probe = scans(
        meta, offsets[0, 0], field, mine, other, probe, amplitudes[0, 0]
    )

    share = keep_probe + swap_cores(send_probe)
    grad = keep_grad + swap_cores(send_grad)
    main, margin = grad[0], grad[1]
    below = move(margin[:, 1:3], lambda z, x, c: (down(z, c), x, c))
    total = main[:, 1:3] + below
    blocks = [total[:, 0], total[:, 1]]
    for step in range(steps):
        block = jnp.where(odd == step, 3, 0)
        beside = move(lax.dynamic_index_in_dim(main, block, 1, keepdims=False), lambda z, x, c: (z, across(x, step), c))
        corner = move(lax.dynamic_index_in_dim(margin, block, 1, keepdims=False), lambda z, x, c: (down(z, c), across(x, step), c))
        extra = beside + corner
        blocks[0] = blocks[0] + jnp.where(odd == step, 0.0, extra)
        blocks[1] = blocks[1] + jnp.where(odd == step, extra, 0.0)
    new_field = inner - field_rate * jnp.concatenate(blocks, axis=2)

    probe_part = lax.dynamic_slice_in_dim(probe, core * (modes // 2), modes // 2, 0)
    own = new_probe_share(share, probe_part, core)
    new_probe = joined(own, swap_cores(own), core)
    return (new_field, new_probe)


def solution(mesh):
    in_specs = (
        P(None, ("groups", "xt"), "yt"),
        P("groups", None, None, None),
        P(("groups", "xt"), "yt", "sg", None, None),
        P(("groups", "xt"), "yt", "sg", None),
        P(("groups", "xt"), "yt"),
    )
    out_specs = (P(None, ("groups", "xt", "sg"), "yt"), P("groups", None, None, None))
    return jax.shard_map(shards, mesh=mesh, in_specs=in_specs, out_specs=out_specs, check_vma=False)
```

time: 294 us -> 106 us (0.36)
  starting transfers between devices: 103 us -> 33 us
  waiting for transfers between devices: 112 us -> 46.2 us
  matrix products: 21.1 us -> 0 us
  between operations: 14.8 us -> 1.58 us
  other arithmetic: 19.1 us -> 8.62 us
  local copies, waits for them, and re-layouts: 17.1 us -> 10.5 us
  Pallas kernels: 0 us -> 5.43 us
  loops' own time: 3.88 us -> 0 us
    ppermute x9 -> x15, starting transfers between devices: 103 us -> 33 us  [move(): return lax.ppermute(block, grid_axes, route(target))]
    psum x1 -> x0, waiting for transfers between devices: 64.4 us -> none  [shards(): probe_total = lax.psum(probe_grad, ('xt', 'yt', 'sg'))]
    dot_general x16 -> x0, matrix products: 21.1 us -> none  [the longest x8 10.7 us: on_right(): jnp.einsum('mkn,nj->mkj', values, table, preferred_element_type=jnp.float32)]
    dynamic_update_slice x1 -> x0, local copies, waits for them, and re-layouts: 6.43 us -> none  [visit(): lax.dynamic_update_slice(grad_pad, current + patch_grad, (zero_index, anc...]
    unnamed x10 -> x26, local copies, waits for them, and re-layouts: 1.98 us -> 7.76 us
    pallas_call x0 -> x1, Pallas kernels: none -> 5.43 us  [scans(): pl.pallas_call(scan_kernel, out_shape=(grad, grad, share, share), in_spec...]
    select_n x0 -> x3, other arithmetic: none -> 3.95 us  [joined(): jnp.where(bit == 0, jnp.concatenate([own, other], 0), jnp.concatenate([ot...]
    another operation x1 -> x0, loops' own time: 3.88 us -> none  [shards(): grad_pad, probe_grad = lax.fori_loop(0, live, visit, start)]
  transfers between devices with their start and end apart: 10 -> 15, of which waited for: 8 -> 11; matrix products, arithmetic and copies ran while one was open for 3% -> 4% of each run, Pallas kernels for 0% -> 0%
where the time goes in v1:
time: 106 us; the launch traced here: 105 us
  waiting for transfers between devices  46.2 us (44%)
  starting transfers between devices  33 us (31%)
  local copies, waits for them, and re-layouts  10.5 us (10%)
  other arithmetic  8.62 us (8%)
  Pallas kernels  5.43 us (5%)
  between operations  1.58 us (1%)
    ppermute x15, waiting for transfers between devices, move(): return lax.ppermute(block, grid_axes, route(target))  46.2 us
    ppermute x15, starting transfers between devices, move(): return lax.ppermute(block, grid_axes, route(target))  33 us
    unnamed x26, local copies, waits for them, and re-layouts  7.76 us
    pallas_call x1, Pallas kernels, scans(): pl.pallas_call(scan_kernel, out_shape=(grad, grad, share, share), in_spec...  5.43 us
    select_n x3, other arithmetic, joined(): jnp.where(bit == 0, jnp.concatenate([own, other], 0), jnp.concatenate([ot...  3.95 us
    add x2, other arithmetic, new_probe_share(): part = pick(part, bit) + got  2.25 us
  transfers between devices with their start and end apart: 15, of which 11 were waited for; matrix products, arithmetic and copies ran while one was open for 4% of the time, Pallas kernels for 0%

profile of v1, /device:TPU:0, one launch (start us, length us, event | category | flops | bytes accessed | tf_op | source)
XLA Modules:
  0.0 105.3 jit_solution(285795195173369610)
XLA Ops:
  1.7 4.9 %collective-permute-start = (f32[2,128,256]{2,1,0:T(8,128)S(1)}, f32[2,128,256]{2,1,0:T(8,128)S(1)}, u32[]{:S(2)}, u32[]{:S(2)}) collective-permute-start(f32[2,128,256]{2,1,0:T(8,128)S(1)} %constant_dynamic-slice_fusion.4), channel_id=1, source_target_pairs={{0,4},{2,6},{4,8},{5,1},{6,10},{7,3},{8,12},{9,5},{10,14},{11,7},{... | collective-permute-start | bytes 786440 | tf_op jit(solution)/shard_map/ppermute | solution.py:200
  6.7 1.1 %constant_dynamic-slice_fusion.2 = (f32[2,128,128]{2,1,0:T(8,128)S(1)}, f32[2,128,128]{2,1,0:T(8,128)S(1)}) fusion(f32[2,256,256]{2,1,0:T(8,128)} %tile_ref.1, s32[]{:T(128)S(6)} %select_n.110, s32[]{:T(128)S(6)} %select_n.109, s32[]{:T(128)S(6)} %select_n.107), kind=kLoop, calls=%fused_computation.22 | loop fusion | bytes 524300 | tf_op jit(solution)/shard_map/dynamic_slice | solution.py:286
  7.8 1.6 %collective-permute-start.1 = (f32[2,128,128]{2,1,0:T(8,128)S(1)}, f32[2,128,128]{2,1,0:T(8,128)S(1)}, u32[]{:S(2)}, u32[]{:S(2)}) collective-permute-start(f32[2,128,128]{2,1,0:T(8,128)S(1)} %get-tuple-element.17), channel_id=1, source_target_pairs={{0,2},{1,3},{2,0},{3,1},{4,6},{5,7},{6,4},{7,5},{8,10},{9,11},{10,... | collective-permute-start | bytes 393224 | tf_op jit(solution)/shard_map/ppermute | solution.py:200
  9.4 3.4 %collective-permute-start.2 = (f32[2,128,128]{2,1,0:T(8,128)S(1)}, f32[2,128,128]{2,1,0:T(8,128)S(1)}, u32[]{:S(2)}, u32[]{:S(2)}) collective-permute-start(f32[2,128,128]{2,1,0:T(8,128)S(1)} %get-tuple-element.16), channel_id=1, source_target_pairs={{0,6},{2,4},{4,10},{5,3},{6,8},{7,1},{8,14},{9,7},{10,12},{11,5},{... | collective-permute-start | bytes 393224 | tf_op jit(solution)/shard_map/ppermute | solution.py:200
  12.9 1.4 %collective-permute-done.1 = f32[2,128,128]{2,1,0:T(8,128)S(1)} collective-permute-done((f32[2,128,128]{2,1,0:T(8,128)S(1)}, f32[2,128,128]{2,1,0:T(8,128)S(1)}, u32[]{:S(2)}, u32[]{:S(2)}) %collective-permute-start.1) | collective-permute-done | bytes 131104 | tf_op jit(solution)/shard_map/ppermute | solution.py:200
  18.1 1.2 %copy-done.1 = bf16[4,2,256,256]{3,2,1,0:T(8,128)(2,1)S(1)} copy-done((bf16[4,2,256,256]{3,2,1,0:T(8,128)(2,1)S(1)}, bf16[4,2,256,256]{3,2,1,0:T(8,128)(2,1)}, u32[]{:S(2)}) %copy-start.1) | copy-done | bytes 1048600
  23.1 5.4 %shard_map.104 = (f32[2,2,4,128,128]{4,3,2,1,0:T(8,128)S(1)}, f32[2,2,4,128,128]{4,3,2,1,0:T(8,128)S(1)}, f32[2,2,256,256]{3,2,1,0:T(8,128)S(1)}, f32[2,2,256,256]{3,2,1,0:T(8,128)}) custom-call(s32[3]{0:T(128)S(1)} %pad_add_fusion.meta_ref, s32[3,2]{1,0:T(4,128)S(1)} %copy.11.offs_ref, f32[2,256,256]{2,1,0:T(8,128)S(1)} %copy-done, ...), custom_call_target="tpu_custom_call" | custom-call | flops 4000000000 | bytes 8388608 | tf_op jit(solution)/shard_map/pallas_call | solution.py:168
  29.5 3.0 %collective-permute-done.8 = f32[2,2,256,256]{3,2,1,0:T(8,128)} collective-permute-done((f32[2,2,256,256]{3,2,1,0:T(8,128)}, f32[2,2,256,256]{3,2,1,0:T(8,128)}, u32[]{:S(2)}, u32[]{:S(2)}) %collective-permute-start.8) | collective-permute-done | bytes 1048608 | tf_op jit(solution)/shard_map/ppermute | solution.py:200
  32.5 1.4 %add.82 = f32[2,2,256,256]{3,2,1,0:T(8,128)S(1)} add(f32[2,2,256,256]{3,2,1,0:T(8,128)S(1)} %get-tuple-element.8, f32[2,2,256,256]{3,2,1,0:T(8,128)} %collective-permute-done.8) | non-fusion elementwise | flops 262144 | bytes 3145728 | tf_op jit(solution)/shard_map/add | solution.py:294
  34.9 8.1 %collective-permute-start.9 = (f32[512,256]{1,0:T(8,128)S(1)}, f32[512,256]{1,0:T(8,128)}, u32[]{:S(2)}, u32[]{:S(2)}) collective-permute-start(f32[512,256]{1,0:T(8,128)S(1)} %dynamic-slice_bitcast_fusion), channel_id=1, source_target_pairs={{0,2},{1,5},{2,0},{3,7},{4,6},{5,1},{6,4},{7,3},{8,10},{9,13},{10,... | collective-permute-start | bytes 1572872 | tf_op jit(solution)/shard_map/ppermute | solution.py:200
  43.0 7.3 %collective-permute-done.9 = f32[512,256]{1,0:T(8,128)} collective-permute-done((f32[512,256]{1,0:T(8,128)S(1)}, f32[512,256]{1,0:T(8,128)}, u32[]{:S(2)}, u32[]{:S(2)}) %collective-permute-start.9) | collective-permute-done | bytes 524320 | tf_op jit(solution)/shard_map/ppermute | solution.py:200
  50.3 1.3 %bitcast_add_fusion = f32[512,256]{1,0:T(8,128)S(1)} fusion(f32[512,256]{1,0:T(8,128)} %collective-permute-done.9, f32[2,512,256]{2,1,0:T(8,128)} %bitcast.45, s32[]{:T(128)S(6)} %select_n.120), kind=kLoop, calls=%fused_computation.3 | loop fusion | flops 131072 | bytes 1572868 | tf_op jit(solution)/shard_map/add | solution.py:259
  51.6 2.4 %collective-permute-start.10 = (f32[256,256]{1,0:T(8,128)S(1)}, f32[256,256]{1,0:T(8,128)}, u32[]{:S(2)}, u32[]{:S(2)}) collective-permute-start(f32[256,256]{1,0:T(8,128)S(1)} %dynamic-slice_bitcast_fusion.1), channel_id=1, source_target_pairs={{0,4},{1,3},{2,6},{3,1},{4,0},{5,7},{6,2},{7,5},{8,12},{9,11},{10,... | collective-permute-start | bytes 786440 | tf_op jit(solution)/shard_map/ppermute | solution.py:200
  54.0 4.5 %collective-permute-done.10 = f32[256,256]{1,0:T(8,128)} collective-permute-done((f32[256,256]{1,0:T(8,128)S(1)}, f32[256,256]{1,0:T(8,128)}, u32[]{:S(2)}, u32[]{:S(2)}) %collective-permute-start.10) | collective-permute-done | bytes 262176 | tf_op jit(solution)/shard_map/ppermute | solution.py:200
  59.5 4.6 %collective-permute-start.11 = (f32[256,256]{1,0:T(8,128)S(1)}, f32[256,256]{1,0:T(8,128)S(1)}, u32[]{:S(2)}, u32[]{:S(2)}) collective-permute-start(f32[256,256]{1,0:T(8,128)S(1)} %bitcast_add_fusion.1), channel_id=1, source_target_pairs={{0,8},{1,9},{2,10},{3,11},{4,12},{5,13},{6,14},{7,15},{8,0},{9,1},... | collective-permute-start | bytes 786440 | tf_op jit(solution)/shard_map/ppermute | solution.py:200
  64.2 10.2 %collective-permute-done.11 = f32[256,256]{1,0:T(8,128)S(1)} collective-permute-done((f32[256,256]{1,0:T(8,128)S(1)}, f32[256,256]{1,0:T(8,128)S(1)}, u32[]{:S(2)}, u32[]{:S(2)}) %collective-permute-start.11) | collective-permute-done | bytes 262176 | tf_op jit(solution)/shard_map/ppermute | solution.py:200
  74.6 6.5 %collective-permute-done.12 = f32[256,256]{1,0:T(8,128)} collective-permute-done((f32[256,256]{1,0:T(8,128)S(1)}, f32[256,256]{1,0:T(8,128)}, u32[]{:S(2)}, u32[]{:S(2)}) %collective-permute-start.12) | collective-permute-done | bytes 262176 | tf_op jit(solution)/shard_map/ppermute | solution.py:200
  81.0 1.1 %maximum_select_fusion.2 = f32[512,256]{1,0:T(8,128)S(1)} fusion(f32[256,256]{1,0:T(8,128)} %collective-permute-done.12, f32[256,256]{1,0:T(8,128)S(1)} %convert_subtract_fusion, pred[]{:T(512)S(6)} %eq.13), kind=kLoop, calls=%fused_computation.2 | loop fusion | flops 393216 | bytes 1048577 | tf_op jit(solution)/shard_map/jit(_where)/select_n | solution.py:247
  83.0 8.5 %collective-permute-done.13 = f32[512,256]{1,0:T(8,128)} collective-permute-done((f32[512,256]{1,0:T(8,128)S(1)}, f32[512,256]{1,0:T(8,128)}, u32[]{:S(2)}, u32[]{:S(2)}) %collective-permute-start.13) | collective-permute-done | bytes 524320 | tf_op jit(solution)/shard_map/ppermute | solution.py:200
  91.4 1.3 %maximum_select_fusion.1 = f32[1024,256]{1,0:T(8,128)S(1)} fusion(f32[512,256]{1,0:T(8,128)} %collective-permute-done.13, f32[512,256]{1,0:T(8,128)S(1)} %maximum_select_fusion.2, pred[]{:T(512)S(6)} %eq.12), kind=kLoop, calls=%fused_computation.1 | loop fusion | flops 786432 | bytes 2097153 | tf_op jit(solution)/shard_map/jit(_where)/select_n | solution.py:247
  93.2 1.9 %collective-permute-start.5 = (f32[2,2,128,128]{3,2,1,0:T(8,128)S(1)}, f32[2,2,128,128]{3,2,1,0:T(8,128)S(1)}, u32[]{:S(2)}, u32[]{:S(2)}) collective-permute-start(f32[2,2,128,128]{3,2,1,0:T(8,128)S(1)} %slice.27), channel_id=1, source_target_pairs={{0,4},{2,6},{4,8},{5,1},{6,10},{7,3},{8,12},{9,5},{10,14},{11,7},{... | collective-permute-start | bytes 786440 | tf_op jit(solution)/shard_map/ppermute | solution.py:200
  95.9 4.2 %collective-permute-start.7 = (f32[2,128,128]{2,1,0:T(8,128)S(1)}, f32[2,128,128]{2,1,0:T(8,128)S(1)}, u32[]{:S(2)}, u32[]{:S(2)}) collective-permute-start(f32[2,128,128]{2,1,0:T(8,128)S(1)} %dynamic-slice_bitcast_fusion.2), channel_id=1, source_target_pairs={{0,6},{2,4},{4,10},{5,3},{6,8},{7,1},{8,14},{9,7},{10,12},{11,5},{... | collective-permute-start | bytes 393224 | tf_op jit(solution)/shard_map/ppermute | solution.py:200
  100.4 2.5 %collective-permute-done.7 = f32[2,128,128]{2,1,0:T(8,128)S(1)} collective-permute-done((f32[2,128,128]{2,1,0:T(8,128)S(1)}, f32[2,128,128]{2,1,0:T(8,128)S(1)}, u32[]{:S(2)}, u32[]{:S(2)}) %collective-permute-start.7) | collective-permute-done | bytes 131104 | tf_op jit(solution)/shard_map/ppermute | solution.py:200
  103.8 1.5 %maximum_select_fusion = f32[4,2,256,256]{3,2,1,0:T(8,128)} fusion(f32[2,2,256,256]{3,2,1,0:T(8,128)S(1)} %collective-permute-done.14, f32[2,2,256,256]{3,2,1,0:T(8,128)S(1)} %bitcast.43, pred[]{:T(512)S(6)} %eq.11), kind=kLoop, calls=%fused_computation | loop fusion | flops 1572864 | bytes 4194305 | tf_op jit(solution)/shard_map/jit(_where)/select_n | solution.py:247
  (57 shorter events, 14.3 us)
Async XLA Ops:
  0.6 17.5 %copy-start = (f32[2,256,256]{2,1,0:T(8,128)S(1)}, f32[2,256,256]{2,1,0:T(8,128)}, u32[]{:S(2)}) copy-start(f32[2,256,256]{2,1,0:T(8,128)} %tile_ref.1) | copy-start | bytes 1572868
  0.6 15.5 %copy-start.11 = (s32[1,1,3,2]{2,3,1,0:T(2,128)S(1)}, s32[1,1,3,2]{2,3,1,0:T(2,128)}, u32[]{:S(2)}) copy-start(s32[1,1,3,2]{2,3,1,0:T(2,128)} %param.12) | copy-start | bytes 76
  0.7 17.5 %copy-start.6 = (bf16[1,1,3,256,256]{4,3,2,1,0:T(8,128)(2,1)S(1)}, bf16[1,1,3,256,256]{4,3,2,1,0:T(8,128)(2,1)}, u32[]{:S(2)}) copy-start(bf16[1,1,3,256,256]{4,3,2,1,0:T(8,128)(2,1)} %param.11) | copy-start | bytes 1179652
  1.7 11.1 %collective-permute-start = (f32[2,128,256]{2,1,0:T(8,128)S(1)}, f32[2,128,256]{2,1,0:T(8,128)S(1)}, u32[]{:S(2)}, u32[]{:S(2)}) collective-permute-start(f32[2,128,256]{2,1,0:T(8,128)S(1)} %constant_dynamic-slice_fusion.4), channel_id=1, source_target_pairs={{0,4},{2,6},{4,8},{5,1},{6,10},{7,3},{8,12},{9,5},{10,14},{11,7},{... | collective-permute-start | bytes 786440 | tf_op jit(solution)/shard_map/ppermute | solution.py:200
  7.8 6.4 %collective-permute-start.1 = (f32[2,128,128]{2,1,0:T(8,128)S(1)}, f32[2,128,128]{2,1,0:T(8,128)S(1)}, u32[]{:S(2)}, u32[]{:S(2)}) collective-permute-start(f32[2,128,128]{2,1,0:T(8,128)S(1)} %get-tuple-element.17), channel_id=1, source_target_pairs={{0,2},{1,3},{2,0},{3,1},{4,6},{5,7},{6,4},{7,5},{8,10},{9,11},{10,... | collective-permute-start | bytes 393224 | tf_op jit(solution)/shard_map/ppermute | solution.py:200
  9.4 5.9 %collective-permute-start.2 = (f32[2,128,128]{2,1,0:T(8,128)S(1)}, f32[2,128,128]{2,1,0:T(8,128)S(1)}, u32[]{:S(2)}, u32[]{:S(2)}) collective-permute-start(f32[2,128,128]{2,1,0:T(8,128)S(1)} %get-tuple-element.16), channel_id=1, source_target_pairs={{0,6},{2,4},{4,10},{5,3},{6,8},{7,1},{8,14},{9,7},{10,12},{11,5},{... | collective-permute-start | bytes 393224 | tf_op jit(solution)/shard_map/ppermute | solution.py:200
  15.4 2.0 %collective-permute-start.3 = (f32[2,128,512]{2,1,0:T(8,128)S(1)}, f32[2,128,512]{2,1,0:T(8,128)S(1)}, u32[]{:S(2)}, u32[]{:S(2)}) collective-permute-start(f32[2,128,512]{2,1,0:T(8,128)S(1)} %constant_dynamic-update-slice_fusion.mine_ref), channel_id=1, source_target_pairs={{0,1},{1,0},{2,3},{3,2},{4,5},{5,4},{6,7},{7,6},{8,9},{9,8},{10,11... | collective-permute-start | bytes 1572872 | tf_op jit(solution)/shard_map/ppermute | solution.py:200
  18.1 1.2 %copy-start.1 = (bf16[4,2,256,256]{3,2,1,0:T(8,128)(2,1)S(1)}, bf16[4,2,256,256]{3,2,1,0:T(8,128)(2,1)}, u32[]{:S(2)}) copy-start(bf16[4,2,256,256]{3,2,1,0:T(8,128)(2,1)} %probe_ref.1) | copy-start | bytes 3145732
  19.4 1.0 copy-start.5
  21.3 0.9 copy-start.8
  28.5 1.0 copy-start.3
  29.5 3.0 %collective-permute-start.8 = (f32[2,2,256,256]{3,2,1,0:T(8,128)}, f32[2,2,256,256]{3,2,1,0:T(8,128)}, u32[]{:S(2)}, u32[]{:S(2)}) collective-permute-start(f32[2,2,256,256]{3,2,1,0:T(8,128)} %get-tuple-element.9), channel_id=1, source_target_pairs={{0,1},{1,0},{2,3},{3,2},{4,5},{5,4},{6,7},{7,6},{8,9},{9,8},{10,11... | collective-permute-start | bytes 3145736 | tf_op jit(solution)/shard_map/ppermute | solution.py:200
  33.9 1.0 copy-start.10
  33.9 30.2 %copy-start.2 = (bf16[4,2,256,256]{3,2,1,0:T(8,128)(2,1)S(1)}, bf16[4,2,256,256]{3,2,1,0:T(8,128)(2,1)}, u32[]{:S(2)}) copy-start(bf16[4,2,256,256]{3,2,1,0:T(8,128)(2,1)} %probe_ref.1) | copy-start | bytes 3145732
  34.9 15.4 %collective-permute-start.9 = (f32[512,256]{1,0:T(8,128)S(1)}, f32[512,256]{1,0:T(8,128)}, u32[]{:S(2)}, u32[]{:S(2)}) collective-permute-start(f32[512,256]{1,0:T(8,128)S(1)} %dynamic-slice_bitcast_fusion), channel_id=1, source_target_pairs={{0,2},{1,5},{2,0},{3,7},{4,6},{5,1},{6,4},{7,3},{8,10},{9,13},{10,... | collective-permute-start | bytes 1572872 | tf_op jit(solution)/shard_map/ppermute | solution.py:200
  51.6 6.9 %collective-permute-start.10 = (f32[256,256]{1,0:T(8,128)S(1)}, f32[256,256]{1,0:T(8,128)}, u32[]{:S(2)}, u32[]{:S(2)}) collective-permute-start(f32[256,256]{1,0:T(8,128)S(1)} %dynamic-slice_bitcast_fusion.1), channel_id=1, source_target_pairs={{0,4},{1,3},{2,6},{3,1},{4,0},{5,7},{6,2},{7,5},{8,12},{9,11},{10,... | collective-permute-start | bytes 786440 | tf_op jit(solution)/shard_map/ppermute | solution.py:200
  59.5 15.0 %collective-permute-start.11 = (f32[256,256]{1,0:T(8,128)S(1)}, f32[256,256]{1,0:T(8,128)S(1)}, u32[]{:S(2)}, u32[]{:S(2)}) collective-permute-start(f32[256,256]{1,0:T(8,128)S(1)} %bitcast_add_fusion.1), channel_id=1, source_target_pairs={{0,8},{1,9},{2,10},{3,11},{4,12},{5,13},{6,14},{7,15},{8,0},{9,1},... | collective-permute-start | bytes 786440 | tf_op jit(solution)/shard_map/ppermute | solution.py:200
  64.1 18.7 %collective-permute-start.4 = (f32[2,2,4,128,128]{4,3,2,1,0:T(8,128)}, f32[2,2,4,128,128]{4,3,2,1,0:T(8,128)S(1)}, u32[]{:S(2)}, u32[]{:S(2)}) collective-permute-start(f32[2,2,4,128,128]{4,3,2,1,0:T(8,128)} %copy-done.3), channel_id=1, source_target_pairs={{0,1},{1,0},{2,3},{3,2},{4,5},{5,4},{6,7},{7,6},{8,9},{9,8},{10,11... | collective-permute-start | bytes 3145736 | tf_op jit(solution)/shard_map/ppermute | solution.py:200
  74.5 6.5 %collective-permute-start.12 = (f32[256,256]{1,0:T(8,128)S(1)}, f32[256,256]{1,0:T(8,128)}, u32[]{:S(2)}, u32[]{:S(2)}) collective-permute-start(f32[256,256]{1,0:T(8,128)S(1)} %convert_subtract_fusion), channel_id=1, source_target_pairs={{0,4},{1,3},{2,6},{3,1},{4,0},{5,7},{6,2},{7,5},{8,12},{9,11},{10,... | collective-permute-start | bytes 786440 | tf_op jit(solution)/shard_map/ppermute | solution.py:200
  82.1 9.4 %collective-permute-start.13 = (f32[512,256]{1,0:T(8,128)S(1)}, f32[512,256]{1,0:T(8,128)}, u32[]{:S(2)}, u32[]{:S(2)}) collective-permute-start(f32[512,256]{1,0:T(8,128)S(1)} %maximum_select_fusion.2), channel_id=1, source_target_pairs={{0,2},{1,5},{2,0},{3,7},{4,6},{5,1},{6,4},{7,3},{8,10},{9,13},{10,... | collective-permute-start | bytes 1572872 | tf_op jit(solution)/shard_map/ppermute | solution.py:200
  92.8 11.0 %collective-permute-start.14 = (f32[2,2,256,256]{3,2,1,0:T(8,128)S(1)}, f32[2,2,256,256]{3,2,1,0:T(8,128)S(1)}, u32[]{:S(2)}, u32[]{:S(2)}) collective-permute-start(f32[2,2,256,256]{3,2,1,0:T(8,128)S(1)} %bitcast.42), channel_id=1, source_target_pairs={{0,1},{1,0},{2,3},{3,2},{4,5},{5,4},{6,7},{7,6},{8,9},{9,8},{10,11... | collective-permute-start | bytes 3145736 | tf_op jit(solution)/shard_map/ppermute | solution.py:200
  93.2 7.0 %collective-permute-start.5 = (f32[2,2,128,128]{3,2,1,0:T(8,128)S(1)}, f32[2,2,128,128]{3,2,1,0:T(8,128)S(1)}, u32[]{:S(2)}, u32[]{:S(2)}) collective-permute-start(f32[2,2,128,128]{3,2,1,0:T(8,128)S(1)} %slice.27), channel_id=1, source_target_pairs={{0,4},{2,6},{4,8},{5,1},{6,10},{7,3},{8,12},{9,5},{10,14},{11,7},{... | collective-permute-start | bytes 786440 | tf_op jit(solution)/shard_map/ppermute | solution.py:200
  95.1 5.3 %collective-permute-start.6 = (f32[2,128,128]{2,1,0:T(8,128)S(1)}, f32[2,128,128]{2,1,0:T(8,128)S(1)}, u32[]{:S(2)}, u32[]{:S(2)}) collective-permute-start(f32[2,128,128]{2,1,0:T(8,128)S(1)} %dynamic-slice_bitcast_fusion.3), channel_id=1, source_target_pairs={{0,2},{1,3},{2,0},{3,1},{4,6},{5,7},{6,4},{7,5},{8,10},{9,11},{10,... | collective-permute-start | bytes 393224 | tf_op jit(solution)/shard_map/ppermute | solution.py:200
  95.9 7.1 %collective-permute-start.7 = (f32[2,128,128]{2,1,0:T(8,128)S(1)}, f32[2,128,128]{2,1,0:T(8,128)S(1)}, u32[]{:S(2)}, u32[]{:S(2)}) collective-permute-start(f32[2,128,128]{2,1,0:T(8,128)S(1)} %dynamic-slice_bitcast_fusion.2), channel_id=1, source_target_pairs={{0,6},{2,4},{4,10},{5,3},{6,8},{7,1},{8,14},{9,7},{10,12},{11,5},{... | collective-permute-start | bytes 393224 | tf_op jit(solution)/shard_map/ppermute | solution.py:200
  (3 other events, 2.6 us)

commit v2 on v1

v2 whole, which is shorter than its diff:
```python
import functools
import math

import jax
import jax.numpy as jnp
from jax import lax
from jax.experimental import pallas as pl
from jax.experimental.pallas import tpu as pltpu
from jax.sharding import PartitionSpec as P

floor_term = 0.5
field_rate = 0.25
probe_rate = 0.1
grid_axes = ("xt", "yt", "sg")


def cosine_of(phase, width):
    phase = phase & (width - 1)
    half = width // 2
    near = jnp.minimum(phase, width - phase)
    quarter = jnp.minimum(near, half - near)
    square = jnp.square(quarter.astype(jnp.float32) * (2.0 * math.pi / width))
    value = jnp.zeros_like(square)
    for power in range(12, -1, -2):
        value = value * square + (-1.0) ** (power // 2) / math.factorial(power)
    return jnp.where(near == quarter, value, -value)


def half_spectrum_table(width, axis):
    half = width // 2
    which = lax.broadcasted_iota(jnp.int32, (width, width), axis)
    other = lax.broadcasted_iota(jnp.int32, (width, width), 1 - axis)
    sine = which > half
    phase = jnp.where(sine, which - half, which) * other + jnp.where(sine, width - width // 4, 0)
    return cosine_of(phase, width).astype(jnp.bfloat16)


def half_spectrum_select(width):
    half = width // 2
    row = lax.broadcasted_iota(jnp.int32, (width, width), 0)
    col = lax.broadcasted_iota(jnp.int32, (width, width), 1)
    return (jnp.where(row > half, width + half - row, row) == col).astype(jnp.float32).astype(jnp.bfloat16)


def dot(a, b):
    return jnp.dot(a, b, preferred_element_type=jnp.float32)


def halves(x, axis):
    cut = x.shape[axis] // 2
    return (x[:cut], x[cut:]) if axis == 0 else (x[:, :cut], x[:, cut:])


def patched(general, special, axis):
    if axis == 0:
        first = lax.broadcasted_iota(jnp.int32, (8, general.shape[1]), 0) == 0
        return jnp.concatenate([jnp.where(first, special[:8], general[:8]), general[8:]], 0)
    first = lax.broadcasted_iota(jnp.int32, general.shape, 1) == 0
    return jnp.where(first, special, general)


def split(re, im, axis):
    ar, br = halves(re, axis)
    ai, bi = halves(im, axis)
    re = jnp.concatenate([patched(ar + bi, ar, axis), patched(ar - bi, br, axis)], axis)
    im = jnp.concatenate([patched(ai - br, ai, axis), patched(ai + br, bi, axis)], axis)
    return re, im


def fold(re, im, axis):
    r1, r2 = halves(re, axis)
    i1, i2 = halves(im, axis)
    re = jnp.concatenate([patched(r1 + r2, r1, axis), patched(i2 - i1, r2, axis)], axis)
    im = jnp.concatenate([patched(i1 + i2, i1, axis), patched(r1 - r2, i2, axis)], axis)
    return re.astype(jnp.bfloat16), im.astype(jnp.bfloat16)


def mode_terms(ur, ui, probe_ref, mode, pr, pi, rows, cols):
    vr, vi = fold(dot(cols, ur), dot(cols, ui), 1)
    g = dot(jnp.concatenate([vr, vi], 0), rows)
    gr, gi = g[: g.shape[0] // 2], g[g.shape[0] // 2 :]
    qr = probe_ref[mode, 0].astype(jnp.float32)
    qi = probe_ref[mode, 1].astype(jnp.float32)
    return (
        (qr * gr + qi * gi, qr * gi - qi * gr),
        (pr * gr + pi * gi, pr * gi - pi * gr),
    )


def place_shares(meta_ref, probe_ref, pg_ref, keep_ref, send_ref, chunk, blocks):
    core, mode_bits, other_bits, base = (meta_ref[i] for i in (1, 3, 4, 5))
    modes, _, width, _ = probe_ref.shape
    share = modes // 2
    part = share // 2
    size = part * 2 * width // blocks
    starting = jnp.where(base == 1, 1.0, 0.0)

    def place(p, carry):
        here = pl.ds(pl.multiple_of(p * size, size), size)
        for target, at, bits, own in ((keep_ref, core, mode_bits, True), (send_ref, 1 - core, other_bits, False)):
            line = (p ^ bits) * size
            first = line // (2 * width)
            comp = line % (2 * width) // width
            inside = pl.ds(pl.multiple_of(line % width, size), size)
            value = -probe_rate * pg_ref[at * part + first, comp, inside]
            if own:
                value += starting * probe_ref[at * share + chunk * part + first, comp, inside].astype(jnp.float32)
            target[here] = value
        return carry

    lax.fori_loop(0, blocks, place, 0, unroll=blocks <= 8)


def chunk_modes(modes, chunk):
    part = modes // 4
    return [core * 2 * part + chunk * part + i for core in range(2) for i in range(part)]


def first_kernel(blocks, meta_ref, offs_ref, tile_ref, mine_ref, other_ref, probe_ref, amp_ref, table_ref,
                 keep_ref, send_ref, patch_ref, later_ref, acc_ref, pad_ref, far_ref, pg_ref):
    modes, _, width, _ = probe_ref.shape
    half = width // 2
    core, side = meta_ref[1], meta_ref[2]
    for source, at in ((mine_ref, core), (other_ref, 1 - core)):
        margin = pl.ds(pl.multiple_of(at * 3 * half, half), half)
        strip = pl.ds(pl.multiple_of((at + 1) * half, half), half)
        pad_ref[:, 1, margin] = source[:, :, :half]
        pad_ref[:, 2, margin] = source[:, :, half:width]
        for step in range(2):
            block = side if step == 0 else 3 - side
            start = width + step * width
            if start < source.shape[-1]:
                pad_ref[:, block, strip] = source[:, :, start : start + half]
                pad_ref[:, block, margin] = source[:, :, start + half : start + width]
            else:
                pad_ref[:, block, strip] = jnp.zeros((2, half, half), jnp.float32)
                pad_ref[:, block, margin] = jnp.zeros((2, half, half), jnp.float32)
    for j in range(2):
        pad_ref[:, 1 + j, half : half + width] = tile_ref[:, :, j * half : (j + 1) * half]
    pg_ref[...] = jnp.zeros_like(pg_ref)
    rows, cols = table_ref[0], table_ref[1]
    now, later = chunk_modes(modes, 0), chunk_modes(modes, 1)

    def visit(s, carry):
        row = offs_ref[0, s]
        col = offs_ref[1, s]
        block = jnp.where(col >= half, 1, 0)
        shift = col - block * half
        for comp in range(2):
            win = jnp.concatenate([pad_ref[comp, block + j, pl.ds(row, width), :] for j in range(3)], axis=1)
            patch_ref[s, comp] = pltpu.roll(win, lax.rem(width + half - shift, width + half), 1)[:, :width]
        inten = None
        for m in range(modes):
            qr = probe_ref[m, 0].astype(jnp.float32)
            qi = probe_ref[m, 1].astype(jnp.float32)
            pr = patch_ref[s, 0]
            pi = patch_ref[s, 1]
            psi_r = (qr * pr - qi * pi).astype(jnp.bfloat16)
            psi_i = (qr * pi + qi * pr).astype(jnp.bfloat16)
            yr, yi = split(dot(rows, psi_r), dot(rows, psi_i), 0)
            y = dot(jnp.concatenate([yr, yi], 0).astype(jnp.bfloat16), cols)
            fr, fi = split(y[:width], y[width:], 1)
            far_ref[m, 0] = fr
            far_ref[m, 1] = fi
            power = fr * fr + fi * fi
            inten = power if inten is None else inten + power
        scale = 1.0 / (width * width)
        factor = scale - amp_ref[s] * scale * lax.rsqrt(inten * scale + floor_term)
        total = None
        for m in now:
            ur, ui = fold(far_ref[m, 0] * factor, far_ref[m, 1] * factor, 0)
            at, term = mode_terms(ur, ui, probe_ref, m, patch_ref[s, 0], patch_ref[s, 1], rows, cols)
            total = at if total is None else (total[0] + at[0], total[1] + at[1])
            for comp in range(2):
                pg_ref[now.index(m), comp] += term[comp]
        for comp in range(2):
            acc_ref[s, comp] = total[comp]
        for m in later:
            ur, ui = fold(far_ref[m, 0] * factor, far_ref[m, 1] * factor, 0)
            later_ref[s, later.index(m), 0] = ur
            later_ref[s, later.index(m), 1] = ui
        return carry

    lax.fori_loop(0, meta_ref[0], visit, 0)
    place_shares(meta_ref, probe_ref, pg_ref, keep_ref, send_ref, 0, blocks)


def second_kernel(blocks, meta_ref, offs_ref, tile_ref, probe_ref, table_ref, patch_ref, later_ref, acc_ref,
                  keep_ref, send_ref, keep_grad_ref, send_grad_ref, grad_ref, pg_ref):
    modes, _, width, _ = probe_ref.shape
    half = width // 2
    core = meta_ref[1]
    grad_ref[...] = jnp.zeros_like(grad_ref)
    pg_ref[...] = jnp.zeros_like(pg_ref)
    rows, cols = table_ref[0], table_ref[1]
    later = chunk_modes(modes, 1)

    def visit(s, carry):
        row = offs_ref[0, s]
        col = offs_ref[1, s]
        block = jnp.where(col >= half, 1, 0)
        shift = col - block * half
        total = (acc_ref[s, 0], acc_ref[s, 1])
        for i, m in enumerate(later):
            at, term = mode_terms(later_ref[s, i, 0], later_ref[s, i, 1], probe_ref, m,
                                  patch_ref[s, 0], patch_ref[s, 1], rows, cols)
            total = (total[0] + at[0], total[1] + at[1])
            for comp in range(2):
                pg_ref[i, comp] += term[comp]
        for comp in range(2):
            wide = jnp.concatenate([total[comp], jnp.zeros((width, half), jnp.float32)], axis=1)
            wide = pltpu.roll(wide, shift, 1)
            for j in range(3):
                at = (comp, block + j, pl.ds(row, width), slice(None))
                grad_ref[at] = grad_ref[at] + wide[:, j * half : (j + 1) * half]
        return carry

    lax.fori_loop(0, meta_ref[0], visit, 0)
    place_shares(meta_ref, probe_ref, pg_ref, keep_ref, send_ref, 1, blocks)
    for target, at in ((keep_grad_ref, core), (send_grad_ref, 1 - core)):
        main = pl.ds(pl.multiple_of((at + 1) * half, half), half)
        margin = pl.ds(pl.multiple_of((1 - at) * 3 * half, half), half)
        target[0] = -field_rate * grad_ref[:, :, main]
        target[1] = -field_rate * grad_ref[:, :, margin]
    inner = pl.ds(pl.multiple_of(core * half, half), half)
    for j in range(2):
        keep_grad_ref[0, :, 1 + j] += tile_ref[:, inner, j * half : (j + 1) * half]


def prepare(probe, amp):
    width = probe.shape[-1]

    def body(probe_hbm, amp_hbm, probe_ref, amp_ref, table_ref, raw_ref, sems):
        copies = [
            pltpu.make_async_copy(source, target, sems.at[i])
            for i, (source, target) in enumerate([(amp_hbm, raw_ref), (probe_hbm, probe_ref)])
        ]
        for copy in copies:
            copy.start()
        for axis in range(2):
            table_ref[axis] = half_spectrum_table(width, axis)
        select = half_spectrum_select(width)
        copies[0].wait()

        def order(s, carry):
            amp_ref[s] = dot(dot(select, raw_ref[s]).astype(jnp.bfloat16), select)
            return carry

        lax.fori_loop(0, raw_ref.shape[0], order, 0)
        copies[1].wait()

    vmem = pl.BlockSpec(memory_space=pltpu.VMEM)
    hbm = pl.BlockSpec(memory_space=pl.ANY)
    return pl.pallas_call(
        body,
        out_shape=(
            jax.ShapeDtypeStruct(probe.shape, jnp.bfloat16),
            jax.ShapeDtypeStruct(amp.shape, jnp.float32),
            jax.ShapeDtypeStruct((2, width, width), jnp.bfloat16),
        ),
        in_specs=[hbm] * 2,
        out_specs=(vmem,) * 3,
        scratch_shapes=[
            pltpu.VMEM(amp.shape, jnp.bfloat16),
            pltpu.SemaphoreType.DMA((2,)),
        ],
        compiler_params=pltpu.CompilerParams(vmem_limit_bytes=51 * 2**20),
        cost_estimate=pl.CostEstimate(flops=2 * 10**8, bytes_accessed=4 * 2**20, transcendentals=0),
    )(probe, amp)


def first_scans(blocks, meta, offs, tile, mine, other, probe, amp, tables):
    modes, _, width, _ = probe.shape
    half = width // 2
    slots = amp.shape[0]
    part = modes // 4
    smem = pl.BlockSpec(memory_space=pltpu.SMEM)
    vmem = pl.BlockSpec(memory_space=pltpu.VMEM)
    share = jax.ShapeDtypeStruct((part * 2 * width, width), jnp.float32)
    image = jax.ShapeDtypeStruct((slots, 2, width, width), jnp.float32)
    return pl.pallas_call(
        functools.partial(first_kernel, blocks),
        out_shape=(share, share, image, jax.ShapeDtypeStruct((slots, 2 * part, 2, width, width), jnp.bfloat16), image),
        in_specs=[smem] * 2 + [vmem] * 6,
        out_specs=(vmem,) * 5,
        scratch_shapes=[
            pltpu.VMEM((2, 4, 2 * width, half), jnp.float32),
            pltpu.VMEM((modes, 2, width, width), jnp.float32),
            pltpu.VMEM((2 * part, 2, width, width), jnp.float32),
        ],
        compiler_params=pltpu.CompilerParams(vmem_limit_bytes=24 * 2**20),
        cost_estimate=pl.CostEstimate(flops=4 * 10**9, bytes_accessed=8 * 2**20, transcendentals=0),
    )(meta, offs, tile, mine, other, probe, amp, tables)


def second_scans(blocks, meta, offs, tile, probe, tables, patch, later, acc):
    modes, _, width, _ = probe.shape
    half = width // 2
    part = modes // 4
    smem = pl.BlockSpec(memory_space=pltpu.SMEM)
    vmem = pl.BlockSpec(memory_space=pltpu.VMEM)
    grad = jax.ShapeDtypeStruct((2, 2, 4, half, half), jnp.float32)
    share = jax.ShapeDtypeStruct((part * 2 * width, width), jnp.float32)
    return pl.pallas_call(
        functools.partial(second_kernel, blocks),
        out_shape=(share, share, grad, grad),
        in_specs=[smem] * 2 + [vmem] * 6,
        out_specs=(vmem,) * 4,
        scratch_shapes=[
            pltpu.VMEM((2, 4, 2 * width, half), jnp.float32),
            pltpu.VMEM((2 * part, 2, width, width), jnp.float32),
        ],
        compiler_params=pltpu.CompilerParams(vmem_limit_bytes=24 * 2**20),
        cost_estimate=pl.CostEstimate(flops=2 * 10**9, bytes_accessed=8 * 2**20, transcendentals=0),
    )(meta, offs, tile, probe, tables, patch, later, acc)


def route(target):
    rows, cols, cores = (lax.axis_size(a) for a in grid_axes)
    pairs = []
    for z in range(rows):
        for x in range(cols):
            for c in range(cores):
                to = target(z, x, c)
                if to is not None and 0 <= to[0] < rows and 0 <= to[1] < cols:
                    pairs.append(((z * cols + x) * cores + c, (to[0] * cols + to[1]) * cores + to[2]))
    return pairs


def move(block, target):
    return lax.ppermute(block, grid_axes, route(target))


def across(x, step):
    return x + 1 if x % 2 == step else x - 1


def down(z, c):
    return z + 1 if c == 0 else z - 1


def swap_cores(block):
    return move(block, lambda z, x, c: (z, x, 1 - c))


def axis_bits(axis):
    return [(axis, b) for b in range(lax.axis_size(axis).bit_length() - 1)]


def reduce_orders():
    first, second = axis_bits("yt"), axis_bits("xt")
    a, b = [], []
    for i in range(max(len(first), len(second))):
        pair = first[i : i + 1] + second[i : i + 1]
        a += pair
        b += pair[::-1]
    return list(zip(a, b))


def flip(order):
    def target(z, x, c):
        axis, bit = order[c]
        return (z ^ (1 << bit), x, c) if axis == "xt" else (z, x ^ (1 << bit), c)

    return target


def bits_of(orders, core):
    total = 0
    for order in orders:
        bits = [(lax.axis_index(axis) >> bit) & 1 for axis, bit in order]
        total = total * 2 + jnp.where(core == 0, bits[0], bits[1])
    return total


def small_call(body, outs, args, meta=None):
    vmem = pl.BlockSpec(memory_space=pltpu.VMEM)
    extra = [] if meta is None else [meta]
    return pl.pallas_call(
        body,
        out_shape=tuple(jax.ShapeDtypeStruct(shape, jnp.float32) for shape in outs),
        in_specs=[pl.BlockSpec(memory_space=pltpu.SMEM)] * len(extra) + [vmem] * len(args),
        out_specs=(vmem,) * len(outs),
        compiler_params=pltpu.CompilerParams(vmem_limit_bytes=6 * 2**20),
        cost_estimate=pl.CostEstimate(flops=10**6, bytes_accessed=2**20, transcendentals=0),
    )(*extra, *args)


def add_split(own, got):
    rows, lanes = own.shape
    cut = rows // 2

    def body(a, b, low, high):
        high[...] = a[cut:] + b[cut:]
        low[...] = a[:cut] + b[:cut]

    return small_call(body, [(cut, lanes)] * 2, [own, got])


def add(own, got):
    def body(a, b, out):
        out[...] = a[...] + b[...]

    return small_call(body, [own.shape], [own, got])[0]


def stack(own, got):
    rows, lanes = own.shape

    def body(a, b, out):
        out[:rows] = a[...]
        out[rows:] = b[...]

    return small_call(body, [(2 * rows, lanes)], [own, got])[0]


def strips(field, meta, steps):
    _, tile, width = field.shape
    half = width // 2

    def body(meta_ref, tile_ref, outer_ref, *refs):
        sems = refs[-1]
        core, odd = meta_ref[0], meta_ref[1]
        outer = pl.ds(pl.multiple_of((1 - core) * half, half), half)
        inner = pl.ds(pl.multiple_of(core * half, half), half)
        copies = [pltpu.make_async_copy(tile_ref.at[:, outer], outer_ref, sems.at[0])]
        for step in range(steps):
            at = odd if step == 1 else 1 - odd
            cols = pl.ds(pl.multiple_of(at * half, half), half)
            for i, rows in enumerate((inner, outer)):
                n = 2 * step + i
                copies.append(pltpu.make_async_copy(tile_ref.at[:, rows, cols], refs[n], sems.at[1 + n]))
        for copy in copies:
            copy.start()
        for copy in copies:
            copy.wait()

    vmem = pl.BlockSpec(memory_space=pltpu.VMEM)
    shapes = [(2, half, width)] + [(2, half, half)] * (2 * steps)
    return pl.pallas_call(
        body,
        out_shape=tuple(jax.ShapeDtypeStruct(shape, jnp.float32) for shape in shapes),
        in_specs=[pl.BlockSpec(memory_space=pltpu.SMEM), pl.BlockSpec(memory_space=pl.ANY)],
        out_specs=(vmem,) * len(shapes),
        scratch_shapes=[pltpu.SemaphoreType.DMA((1 + 2 * steps,))],
        compiler_params=pltpu.CompilerParams(vmem_limit_bytes=6 * 2**20),
        cost_estimate=pl.CostEstimate(flops=10**6, bytes_accessed=2**20, transcendentals=0),
    )(meta, field)


def fold_sends(keep, got, meta, steps):
    half = keep.shape[-1]

    def body(meta_ref, a, b, *refs):
        mid_ref, refs = refs[-1], refs[:-1]
        for step in range(steps):
            block = meta_ref[2] if step == 0 else 3 - meta_ref[2]
            refs[step][...] = a[:, :, block] + b[:, :, block]
        mid_ref[...] = a[:, :, 1:3] + b[:, :, 1:3]

    shapes = [(2, 2, half, half)] * steps + [(2, 2, 2, half, half)]
    *edges, mid = small_call(body, shapes, [keep, got], meta)
    return edges, mid


def fold_join(mid, arrived, meta):
    half = mid.shape[-1]

    def body(meta_ref, mid_ref, *refs):
        down_ref, main_ref = refs[-2:]
        for j in range(2):
            total = mid_ref[:, :, j]
            for step, ref in enumerate(refs[:-2]):
                total += jnp.where((meta_ref[6] + step + j) % 2 == 1, 1.0, 0.0) * ref[...]
            main_ref[:, j] = total[0]
            down_ref[:, j] = total[1]

    return small_call(body, [(2, 2, half, half)] * 2, [mid, *arrived], meta)


def fold_finish(main, below):
    half = main.shape[-1]

    def body(main_ref, below_ref, out_ref):
        for j in range(2):
            out_ref[:, :, j * half : (j + 1) * half] = main_ref[:, j] + below_ref[:, j]

    return small_call(body, [(2, half, 2 * half)], [main, below])[0]


def place_probe(chunks, meta, blocks, shape, sibling, into=None):
    modes, _, width, _ = shape
    share = modes // 2
    part = share // 2
    size = part * 2 * width // blocks
    given = [] if into is None else [into]

    def body(meta_ref, *refs):
        sem = refs[-1]
        out_ref = refs[-2]
        at = 1 - meta_ref[1] if sibling else meta_ref[1]
        bits = meta_ref[4] if sibling else meta_ref[3]

        def copies(p):
            found = []
            for k in range(2):
                line = ((at * share + k * part) * 2 * width) + (p ^ bits) * size
                target = out_ref.at[line // (2 * width), line % (2 * width) // width,
                                    pl.ds(pl.multiple_of(line % width, size), size)]
                here = refs[k].at[pl.ds(pl.multiple_of(p * size, size), size)]
                found.append(pltpu.make_async_copy(here, target, sem.at[p, k]))
            return found

        def start(p, carry):
            for copy in copies(p):
                copy.start()
            return carry

        def wait(p, carry):
            for copy in copies(p):
                copy.wait()
            return carry

        lax.fori_loop(0, blocks, start, 0)
        lax.fori_loop(0, blocks, wait, 0)

    anywhere = pl.BlockSpec(memory_space=pl.ANY)
    return pl.pallas_call(
        body,
        out_shape=jax.ShapeDtypeStruct(shape, jnp.float32),
        in_specs=[pl.BlockSpec(memory_space=pltpu.SMEM)] + [anywhere] * (2 + len(given)),
        out_specs=anywhere,
        input_output_aliases={3: 0} if given else {},
        scratch_shapes=[pltpu.SemaphoreType.DMA((blocks, 2))],
        compiler_params=pltpu.CompilerParams(vmem_limit_bytes=6 * 2**20),
        cost_estimate=pl.CostEstimate(flops=10**6, bytes_accessed=2**21, transcendentals=0),
    )(meta, *chunks, *given)


def shards(field, probe, amplitudes, offsets, counts):
    modes, _, width, _ = probe.shape
    per_device = amplitudes.shape[2]
    core = lax.axis_index("sg")
    odd = lax.axis_index("yt") % 2
    steps = min(2, lax.axis_size("yt") - 1)
    orders = reduce_orders()
    early, last = orders[:-1], orders[-1]
    blocks = 2 ** len(early)
    live = jnp.clip(counts[0, 0] - core * per_device, 0, per_device)
    side = jnp.where(odd == 0, 3, 0)
    base = jnp.where((lax.axis_index("xt") == 0) & (lax.axis_index("yt") == 0), 1, 0)
    meta = jnp.stack(
        [live, core, side, bits_of(early, core), bits_of(early, 1 - core), base, odd]
    ).astype(jnp.int32)
    offs = offsets[0, 0].T
    place = jnp.stack([core, odd]).astype(jnp.int32)

    outer, *edges = strips(field, place, steps)
    prepared = prepare(probe, amplitudes[0, 0])
    parts = [move(outer, lambda z, x, c: (down(z, c), x, c))]
    for step in range(steps):
        parts.append(move(edges[2 * step], lambda z, x, c: (z, across(x, step), c)))
        parts.append(move(edges[2 * step + 1], lambda z, x, c: (down(z, c), across(x, step), c)))
    parts, prepared, meta = lax.optimization_barrier((parts, prepared, meta))
    mine = jnp.concatenate(parts, axis=2)
    other = swap_cores(mine)

    probe_now, amp_now, tables = prepared
    keep, send, *kept = first_scans(blocks, meta, offs, field, mine, other, probe_now, amp_now, tables)
    second = second_scans(blocks, meta, offs, field, probe_now, tables, *kept)
    received, second = lax.optimization_barrier((swap_cores(send), second))
    keep2, send2, keep_grad, send_grad = second
    pairs = [add_split(keep, received), add_split(keep2, swap_cores(send2))]
    got = [move(high, flip(early[0])) for _, high in pairs]
    edges, mid = fold_sends(keep_grad, swap_cores(send_grad), meta, steps)
    arrived = [
        move(edge, lambda z, x, c, step=step: (z, across(x, step), c)) for step, edge in enumerate(edges)
    ]
    for order in early[1:]:
        pairs = [add_split(low, g) for (low, _), g in zip(pairs, got)]
        got = [move(high, flip(order)) for _, high in pairs]
    parts = [add(low, g) for (low, _), g in zip(pairs, got)]
    parts = [add(p, move(p, flip(last))) for p in parts]
    parts[1], arrived = lax.optimization_barrier((parts[1], arrived))
    down_part, main = fold_join(mid, arrived, meta)
    below = move(down_part, lambda z, x, c: (down(z, c), x, c))
    for order in early[::-1]:
        parts = [stack(p, move(p, flip(order))) for p in parts]
    parts[0], below = lax.optimization_barrier((parts[0], below))
    new_field = fold_finish(main, below)
    theirs = [swap_cores(p) for p in parts]
    new_probe = place_probe(parts, meta, blocks, probe.shape, False)
    new_probe = place_probe(theirs, meta, blocks, probe.shape, True, new_probe)
    return (new_field, new_probe)


def solution(mesh):
    in_specs = (
        P(None, ("groups", "xt"), "yt"),
        P("groups", None, None, None),
        P(("groups", "xt"), "yt", "sg", None, None),
        P(("groups", "xt"), "yt", "sg", None),
        P(("groups", "xt"), "yt"),
    )
    out_specs = (P(None, ("groups", "xt", "sg"), "yt"), P("groups", None, None, None))
    return jax.shard_map(shards, mesh=mesh, in_specs=in_specs, out_specs=out_specs, check_vma=False)
```

time: 106 us -> 76.2 us (0.72)
  waiting for transfers between devices: 46.2 us -> 24.5 us
  Pallas kernels: 5.43 us -> 19.7 us
  other arithmetic: 8.62 us -> 0.08 us
  local copies, waits for them, and re-layouts: 10.5 us -> 2.18 us
  starting transfers between devices: 33 us -> 27.9 us
    ppermute x15 -> x21, waiting for transfers between devices: 46.2 us -> 24.5 us  [move(): return lax.ppermute(block, grid_axes, route(target))]
    pallas_call x1 -> x21, Pallas kernels: 5.43 us -> 19.7 us  [the longest x1 7.75 us: first_scans(): pl.pallas_call(functools.partial(first_kernel, blocks), out_shape=(share,...]
    unnamed x26 -> x10, local copies, waits for them, and re-layouts: 7.76 us -> 2.08 us
    ppermute x15 -> x21, starting transfers between devices: 33 us -> 27.9 us  [move(): return lax.ppermute(block, grid_axes, route(target))]
    select_n x3 -> x0, other arithmetic: 3.95 us -> none  [joined(): jnp.where(bit == 0, jnp.concatenate([own, other], 0), jnp.concatenate([ot...]
    add x6 -> x0, other arithmetic: 3.81 us -> none  [the longest x2 2.25 us: new_probe_share(): part = pick(part, bit) + got]
    dynamic_slice x4 -> x0, local copies, waits for them, and re-layouts: 2.25 us -> none  [the longest x1 1.13 us: shards(): lax.dynamic_slice_in_dim(outer, start, half, 2)]
  transfers between devices with their start and end apart: 15 -> 21, of which waited for: 11 -> 11; matrix products, arithmetic and copies ran while one was open for 4% -> 0% of each run, Pallas kernels for 0% -> 13%
where the time goes in v2:
time: 76.2 us; the launch traced here: 76 us
  starting transfers between devices  27.9 us (37%)
  waiting for transfers between devices  24.5 us (32%)
  Pallas kernels  19.7 us (26%)
  local copies, waits for them, and re-layouts  2.18 us (3%)
  between operations  1.6 us (2%)
    ppermute x21, starting transfers between devices, move(): return lax.ppermute(block, grid_axes, route(target))  27.9 us
    ppermute x21, waiting for transfers between devices, move(): return lax.ppermute(block, grid_axes, route(target))  24.5 us
    pallas_call x1, Pallas kernels, first_scans(): pl.pallas_call(functools.partial(first_kernel, blocks), out_shape=(share,...  7.75 us
    pallas_call x1, Pallas kernels, second_scans(): pl.pallas_call(functools.partial(second_kernel, blocks), out_shape=(share...  4.13 us
    pallas_call x2, Pallas kernels, place_probe(): pl.pallas_call(body, out_shape=jax.ShapeDtypeStruct(shape, jnp.float32),...  3.17 us
    pallas_call x15, Pallas kernels, small_call(): pl.pallas_call(body, out_shape=tuple((jax.ShapeDtypeStruct(shape, jnp.flo...  2.29 us
    unnamed x10, local copies, waits for them, and re-layouts  2.08 us
    pallas_call x1, Pallas kernels, prepare(): pl.pallas_call(body, out_shape=(jax.ShapeDtypeStruct(probe.shape, jnp.bfl...  1.68 us
  transfers between devices with their start and end apart: 21, of which 11 were waited for; matrix products, arithmetic and copies ran while one was open for 0% of the time, Pallas kernels for 13%

profile of v2, /device:TPU:0, one launch (start us, length us, event | category | flops | bytes accessed | tf_op | source)
XLA Modules:
  0.0 76.0 jit_solution(11184036820066684895)
XLA Ops:
  2.4 4.9 %collective-permute-start = (f32[2,128,256]{2,1,0:T(8,128)S(1)}, f32[2,128,256]{2,1,0:T(8,128)S(1)}, u32[]{:S(2)}, u32[]{:S(2)}) collective-permute-start(f32[2,128,256]{2,1,0:T(8,128)S(1)} %get-tuple-element.45), channel_id=1, source_target_pairs={{0,4},{2,6},{4,8},{5,1},{6,10},{7,3},{8,12},{9,5},{10,14},{11,7},{... | collective-permute-start | bytes 786440 | tf_op jit(solution)/shard_map/ppermute | solution.py:331
  7.4 1.6 %collective-permute-start.1 = (f32[2,128,128]{2,1,0:T(8,128)S(1)}, f32[2,128,128]{2,1,0:T(8,128)S(1)}, u32[]{:S(2)}, u32[]{:S(2)}) collective-permute-start(f32[2,128,128]{2,1,0:T(8,128)S(1)} %get-tuple-element.46), channel_id=1, source_target_pairs={{0,2},{1,3},{2,0},{3,1},{4,6},{5,7},{6,4},{7,5},{8,10},{9,11},{10,... | collective-permute-start | bytes 393224 | tf_op jit(solution)/shard_map/ppermute | solution.py:331
  8.9 3.4 %collective-permute-start.2 = (f32[2,128,128]{2,1,0:T(8,128)S(1)}, f32[2,128,128]{2,1,0:T(8,128)S(1)}, u32[]{:S(2)}, u32[]{:S(2)}) collective-permute-start(f32[2,128,128]{2,1,0:T(8,128)S(1)} %get-tuple-element.47), channel_id=1, source_target_pairs={{0,6},{2,4},{4,10},{5,3},{6,8},{7,1},{8,14},{9,7},{10,12},{11,5},{... | collective-permute-start | bytes 393224 | tf_op jit(solution)/shard_map/ppermute | solution.py:331
  14.1 1.7 %shard_map.69 = (bf16[4,2,256,256]{3,2,1,0:T(8,128)(2,1)S(1)}, f32[3,256,256]{2,1,0:T(8,128)S(1)}, bf16[2,256,256]{2,1,0:T(8,128)(2,1)S(1)}) custom-call(bf16[4,2,256,256]{3,2,1,0:T(8,128)(2,1)} %probe_hbm.1, bf16[3,256,256]{2,1,0:T(8,128)(2,1)S(1)} %bitcast.13), custom_call_target="tpu_custom_call" | custom-call | flops 200000000 | bytes 4194304 | tf_op jit(solution)/shard_map/pallas_call | solution.py:254
  16.0 1.9 %collective-permute-done.3.other_ref = f32[2,128,512]{2,1,0:T(8,128)S(1)} collective-permute-done((f32[2,128,512]{2,1,0:T(8,128)S(1)}, f32[2,128,512]{2,1,0:T(8,128)S(1)}, u32[]{:S(2)}, u32[]{:S(2)}) %collective-permute-start.3) | collective-permute-done | bytes 524320 | tf_op jit(solution)/shard_map/ppermute | solution.py:331
  17.9 7.8 %shard_map.70 = (f32[512,256]{1,0:T(8,128)S(1)}, f32[512,256]{1,0:T(8,128)S(1)}, f32[3,2,256,256]{3,2,1,0:T(8,128)S(1)}, bf16[3,2,2,256,256]{4,3,2,1,0:T(8,128)(2,1)S(1)}, f32[3,2,256,256]{3,2,1,0:T(8,128)S(1)}) custom-call(s32[7]{0:T(128)S(1)} %stack.37.meta_ref, s32[2,3]{1,0:T(2,128)S(1)} %bitcast.14, f32[2,256,256]{2,1,0:T(8,128)S(1)} %copy-done.1, ...), custom_call_target="tpu_custom_call" | custom-call | flops 4000000000 | bytes 8388608 | tf_op jit(solution)/shard_map/pallas_call | solution.py:281
  25.7 4.1 %shard_map.71 = (f32[512,256]{1,0:T(8,128)S(1)}, f32[512,256]{1,0:T(8,128)S(1)}, f32[2,2,4,128,128]{4,3,2,1,0:T(8,128)S(1)}, f32[2,2,4,128,128]{4,3,2,1,0:T(8,128)S(1)}) custom-call(s32[7]{0:T(128)S(1)} %stack.37.meta_ref, s32[2,3]{1,0:T(2,128)S(1)} %bitcast.15, f32[2,256,256]{2,1,0:T(8,128)S(1)} %copy-done.1, ...), custom_call_target="tpu_custom_call" | custom-call | flops 2000000000 | bytes 8388608 | tf_op jit(solution)/shard_map/pallas_call | solution.py:304
  30.5 1.6 %collective-permute-start.11 = (f32[256,256]{1,0:T(8,128)S(1)}, f32[256,256]{1,0:T(8,128)S(1)}, u32[]{:S(2)}, u32[]{:S(2)}) collective-permute-start(f32[256,256]{1,0:T(8,128)S(1)} %get-tuple-element.81), channel_id=1, source_target_pairs={{0,2},{1,5},{2,0},{3,7},{4,6},{5,1},{6,4},{7,3},{8,10},{9,13},{10,... | collective-permute-start | bytes 786440 | tf_op jit(solution)/shard_map/ppermute | solution.py:331
  32.1 1.2 %collective-permute-done.6.b = f32[512,256]{1,0:T(8,128)S(1)} collective-permute-done((f32[512,256]{1,0:T(8,128)S(1)}, f32[512,256]{1,0:T(8,128)S(1)}, u32[]{:S(2)}, u32[]{:S(2)}) %collective-permute-start.6) | collective-permute-done | bytes 524320 | tf_op jit(solution)/shard_map/ppermute | solution.py:331
  33.4 1.6 %collective-permute-start.7 = (f32[256,256]{1,0:T(8,128)S(1)}, f32[256,256]{1,0:T(8,128)S(1)}, u32[]{:S(2)}, u32[]{:S(2)}) collective-permute-start(f32[256,256]{1,0:T(8,128)S(1)} %get-tuple-element.72), channel_id=1, source_target_pairs={{0,2},{1,5},{2,0},{3,7},{4,6},{5,1},{6,4},{7,3},{8,10},{9,13},{10,... | collective-permute-start | bytes 786440 | tf_op jit(solution)/shard_map/ppermute | solution.py:331
  35.0 1.9 %collective-permute-done.11.b = f32[256,256]{1,0:T(8,128)S(1)} collective-permute-done((f32[256,256]{1,0:T(8,128)S(1)}, f32[256,256]{1,0:T(8,128)S(1)}, u32[]{:S(2)}, u32[]{:S(2)}) %collective-permute-start.11) | collective-permute-done | bytes 262176 | tf_op jit(solution)/shard_map/ppermute | solution.py:331
  37.0 1.1 %collective-permute-start.12 = (f32[128,256]{1,0:T(8,128)S(1)}, f32[128,256]{1,0:T(8,128)S(1)}, u32[]{:S(2)}, u32[]{:S(2)}) collective-permute-start(f32[128,256]{1,0:T(8,128)S(1)} %get-tuple-element.83), channel_id=1, source_target_pairs={{0,4},{1,3},{2,6},{3,1},{4,0},{5,7},{6,2},{7,5},{8,12},{9,11},{10,... | collective-permute-start | bytes 393224 | tf_op jit(solution)/shard_map/ppermute | solution.py:331
  38.1 2.7 %collective-permute-done.7.b = f32[256,256]{1,0:T(8,128)S(1)} collective-permute-done((f32[256,256]{1,0:T(8,128)S(1)}, f32[256,256]{1,0:T(8,128)S(1)}, u32[]{:S(2)}, u32[]{:S(2)}) %collective-permute-start.7) | collective-permute-done | bytes 262176 | tf_op jit(solution)/shard_map/ppermute | solution.py:331
  42.3 2.4 %collective-permute-start.10 = (f32[2,2,128,128]{3,2,1,0:T(8,128)S(1)}, f32[2,2,128,128]{3,2,1,0:T(8,128)S(1)}, u32[]{:S(2)}, u32[]{:S(2)}) collective-permute-start(f32[2,2,128,128]{3,2,1,0:T(8,128)S(1)} %get-tuple-element.75), channel_id=1, source_target_pairs={{0,2},{1,3},{2,0},{3,1},{4,6},{5,7},{6,4},{7,5},{8,10},{9,11},{10,... | collective-permute-start | bytes 786440 | tf_op jit(solution)/shard_map/ppermute | solution.py:331
  45.9 4.0 %collective-permute-start.9 = (f32[128,256]{1,0:T(8,128)S(1)}, f32[128,256]{1,0:T(8,128)S(1)}, u32[]{:S(2)}, u32[]{:S(2)}) collective-permute-start(f32[128,256]{1,0:T(8,128)S(1)} %shard_map.75.a), channel_id=1, source_target_pairs={{0,8},{1,9},{2,10},{3,11},{4,12},{5,13},{6,14},{7,15},{8,0},{9,1},... | collective-permute-start | bytes 393224 | tf_op jit(solution)/shard_map/ppermute | solution.py:331
  49.8 5.8 %collective-permute-done.13.b = f32[128,256]{1,0:T(8,128)S(1)} collective-permute-done((f32[128,256]{1,0:T(8,128)S(1)}, f32[128,256]{1,0:T(8,128)S(1)}, u32[]{:S(2)}, u32[]{:S(2)}) %collective-permute-start.13) | collective-permute-done | bytes 131104 | tf_op jit(solution)/shard_map/ppermute | solution.py:331
  55.7 1.3 %collective-permute-done.9.b = f32[128,256]{1,0:T(8,128)S(1)} collective-permute-done((f32[128,256]{1,0:T(8,128)S(1)}, f32[128,256]{1,0:T(8,128)S(1)}, u32[]{:S(2)}, u32[]{:S(2)}) %collective-permute-start.9) | collective-permute-done | bytes 131104 | tf_op jit(solution)/shard_map/ppermute | solution.py:331
  57.8 4.2 %collective-permute-done.14.b = f32[128,256]{1,0:T(8,128)S(1)} collective-permute-done((f32[128,256]{1,0:T(8,128)S(1)}, f32[128,256]{1,0:T(8,128)S(1)}, u32[]{:S(2)}, u32[]{:S(2)}) %collective-permute-start.14) | collective-permute-done | bytes 131104 | tf_op jit(solution)/shard_map/ppermute | solution.py:331
  63.7 1.7 %collective-permute-start.16 = (f32[2,2,128,128]{3,2,1,0:T(8,128)S(1)}, f32[2,2,128,128]{3,2,1,0:T(8,128)S(1)}, u32[]{:S(2)}, u32[]{:S(2)}) collective-permute-start(f32[2,2,128,128]{3,2,1,0:T(8,128)S(1)} %get-tuple-element.84), channel_id=1, source_target_pairs={{0,4},{2,6},{4,8},{5,1},{6,10},{7,3},{8,12},{9,5},{10,14},{11,7},{... | collective-permute-start | bytes 786440 | tf_op jit(solution)/shard_map/ppermute | solution.py:331
  65.5 1.2 %collective-permute-start.19 = (f32[256,256]{1,0:T(8,128)S(1)}, f32[256,256]{1,0:T(8,128)S(1)}, u32[]{:S(2)}, u32[]{:S(2)}) collective-permute-start(f32[256,256]{1,0:T(8,128)S(1)} %shard_map.85.a), channel_id=1, source_target_pairs={{0,2},{1,5},{2,0},{3,7},{4,6},{5,1},{6,4},{7,3},{8,10},{9,13},{10,... | collective-permute-start | bytes 786440 | tf_op jit(solution)/shard_map/ppermute | solution.py:331
  66.7 1.8 %collective-permute-done.15.b = f32[256,256]{1,0:T(8,128)S(1)} collective-permute-done((f32[256,256]{1,0:T(8,128)S(1)}, f32[256,256]{1,0:T(8,128)S(1)}, u32[]{:S(2)}, u32[]{:S(2)}) %collective-permute-start.15) | collective-permute-done | bytes 262176 | tf_op jit(solution)/shard_map/ppermute | solution.py:331
  69.3 2.6 %collective-permute-done.19.b = f32[256,256]{1,0:T(8,128)S(1)} collective-permute-done((f32[256,256]{1,0:T(8,128)S(1)}, f32[256,256]{1,0:T(8,128)S(1)}, u32[]{:S(2)}, u32[]{:S(2)}) %collective-permute-start.19) | collective-permute-done | bytes 262176 | tf_op jit(solution)/shard_map/ppermute | solution.py:331
  72.8 1.6 %shard_map.87.refs_2_ = f32[4,2,256,256]{3,2,1,0:T(8,128)} custom-call(s32[7]{0:T(128)S(1)} %stack.37.meta_ref, f32[512,256]{1,0:T(8,128)S(1)} %shard_map.83.refs_0_, f32[512,256]{1,0:T(8,128)S(1)} %shard_map.86.refs_1_), custom_call_target="tpu_custom_call" | custom-call | flops 1000000 | bytes 2097152 | tf_op jit(solution)/shard_map/pallas_call | solution.py:528
  74.4 1.6 %shard_map.88 = f32[4,2,256,256]{3,2,1,0:T(8,128)} custom-call(s32[7]{0:T(128)S(1)} %stack.37.meta_ref, f32[512,256]{1,0:T(8,128)S(1)} %collective-permute-done.17.refs_0_, f32[512,256]{1,0:T(8,128)S(1)} %collective-permute-done.20.refs_1_, f32[4,2,256,256]{3,2,1,0:T(8,128)} %shard_map.87.refs_2_), custom_call_target="tpu_custom_call", output_to_operand_aliasing={{}: (3, {})} | custom-call | flops 1000000 | bytes 2097152 | tf_op jit(solution)/shard_map/pallas_call | solution.py:528
  (52 shorter events, 10.6 us)
Async XLA Ops:
  0.6 17.3 %copy-start.3 = (s32[1,1,3,2]{2,3,1,0:T(2,128)S(1)}, s32[1,1,3,2]{2,3,1,0:T(2,128)}, u32[]{:S(2)}) copy-start(s32[1,1,3,2]{2,3,1,0:T(2,128)} %param.8) | copy-start | bytes 76
  0.7 1.0 %copy-start = (f32[2,256,256]{2,1,0:T(8,128)S(1)}, f32[2,256,256]{2,1,0:T(8,128)}, u32[]{:S(2)}) copy-start(f32[2,256,256]{2,1,0:T(8,128)} %tile_ref.5) | copy-start | bytes 1572868
  1.8 16.1 %copy-start.1 = (f32[2,256,256]{2,1,0:T(8,128)S(1)}, f32[2,256,256]{2,1,0:T(8,128)}, u32[]{:S(2)}) copy-start(f32[2,256,256]{2,1,0:T(8,128)} %tile_ref.5) | copy-start | bytes 1572868
  2.4 13.4 %collective-permute-start = (f32[2,128,256]{2,1,0:T(8,128)S(1)}, f32[2,128,256]{2,1,0:T(8,128)S(1)}, u32[]{:S(2)}, u32[]{:S(2)}) collective-permute-start(f32[2,128,256]{2,1,0:T(8,128)S(1)} %get-tuple-element.45), channel_id=1, source_target_pairs={{0,4},{2,6},{4,8},{5,1},{6,10},{7,3},{8,12},{9,5},{10,14},{11,7},{... | collective-permute-start | bytes 786440 | tf_op jit(solution)/shard_map/ppermute | solution.py:331
  7.4 8.5 %collective-permute-start.1 = (f32[2,128,128]{2,1,0:T(8,128)S(1)}, f32[2,128,128]{2,1,0:T(8,128)S(1)}, u32[]{:S(2)}, u32[]{:S(2)}) collective-permute-start(f32[2,128,128]{2,1,0:T(8,128)S(1)} %get-tuple-element.46), channel_id=1, source_target_pairs={{0,2},{1,3},{2,0},{3,1},{4,6},{5,7},{6,4},{7,5},{8,10},{9,11},{10,... | collective-permute-start | bytes 393224 | tf_op jit(solution)/shard_map/ppermute | solution.py:331
  8.9 6.9 %collective-permute-start.2 = (f32[2,128,128]{2,1,0:T(8,128)S(1)}, f32[2,128,128]{2,1,0:T(8,128)S(1)}, u32[]{:S(2)}, u32[]{:S(2)}) collective-permute-start(f32[2,128,128]{2,1,0:T(8,128)S(1)} %get-tuple-element.47), channel_id=1, source_target_pairs={{0,6},{2,4},{4,10},{5,3},{6,8},{7,1},{8,14},{9,7},{10,12},{11,5},{... | collective-permute-start | bytes 393224 | tf_op jit(solution)/shard_map/ppermute | solution.py:331
  15.9 2.0 %collective-permute-start.3 = (f32[2,128,512]{2,1,0:T(8,128)S(1)}, f32[2,128,512]{2,1,0:T(8,128)S(1)}, u32[]{:S(2)}, u32[]{:S(2)}) collective-permute-start(f32[2,128,512]{2,1,0:T(8,128)S(1)} %constant_dynamic-update-slice_fusion.mine_ref), channel_id=1, source_target_pairs={{0,1},{1,0},{2,3},{3,2},{4,5},{5,4},{6,7},{7,6},{8,9},{9,8},{10,11... | collective-permute-start | bytes 1572872 | tf_op jit(solution)/shard_map/ppermute | solution.py:331
  25.7 4.2 %collective-permute-start.4 = (f32[512,256]{1,0:T(8,128)S(1)}, f32[512,256]{1,0:T(8,128)S(1)}, u32[]{:S(2)}, u32[]{:S(2)}) collective-permute-start(f32[512,256]{1,0:T(8,128)S(1)} %get-tuple-element.58), channel_id=1, source_target_pairs={{0,1},{1,0},{2,3},{3,2},{4,5},{5,4},{6,7},{7,6},{8,9},{9,8},{10,11... | collective-permute-start | bytes 1572872 | tf_op jit(solution)/shard_map/ppermute | solution.py:331
  29.9 11.8 %collective-permute-start.5 = (f32[2,2,4,128,128]{4,3,2,1,0:T(8,128)S(1)}, f32[2,2,4,128,128]{4,3,2,1,0:T(8,128)S(1)}, u32[]{:S(2)}, u32[]{:S(2)}) collective-permute-start(f32[2,2,4,128,128]{4,3,2,1,0:T(8,128)S(1)} %get-tuple-element.67), channel_id=1, source_target_pairs={{0,1},{1,0},{2,3},{3,2},{4,5},{5,4},{6,7},{7,6},{8,9},{9,8},{10,11... | collective-permute-start | bytes 3145736 | tf_op jit(solution)/shard_map/ppermute | solution.py:331
  30.0 3.4 %collective-permute-start.6 = (f32[512,256]{1,0:T(8,128)S(1)}, f32[512,256]{1,0:T(8,128)S(1)}, u32[]{:S(2)}, u32[]{:S(2)}) collective-permute-start(f32[512,256]{1,0:T(8,128)S(1)} %get-tuple-element.70), channel_id=1, source_target_pairs={{0,1},{1,0},{2,3},{3,2},{4,5},{5,4},{6,7},{7,6},{8,9},{9,8},{10,11... | collective-permute-start | bytes 1572872 | tf_op jit(solution)/shard_map/ppermute | solution.py:331
  30.5 6.4 %collective-permute-start.11 = (f32[256,256]{1,0:T(8,128)S(1)}, f32[256,256]{1,0:T(8,128)S(1)}, u32[]{:S(2)}, u32[]{:S(2)}) collective-permute-start(f32[256,256]{1,0:T(8,128)S(1)} %get-tuple-element.81), channel_id=1, source_target_pairs={{0,2},{1,5},{2,0},{3,7},{4,6},{5,1},{6,4},{7,3},{8,10},{9,13},{10,... | collective-permute-start | bytes 786440 | tf_op jit(solution)/shard_map/ppermute | solution.py:331
  33.4 7.4 %collective-permute-start.7 = (f32[256,256]{1,0:T(8,128)S(1)}, f32[256,256]{1,0:T(8,128)S(1)}, u32[]{:S(2)}, u32[]{:S(2)}) collective-permute-start(f32[256,256]{1,0:T(8,128)S(1)} %get-tuple-element.72), channel_id=1, source_target_pairs={{0,2},{1,5},{2,0},{3,7},{4,6},{5,1},{6,4},{7,3},{8,10},{9,13},{10,... | collective-permute-start | bytes 786440 | tf_op jit(solution)/shard_map/ppermute | solution.py:331
  37.0 7.6 %collective-permute-start.12 = (f32[128,256]{1,0:T(8,128)S(1)}, f32[128,256]{1,0:T(8,128)S(1)}, u32[]{:S(2)}, u32[]{:S(2)}) collective-permute-start(f32[128,256]{1,0:T(8,128)S(1)} %get-tuple-element.83), channel_id=1, source_target_pairs={{0,4},{1,3},{2,6},{3,1},{4,0},{5,7},{6,2},{7,5},{8,12},{9,11},{10,... | collective-permute-start | bytes 393224 | tf_op jit(solution)/shard_map/ppermute | solution.py:331
  40.8 5.0 %collective-permute-start.8 = (f32[128,256]{1,0:T(8,128)S(1)}, f32[128,256]{1,0:T(8,128)S(1)}, u32[]{:S(2)}, u32[]{:S(2)}) collective-permute-start(f32[128,256]{1,0:T(8,128)S(1)} %get-tuple-element.74), channel_id=1, source_target_pairs={{0,4},{1,3},{2,6},{3,1},{4,0},{5,7},{6,2},{7,5},{8,12},{9,11},{10,... | collective-permute-start | bytes 393224 | tf_op jit(solution)/shard_map/ppermute | solution.py:331
  42.3 14.8 %collective-permute-start.10 = (f32[2,2,128,128]{3,2,1,0:T(8,128)S(1)}, f32[2,2,128,128]{3,2,1,0:T(8,128)S(1)}, u32[]{:S(2)}, u32[]{:S(2)}) collective-permute-start(f32[2,2,128,128]{3,2,1,0:T(8,128)S(1)} %get-tuple-element.75), channel_id=1, source_target_pairs={{0,2},{1,3},{2,0},{3,1},{4,6},{5,7},{6,4},{7,5},{8,10},{9,11},{10,... | collective-permute-start | bytes 786440 | tf_op jit(solution)/shard_map/ppermute | solution.py:331
  44.7 10.9 %collective-permute-start.13 = (f32[128,256]{1,0:T(8,128)S(1)}, f32[128,256]{1,0:T(8,128)S(1)}, u32[]{:S(2)}, u32[]{:S(2)}) collective-permute-start(f32[128,256]{1,0:T(8,128)S(1)} %shard_map.80.a), channel_id=1, source_target_pairs={{0,8},{1,9},{2,10},{3,11},{4,12},{5,13},{6,14},{7,15},{8,0},{9,1},... | collective-permute-start | bytes 393224 | tf_op jit(solution)/shard_map/ppermute | solution.py:331
  45.9 11.1 %collective-permute-start.9 = (f32[128,256]{1,0:T(8,128)S(1)}, f32[128,256]{1,0:T(8,128)S(1)}, u32[]{:S(2)}, u32[]{:S(2)}) collective-permute-start(f32[128,256]{1,0:T(8,128)S(1)} %shard_map.75.a), channel_id=1, source_target_pairs={{0,8},{1,9},{2,10},{3,11},{4,12},{5,13},{6,14},{7,15},{8,0},{9,1},... | collective-permute-start | bytes 393224 | tf_op jit(solution)/shard_map/ppermute | solution.py:331
  55.6 6.4 %collective-permute-start.14 = (f32[128,256]{1,0:T(8,128)S(1)}, f32[128,256]{1,0:T(8,128)S(1)}, u32[]{:S(2)}, u32[]{:S(2)}) collective-permute-start(f32[128,256]{1,0:T(8,128)S(1)} %shard_map.81.a), channel_id=1, source_target_pairs={{0,4},{1,3},{2,6},{3,1},{4,0},{5,7},{6,2},{7,5},{8,12},{9,11},{10,... | collective-permute-start | bytes 393224 | tf_op jit(solution)/shard_map/ppermute | solution.py:331
  57.0 8.4 %collective-permute-start.18 = (f32[128,256]{1,0:T(8,128)S(1)}, f32[128,256]{1,0:T(8,128)S(1)}, u32[]{:S(2)}, u32[]{:S(2)}) collective-permute-start(f32[128,256]{1,0:T(8,128)S(1)} %shard_map.76.a), channel_id=1, source_target_pairs={{0,4},{1,3},{2,6},{3,1},{4,0},{5,7},{6,2},{7,5},{8,12},{9,11},{10,... | collective-permute-start | bytes 393224 | tf_op jit(solution)/shard_map/ppermute | solution.py:331
  62.1 6.4 %collective-permute-start.15 = (f32[256,256]{1,0:T(8,128)S(1)}, f32[256,256]{1,0:T(8,128)S(1)}, u32[]{:S(2)}, u32[]{:S(2)}) collective-permute-start(f32[256,256]{1,0:T(8,128)S(1)} %shard_map.82.a), channel_id=1, source_target_pairs={{0,2},{1,5},{2,0},{3,7},{4,6},{5,1},{6,4},{7,3},{8,10},{9,13},{10,... | collective-permute-start | bytes 786440 | tf_op jit(solution)/shard_map/ppermute | solution.py:331
  63.7 5.6 %collective-permute-start.16 = (f32[2,2,128,128]{3,2,1,0:T(8,128)S(1)}, f32[2,2,128,128]{3,2,1,0:T(8,128)S(1)}, u32[]{:S(2)}, u32[]{:S(2)}) collective-permute-start(f32[2,2,128,128]{3,2,1,0:T(8,128)S(1)} %get-tuple-element.84), channel_id=1, source_target_pairs={{0,4},{2,6},{4,8},{5,1},{6,10},{7,3},{8,12},{9,5},{10,14},{11,7},{... | collective-permute-start | bytes 786440 | tf_op jit(solution)/shard_map/ppermute | solution.py:331
  65.5 6.4 %collective-permute-start.19 = (f32[256,256]{1,0:T(8,128)S(1)}, f32[256,256]{1,0:T(8,128)S(1)}, u32[]{:S(2)}, u32[]{:S(2)}) collective-permute-start(f32[256,256]{1,0:T(8,128)S(1)} %shard_map.85.a), channel_id=1, source_target_pairs={{0,2},{1,5},{2,0},{3,7},{4,6},{5,1},{6,4},{7,3},{8,10},{9,13},{10,... | collective-permute-start | bytes 786440 | tf_op jit(solution)/shard_map/ppermute | solution.py:331
  69.3 5.1 %collective-permute-start.17 = (f32[512,256]{1,0:T(8,128)S(1)}, f32[512,256]{1,0:T(8,128)S(1)}, u32[]{:S(2)}, u32[]{:S(2)}) collective-permute-start(f32[512,256]{1,0:T(8,128)S(1)} %shard_map.83.refs_0_), channel_id=1, source_target_pairs={{0,1},{1,0},{2,3},{3,2},{4,5},{5,4},{6,7},{7,6},{8,9},{9,8},{10,11... | collective-permute-start | bytes 1572872 | tf_op jit(solution)/shard_map/ppermute | solution.py:331
  72.0 2.4 %collective-permute-start.20 = (f32[512,256]{1,0:T(8,128)S(1)}, f32[512,256]{1,0:T(8,128)S(1)}, u32[]{:S(2)}, u32[]{:S(2)}) collective-permute-start(f32[512,256]{1,0:T(8,128)S(1)} %shard_map.86.refs_1_), channel_id=1, source_target_pairs={{0,1},{1,0},{2,3},{3,2},{4,5},{5,4},{6,7},{7,6},{8,9},{9,8},{10,11... | collective-permute-start | bytes 1572872 | tf_op jit(solution)/shard_map/ppermute | solution.py:331
  (1 other events, 1.0 us)

commit v3 on v2

--- a/solution.py
+++ b/solution.py
@@ -373,17 +373,16 @@
     return total
 
 
-def small_call(body, outs, args, meta=None):
+def small_call(body, outs, args):
     vmem = pl.BlockSpec(memory_space=pltpu.VMEM)
-    extra = [] if meta is None else [meta]
     return pl.pallas_call(
         body,
         out_shape=tuple(jax.ShapeDtypeStruct(shape, jnp.float32) for shape in outs),
-        in_specs=[pl.BlockSpec(memory_space=pltpu.SMEM)] * len(extra) + [vmem] * len(args),
+        in_specs=[vmem] * len(args),
         out_specs=(vmem,) * len(outs),
         compiler_params=pltpu.CompilerParams(vmem_limit_bytes=6 * 2**20),
         cost_estimate=pl.CostEstimate(flops=10**6, bytes_accessed=2**20, transcendentals=0),
-    )(*extra, *args)
+    )(*args)
 
 
 def add_split(own, got):
@@ -414,13 +413,13 @@
     return small_call(body, [(2 * rows, lanes)], [own, got])[0]
 
 
-def strips(field, meta, steps):
+def strips(field, steps):
     _, tile, width = field.shape
     half = width // 2
 
-    def body(meta_ref, tile_ref, outer_ref, *refs):
+    def body(tile_ref, outer_ref, *refs):
         sems = refs[-1]
-        core, odd = meta_ref[0], meta_ref[1]
+        core, odd = lax.axis_index("sg"), lax.axis_index("yt") % 2
         outer = pl.ds(pl.multiple_of((1 - core) * half, half), half)
         inner = pl.ds(pl.multiple_of(core * half, half), half)
         copies = [pltpu.make_async_copy(tile_ref.at[:, outer], outer_ref, sems.at[0])]
@@ -440,42 +439,44 @@
     return pl.pallas_call(
         body,
         out_shape=tuple(jax.ShapeDtypeStruct(shape, jnp.float32) for shape in shapes),
-        in_specs=[pl.BlockSpec(memory_space=pltpu.SMEM), pl.BlockSpec(memory_space=pl.ANY)],
+        in_specs=[pl.BlockSpec(memory_space=pl.ANY)],
         out_specs=(vmem,) * len(shapes),
         scratch_shapes=[pltpu.SemaphoreType.DMA((1 + 2 * steps,))],
         compiler_params=pltpu.CompilerParams(vmem_limit_bytes=6 * 2**20),
         cost_estimate=pl.CostEstimate(flops=10**6, bytes_accessed=2**20, transcendentals=0),
-    )(meta, field)
-
-
-def fold_sends(keep, got, meta, steps):
+    )(field)
+
+
+def fold_sends(keep, got, steps):
     half = keep.shape[-1]
 
-    def body(meta_ref, a, b, *refs):
+    def body(a, b, *refs):
         mid_ref, refs = refs[-1], refs[:-1]
+        odd = lax.axis_index("yt") % 2
         for step in range(steps):
-            block = meta_ref[2] if step == 0 else 3 - meta_ref[2]
+            block = 3 * (1 - odd) if step == 0 else 3 * odd
             refs[step][...] = a[:, :, block] + b[:, :, block]
         mid_ref[...] = a[:, :, 1:3] + b[:, :, 1:3]
 
     shapes = [(2, 2, half, half)] * steps + [(2, 2, 2, half, half)]
-    *edges, mid = small_call(body, shapes, [keep, got], meta)
+    *edges, mid = small_call(body, shapes, [keep, got])
     return edges, mid
 
 
-def fold_join(mid, arrived, meta):
+def fold_join(mid, arrived):
     half = mid.shape[-1]
 
-    def body(meta_ref, mid_ref, *refs):
+    def body(mid_ref, *refs):
+        odd = lax.axis_index("yt") % 2
         down_ref, main_ref = refs[-2:]
         for j in range(2):
             total = mid_ref[:, :, j]
             for step, ref in enumerate(refs[:-2]):
-                total += jnp.where((meta_ref[6] + step + j) % 2 == 1, 1.0, 0.0) * ref[...]
+                total += jnp.where((odd + step + j) % 2 == 1, 1.0, 0.0) * ref[...]
             main_ref[:, j] = total[0]
             down_ref[:, j] = total[1]
 
-    return small_call(body, [(2, 2, half, half)] * 2, [mid, *arrived], meta)
+    return small_call(body, [(2, 2, half, half)] * 2, [mid, *arrived])
 
 
 def fold_finish(main, below):
@@ -488,18 +489,19 @@
     return small_call(body, [(2, half, 2 * half)], [main, below])[0]
 
 
-def place_probe(chunks, meta, blocks, shape, sibling, into=None):
+def place_probe(chunks, early, blocks, shape, sibling, into=None):
     modes, _, width, _ = shape
     share = modes // 2
     part = share // 2
     size = part * 2 * width // blocks
     given = [] if into is None else [into]
 
-    def body(meta_ref, *refs):
+    def body(*refs):
         sem = refs[-1]
         out_ref = refs[-2]
-        at = 1 - meta_ref[1] if sibling else meta_ref[1]
-        bits = meta_ref[4] if sibling else meta_ref[3]
+        core = lax.axis_index("sg")
+        at = 1 - core if sibling else core
+        bits = bits_of(early, at)
 
         def copies(p):
             found = []
@@ -528,13 +530,13 @@
     return pl.pallas_call(
         body,
         out_shape=jax.ShapeDtypeStruct(shape, jnp.float32),
-        in_specs=[pl.BlockSpec(memory_space=pltpu.SMEM)] + [anywhere] * (2 + len(given)),
+        in_specs=[anywhere] * (2 + len(given)),
         out_specs=anywhere,
-        input_output_aliases={3: 0} if given else {},
+        input_output_aliases={2: 0} if given else {},
         scratch_shapes=[pltpu.SemaphoreType.DMA((blocks, 2))],
         compiler_params=pltpu.CompilerParams(vmem_limit_bytes=6 * 2**20),
         cost_estimate=pl.CostEstimate(flops=10**6, bytes_accessed=2**21, transcendentals=0),
-    )(meta, *chunks, *given)
+    )(*chunks, *given)
 
 
 def shards(field, probe, amplitudes, offsets, counts):
@@ -553,9 +555,8 @@
         [live, core, side, bits_of(early, core), bits_of(early, 1 - core), base, odd]
     ).astype(jnp.int32)
     offs = offsets[0, 0].T
-    place = jnp.stack([core, odd]).astype(jnp.int32)
-
-    outer, *edges = strips(field, place, steps)
+
+    outer, *edges = strips(field, steps)
     prepared = prepare(probe, amplitudes[0, 0])
     parts = [move(outer, lambda z, x, c: (down(z, c), x, c))]
     for step in range(steps):
@@ -572,7 +573,7 @@
     keep2, send2, keep_grad, send_grad = second
     pairs = [add_split(keep, received), add_split(keep2, swap_cores(send2))]
     got = [move(high, flip(early[0])) for _, high in pairs]
-    edges, mid = fold_sends(keep_grad, swap_cores(send_grad), meta, steps)
+    edges, mid = fold_sends(keep_grad, swap_cores(send_grad), steps)
     arrived = [
         move(edge, lambda z, x, c, step=step: (z, across(x, step), c)) for step, edge in enumerate(edges)
     ]
@@ -582,15 +583,15 @@
     parts = [add(low, g) for (low, _), g in zip(pairs, got)]
     parts = [add(p, move(p, flip(last))) for p in parts]
     parts[1], arrived = lax.optimization_barrier((parts[1], arrived))
-    down_part, main = fold_join(mid, arrived, meta)
+    down_part, main = fold_join(mid, arrived)
     below = move(down_part, lambda z, x, c: (down(z, c), x, c))
     for order in early[::-1]:
         parts = [stack(p, move(p, flip(order))) for p in parts]
     parts[0], below = lax.optimization_barrier((parts[0], below))
     new_field = fold_finish(main, below)
     theirs = [swap_cores(p) for p in parts]
-    new_probe = place_probe(parts, meta, blocks, probe.shape, False)
-    new_probe = place_probe(theirs, meta, blocks, probe.shape, True, new_probe)
+    new_probe = place_probe(parts, early, blocks, probe.shape, False)
+    new_probe = place_probe(theirs, early, blocks, probe.shape, True, new_probe)
     return (new_field, new_probe)
 
 

time: 76.2 us -> 74 us (0.971)
  starting transfers between devices: 27.9 us -> 35.3 us
  Pallas kernels: 19.7 us -> 13.7 us
  waiting for transfers between devices: 24.5 us -> 20.9 us
    ppermute x21, starting transfers between devices: 27.9 us -> 35.3 us  [move(): return lax.ppermute(block, grid_axes, route(target))]
    ppermute x21, waiting for transfers between devices: 24.5 us -> 20.9 us  [move(): return lax.ppermute(block, grid_axes, route(target))]
    pallas_call x1, Pallas kernels: 7.75 us -> 5.49 us  [first_scans(): pl.pallas_call(functools.partial(first_kernel, blocks), out_shape=(share,...]
    pallas_call x2, Pallas kernels: 3.17 us -> 2.05 us  [place_probe(): pl.pallas_call(body, out_shape=jax.ShapeDtypeStruct(shape, jnp.float32),...]
    pallas_call x15, Pallas kernels: 2.29 us -> 1.22 us  [small_call(): pl.pallas_call(body, out_shape=tuple((jax.ShapeDtypeStruct(shape, jnp.flo...]
    pallas_call x1, Pallas kernels: 4.13 us -> 3.15 us  [second_scans(): pl.pallas_call(functools.partial(second_kernel, blocks), out_shape=(share...]
  transfers between devices with their start and end apart: 21 -> 21, of which waited for: 11 -> 11; matrix products, arithmetic and copies ran while one was open for 0% -> 0% of each run, Pallas kernels for 13% -> 10%
where the time goes in v3:
time: 74 us; the launch traced here: 73.7 us
  starting transfers between devices  35.3 us (48%)
  waiting for transfers between devices  20.9 us (28%)
  Pallas kernels  13.7 us (19%)
  local copies, waits for them, and re-layouts  2.17 us (3%)
  between operations  1.59 us (2%)
    ppermute x21, starting transfers between devices, move(): return lax.ppermute(block, grid_axes, route(target))  35.3 us
    ppermute x21, waiting for transfers between devices, move(): return lax.ppermute(block, grid_axes, route(target))  20.9 us
    pallas_call x1, Pallas kernels, first_scans(): pl.pallas_call(functools.partial(first_kernel, blocks), out_shape=(share,...  5.49 us
    pallas_call x1, Pallas kernels, second_scans(): pl.pallas_call(functools.partial(second_kernel, blocks), out_shape=(share...  3.15 us
    unnamed x10, local copies, waits for them, and re-layouts  2.07 us
    pallas_call x2, Pallas kernels, place_probe(): pl.pallas_call(body, out_shape=jax.ShapeDtypeStruct(shape, jnp.float32),...  2.05 us
    pallas_call x1, Pallas kernels, prepare(): pl.pallas_call(body, out_shape=(jax.ShapeDtypeStruct(probe.shape, jnp.bfl...  1.68 us
  transfers between devices with their start and end apart: 21, of which 11 were waited for; matrix products, arithmetic and copies ran while one was open for 0% of the time, Pallas kernels for 10%

profile of v3, /device:TPU:0, one launch (start us, length us, event | category | flops | bytes accessed | tf_op | source)
XLA Modules:
  0.0 73.7 jit_solution(2537409159098268788)
XLA Ops:
  0.6 1.0 %copy-done = f32[2,256,256]{2,1,0:T(8,128)S(1)} copy-done((f32[2,256,256]{2,1,0:T(8,128)S(1)}, f32[2,256,256]{2,1,0:T(8,128)}, u32[]{:S(2)}) %copy-start) | copy-done | bytes 524312
  1.8 5.1 %collective-permute-start = (f32[2,128,256]{2,1,0:T(8,128)S(1)}, f32[2,128,256]{2,1,0:T(8,128)S(1)}, u32[]{:S(2)}, u32[]{:S(2)}) collective-permute-start(f32[2,128,256]{2,1,0:T(8,128)S(1)} %get-tuple-element.45), channel_id=1, source_target_pairs={{0,4},{2,6},{4,8},{5,1},{6,10},{7,3},{8,12},{9,5},{10,14},{11,7},{... | collective-permute-start | bytes 786440 | tf_op jit(solution)/shard_map/ppermute | solution.py:331
  6.8 1.6 %collective-permute-start.1 = (f32[2,128,128]{2,1,0:T(8,128)S(1)}, f32[2,128,128]{2,1,0:T(8,128)S(1)}, u32[]{:S(2)}, u32[]{:S(2)}) collective-permute-start(f32[2,128,128]{2,1,0:T(8,128)S(1)} %get-tuple-element.46), channel_id=1, source_target_pairs={{0,2},{1,3},{2,0},{3,1},{4,6},{5,7},{6,4},{7,5},{8,10},{9,11},{10,... | collective-permute-start | bytes 393224 | tf_op jit(solution)/shard_map/ppermute | solution.py:331
  8.4 3.4 %collective-permute-start.2 = (f32[2,128,128]{2,1,0:T(8,128)S(1)}, f32[2,128,128]{2,1,0:T(8,128)S(1)}, u32[]{:S(2)}, u32[]{:S(2)}) collective-permute-start(f32[2,128,128]{2,1,0:T(8,128)S(1)} %get-tuple-element.47), channel_id=1, source_target_pairs={{0,6},{2,4},{4,10},{5,3},{6,8},{7,1},{8,14},{9,7},{10,12},{11,5},{... | collective-permute-start | bytes 393224 | tf_op jit(solution)/shard_map/ppermute | solution.py:331
  13.6 1.7 %shard_map.69 = (bf16[4,2,256,256]{3,2,1,0:T(8,128)(2,1)S(1)}, f32[3,256,256]{2,1,0:T(8,128)S(1)}, bf16[2,256,256]{2,1,0:T(8,128)(2,1)S(1)}) custom-call(bf16[4,2,256,256]{3,2,1,0:T(8,128)(2,1)} %probe_hbm.1, bf16[3,256,256]{2,1,0:T(8,128)(2,1)S(1)} %bitcast.13), custom_call_target="tpu_custom_call" | custom-call | flops 200000000 | bytes 4194304 | tf_op jit(solution)/shard_map/pallas_call | solution.py:254
  15.5 1.9 %collective-permute-done.3.other_ref = f32[2,128,512]{2,1,0:T(8,128)S(1)} collective-permute-done((f32[2,128,512]{2,1,0:T(8,128)S(1)}, f32[2,128,512]{2,1,0:T(8,128)S(1)}, u32[]{:S(2)}, u32[]{:S(2)}) %collective-permute-start.3) | collective-permute-done | bytes 524320 | tf_op jit(solution)/shard_map/ppermute | solution.py:331
  17.4 5.5 %shard_map.70 = (f32[512,256]{1,0:T(8,128)S(1)}, f32[512,256]{1,0:T(8,128)S(1)}, f32[3,2,256,256]{3,2,1,0:T(8,128)S(1)}, bf16[3,2,2,256,256]{4,3,2,1,0:T(8,128)(2,1)S(1)}, f32[3,2,256,256]{3,2,1,0:T(8,128)S(1)}) custom-call(s32[7]{0:T(128)S(1)} %stack.31.meta_ref, s32[2,3]{1,0:T(2,128)S(1)} %bitcast.14, f32[2,256,256]{2,1,0:T(8,128)S(1)} %copy-done.1, ...), custom_call_target="tpu_custom_call" | custom-call | flops 4000000000 | bytes 8388608 | tf_op jit(solution)/shard_map/pallas_call | solution.py:281
  23.0 3.1 %shard_map.71 = (f32[512,256]{1,0:T(8,128)S(1)}, f32[512,256]{1,0:T(8,128)S(1)}, f32[2,2,4,128,128]{4,3,2,1,0:T(8,128)S(1)}, f32[2,2,4,128,128]{4,3,2,1,0:T(8,128)S(1)}) custom-call(s32[7]{0:T(128)S(1)} %stack.31.meta_ref, s32[2,3]{1,0:T(2,128)S(1)} %bitcast.15, f32[2,256,256]{2,1,0:T(8,128)S(1)} %copy-done.1, ...), custom_call_target="tpu_custom_call" | custom-call | flops 2000000000 | bytes 8388608 | tf_op jit(solution)/shard_map/pallas_call | solution.py:304
  26.8 4.9 %collective-permute-start.11 = (f32[256,256]{1,0:T(8,128)S(1)}, f32[256,256]{1,0:T(8,128)S(1)}, u32[]{:S(2)}, u32[]{:S(2)}) collective-permute-start(f32[256,256]{1,0:T(8,128)S(1)} %get-tuple-element.81), channel_id=1, source_target_pairs={{0,2},{1,5},{2,0},{3,7},{4,6},{5,1},{6,4},{7,3},{8,10},{9,13},{10,... | collective-permute-start | bytes 786440 | tf_op jit(solution)/shard_map/ppermute | solution.py:331
  31.7 2.8 %collective-permute-start.7 = (f32[256,256]{1,0:T(8,128)S(1)}, f32[256,256]{1,0:T(8,128)S(1)}, u32[]{:S(2)}, u32[]{:S(2)}) collective-permute-start(f32[256,256]{1,0:T(8,128)S(1)} %get-tuple-element.72), channel_id=1, source_target_pairs={{0,2},{1,5},{2,0},{3,7},{4,6},{5,1},{6,4},{7,3},{8,10},{9,13},{10,... | collective-permute-start | bytes 786440 | tf_op jit(solution)/shard_map/ppermute | solution.py:331
  34.6 1.4 %collective-permute-done.11.b = f32[256,256]{1,0:T(8,128)S(1)} collective-permute-done((f32[256,256]{1,0:T(8,128)S(1)}, f32[256,256]{1,0:T(8,128)S(1)}, u32[]{:S(2)}, u32[]{:S(2)}) %collective-permute-start.11) | collective-permute-done | bytes 262176 | tf_op jit(solution)/shard_map/ppermute | solution.py:331
  36.1 2.9 %collective-permute-start.12 = (f32[128,256]{1,0:T(8,128)S(1)}, f32[128,256]{1,0:T(8,128)S(1)}, u32[]{:S(2)}, u32[]{:S(2)}) collective-permute-start(f32[128,256]{1,0:T(8,128)S(1)} %get-tuple-element.83), channel_id=1, source_target_pairs={{0,4},{1,3},{2,6},{3,1},{4,0},{5,7},{6,2},{7,5},{8,12},{9,11},{10,... | collective-permute-start | bytes 393224 | tf_op jit(solution)/shard_map/ppermute | solution.py:331
  39.1 3.6 %collective-permute-start.8 = (f32[128,256]{1,0:T(8,128)S(1)}, f32[128,256]{1,0:T(8,128)S(1)}, u32[]{:S(2)}, u32[]{:S(2)}) collective-permute-start(f32[128,256]{1,0:T(8,128)S(1)} %get-tuple-element.74), channel_id=1, source_target_pairs={{0,4},{1,3},{2,6},{3,1},{4,0},{5,7},{6,2},{7,5},{8,12},{9,11},{10,... | collective-permute-start | bytes 393224 | tf_op jit(solution)/shard_map/ppermute | solution.py:331
  43.0 2.0 %collective-permute-start.13 = (f32[128,256]{1,0:T(8,128)S(1)}, f32[128,256]{1,0:T(8,128)S(1)}, u32[]{:S(2)}, u32[]{:S(2)}) collective-permute-start(f32[128,256]{1,0:T(8,128)S(1)} %shard_map.80.a), channel_id=1, source_target_pairs={{0,8},{1,9},{2,10},{3,11},{4,12},{5,13},{6,14},{7,15},{8,0},{9,1},... | collective-permute-start | bytes 393224 | tf_op jit(solution)/shard_map/ppermute | solution.py:331
  45.0 1.8 %collective-permute-done.8.b = f32[128,256]{1,0:T(8,128)S(1)} collective-permute-done((f32[128,256]{1,0:T(8,128)S(1)}, f32[128,256]{1,0:T(8,128)S(1)}, u32[]{:S(2)}, u32[]{:S(2)}) %collective-permute-start.8) | collective-permute-done | bytes 131104 | tf_op jit(solution)/shard_map/ppermute | solution.py:331
  46.8 3.3 %collective-permute-start.9 = (f32[128,256]{1,0:T(8,128)S(1)}, f32[128,256]{1,0:T(8,128)S(1)}, u32[]{:S(2)}, u32[]{:S(2)}) collective-permute-start(f32[128,256]{1,0:T(8,128)S(1)} %shard_map.75.a), channel_id=1, source_target_pairs={{0,8},{1,9},{2,10},{3,11},{4,12},{5,13},{6,14},{7,15},{8,0},{9,1},... | collective-permute-start | bytes 393224 | tf_op jit(solution)/shard_map/ppermute | solution.py:331
  50.1 4.9 %collective-permute-done.13.b = f32[128,256]{1,0:T(8,128)S(1)} collective-permute-done((f32[128,256]{1,0:T(8,128)S(1)}, f32[128,256]{1,0:T(8,128)S(1)}, u32[]{:S(2)}, u32[]{:S(2)}) %collective-permute-start.13) | collective-permute-done | bytes 131104 | tf_op jit(solution)/shard_map/ppermute | solution.py:331
  55.1 1.4 %collective-permute-done.9.b = f32[128,256]{1,0:T(8,128)S(1)} collective-permute-done((f32[128,256]{1,0:T(8,128)S(1)}, f32[128,256]{1,0:T(8,128)S(1)}, u32[]{:S(2)}, u32[]{:S(2)}) %collective-permute-start.9) | collective-permute-done | bytes 131104 | tf_op jit(solution)/shard_map/ppermute | solution.py:331
  57.2 4.2 %collective-permute-done.14.b = f32[128,256]{1,0:T(8,128)S(1)} collective-permute-done((f32[128,256]{1,0:T(8,128)S(1)}, f32[128,256]{1,0:T(8,128)S(1)}, u32[]{:S(2)}, u32[]{:S(2)}) %collective-permute-start.14) | collective-permute-done | bytes 131104 | tf_op jit(solution)/shard_map/ppermute | solution.py:331
  62.2 1.7 %collective-permute-start.16 = (f32[2,2,128,128]{3,2,1,0:T(8,128)S(1)}, f32[2,2,128,128]{3,2,1,0:T(8,128)S(1)}, u32[]{:S(2)}, u32[]{:S(2)}) collective-permute-start(f32[2,2,128,128]{3,2,1,0:T(8,128)S(1)} %get-tuple-element.84), channel_id=1, source_target_pairs={{0,4},{2,6},{4,8},{5,1},{6,10},{7,3},{8,12},{9,5},{10,14},{11,7},{... | collective-permute-start | bytes 786440 | tf_op jit(solution)/shard_map/ppermute | solution.py:331
  64.2 1.5 %collective-permute-start.19 = (f32[256,256]{1,0:T(8,128)S(1)}, f32[256,256]{1,0:T(8,128)S(1)}, u32[]{:S(2)}, u32[]{:S(2)}) collective-permute-start(f32[256,256]{1,0:T(8,128)S(1)} %shard_map.85.a), channel_id=1, source_target_pairs={{0,2},{1,5},{2,0},{3,7},{4,6},{5,1},{6,4},{7,3},{8,10},{9,13},{10,... | collective-permute-start | bytes 786440 | tf_op jit(solution)/shard_map/ppermute | solution.py:331
  65.7 2.2 %collective-permute-done.15.b = f32[256,256]{1,0:T(8,128)S(1)} collective-permute-done((f32[256,256]{1,0:T(8,128)S(1)}, f32[256,256]{1,0:T(8,128)S(1)}, u32[]{:S(2)}, u32[]{:S(2)}) %collective-permute-start.15) | collective-permute-done | bytes 262176 | tf_op jit(solution)/shard_map/ppermute | solution.py:331
  68.0 2.7 %collective-permute-done.19.b = f32[256,256]{1,0:T(8,128)S(1)} collective-permute-done((f32[256,256]{1,0:T(8,128)S(1)}, f32[256,256]{1,0:T(8,128)S(1)}, u32[]{:S(2)}, u32[]{:S(2)}) %collective-permute-start.19) | collective-permute-done | bytes 262176 | tf_op jit(solution)/shard_map/ppermute | solution.py:331
  72.7 1.0 %shard_map.88 = f32[4,2,256,256]{3,2,1,0:T(8,128)} custom-call(f32[512,256]{1,0:T(8,128)S(1)} %collective-permute-done.17.refs_0_, f32[512,256]{1,0:T(8,128)S(1)} %collective-permute-done.20.refs_1_, f32[4,2,256,256]{3,2,1,0:T(8,128)} %shard_map.87.refs_2_), custom_call_target="tpu_custom_call", output_to_operand_aliasing={{}: (2, {})} | custom-call | flops 1000000 | bytes 2097152 | tf_op jit(solution)/shard_map/pallas_call | solution.py:530
  (51 shorter events, 6.5 us)
Async XLA Ops:
  0.6 1.0 %copy-start = (f32[2,256,256]{2,1,0:T(8,128)S(1)}, f32[2,256,256]{2,1,0:T(8,128)}, u32[]{:S(2)}) copy-start(f32[2,256,256]{2,1,0:T(8,128)} %tile_ref.5) | copy-start | bytes 1572868
  1.7 15.7 %copy-start.1 = (f32[2,256,256]{2,1,0:T(8,128)S(1)}, f32[2,256,256]{2,1,0:T(8,128)}, u32[]{:S(2)}) copy-start(f32[2,256,256]{2,1,0:T(8,128)} %tile_ref.5) | copy-start | bytes 1572868
  1.7 15.7 %copy-start.3 = (s32[1,1,3,2]{2,3,1,0:T(2,128)S(1)}, s32[1,1,3,2]{2,3,1,0:T(2,128)}, u32[]{:S(2)}) copy-start(s32[1,1,3,2]{2,3,1,0:T(2,128)} %param.8) | copy-start | bytes 76
  1.8 13.6 %collective-permute-start = (f32[2,128,256]{2,1,0:T(8,128)S(1)}, f32[2,128,256]{2,1,0:T(8,128)S(1)}, u32[]{:S(2)}, u32[]{:S(2)}) collective-permute-start(f32[2,128,256]{2,1,0:T(8,128)S(1)} %get-tuple-element.45), channel_id=1, source_target_pairs={{0,4},{2,6},{4,8},{5,1},{6,10},{7,3},{8,12},{9,5},{10,14},{11,7},{... | collective-permute-start | bytes 786440 | tf_op jit(solution)/shard_map/ppermute | solution.py:331
  6.8 8.5 %collective-permute-start.1 = (f32[2,128,128]{2,1,0:T(8,128)S(1)}, f32[2,128,128]{2,1,0:T(8,128)S(1)}, u32[]{:S(2)}, u32[]{:S(2)}) collective-permute-start(f32[2,128,128]{2,1,0:T(8,128)S(1)} %get-tuple-element.46), channel_id=1, source_target_pairs={{0,2},{1,3},{2,0},{3,1},{4,6},{5,7},{6,4},{7,5},{8,10},{9,11},{10,... | collective-permute-start | bytes 393224 | tf_op jit(solution)/shard_map/ppermute | solution.py:331
  8.4 6.9 %collective-permute-start.2 = (f32[2,128,128]{2,1,0:T(8,128)S(1)}, f32[2,128,128]{2,1,0:T(8,128)S(1)}, u32[]{:S(2)}, u32[]{:S(2)}) collective-permute-start(f32[2,128,128]{2,1,0:T(8,128)S(1)} %get-tuple-element.47), channel_id=1, source_target_pairs={{0,6},{2,4},{4,10},{5,3},{6,8},{7,1},{8,14},{9,7},{10,12},{11,5},{... | collective-permute-start | bytes 393224 | tf_op jit(solution)/shard_map/ppermute | solution.py:331
  15.4 2.0 %collective-permute-start.3 = (f32[2,128,512]{2,1,0:T(8,128)S(1)}, f32[2,128,512]{2,1,0:T(8,128)S(1)}, u32[]{:S(2)}, u32[]{:S(2)}) collective-permute-start(f32[2,128,512]{2,1,0:T(8,128)S(1)} %constant_dynamic-update-slice_fusion.mine_ref), channel_id=1, source_target_pairs={{0,1},{1,0},{2,3},{3,2},{4,5},{5,4},{6,7},{7,6},{8,9},{9,8},{10,11... | collective-permute-start | bytes 1572872 | tf_op jit(solution)/shard_map/ppermute | solution.py:331
  22.9 3.2 %collective-permute-start.4 = (f32[512,256]{1,0:T(8,128)S(1)}, f32[512,256]{1,0:T(8,128)S(1)}, u32[]{:S(2)}, u32[]{:S(2)}) collective-permute-start(f32[512,256]{1,0:T(8,128)S(1)} %get-tuple-element.58), channel_id=1, source_target_pairs={{0,1},{1,0},{2,3},{3,2},{4,5},{5,4},{6,7},{7,6},{8,9},{9,8},{10,11... | collective-permute-start | bytes 1572872 | tf_op jit(solution)/shard_map/ppermute | solution.py:331
  26.1 16.6 %collective-permute-start.5 = (f32[2,2,4,128,128]{4,3,2,1,0:T(8,128)S(1)}, f32[2,2,4,128,128]{4,3,2,1,0:T(8,128)S(1)}, u32[]{:S(2)}, u32[]{:S(2)}) collective-permute-start(f32[2,2,4,128,128]{4,3,2,1,0:T(8,128)S(1)} %get-tuple-element.67), channel_id=1, source_target_pairs={{0,1},{1,0},{2,3},{3,2},{4,5},{5,4},{6,7},{7,6},{8,9},{9,8},{10,11... | collective-permute-start | bytes 3145736 | tf_op jit(solution)/shard_map/ppermute | solution.py:331
  26.2 5.5 %collective-permute-start.6 = (f32[512,256]{1,0:T(8,128)S(1)}, f32[512,256]{1,0:T(8,128)S(1)}, u32[]{:S(2)}, u32[]{:S(2)}) collective-permute-start(f32[512,256]{1,0:T(8,128)S(1)} %get-tuple-element.70), channel_id=1, source_target_pairs={{0,1},{1,0},{2,3},{3,2},{4,5},{5,4},{6,7},{7,6},{8,9},{9,8},{10,11... | collective-permute-start | bytes 1572872 | tf_op jit(solution)/shard_map/ppermute | solution.py:331
  26.8 9.3 %collective-permute-start.11 = (f32[256,256]{1,0:T(8,128)S(1)}, f32[256,256]{1,0:T(8,128)S(1)}, u32[]{:S(2)}, u32[]{:S(2)}) collective-permute-start(f32[256,256]{1,0:T(8,128)S(1)} %get-tuple-element.81), channel_id=1, source_target_pairs={{0,2},{1,5},{2,0},{3,7},{4,6},{5,1},{6,4},{7,3},{8,10},{9,13},{10,... | collective-permute-start | bytes 786440 | tf_op jit(solution)/shard_map/ppermute | solution.py:331
  31.7 7.4 %collective-permute-start.7 = (f32[256,256]{1,0:T(8,128)S(1)}, f32[256,256]{1,0:T(8,128)S(1)}, u32[]{:S(2)}, u32[]{:S(2)}) collective-permute-start(f32[256,256]{1,0:T(8,128)S(1)} %get-tuple-element.72), channel_id=1, source_target_pairs={{0,2},{1,5},{2,0},{3,7},{4,6},{5,1},{6,4},{7,3},{8,10},{9,13},{10,... | collective-permute-start | bytes 786440 | tf_op jit(solution)/shard_map/ppermute | solution.py:331
  36.1 6.9 %collective-permute-start.12 = (f32[128,256]{1,0:T(8,128)S(1)}, f32[128,256]{1,0:T(8,128)S(1)}, u32[]{:S(2)}, u32[]{:S(2)}) collective-permute-start(f32[128,256]{1,0:T(8,128)S(1)} %get-tuple-element.83), channel_id=1, source_target_pairs={{0,4},{1,3},{2,6},{3,1},{4,0},{5,7},{6,2},{7,5},{8,12},{9,11},{10,... | collective-permute-start | bytes 393224 | tf_op jit(solution)/shard_map/ppermute | solution.py:331
  39.1 7.7 %collective-permute-start.8 = (f32[128,256]{1,0:T(8,128)S(1)}, f32[128,256]{1,0:T(8,128)S(1)}, u32[]{:S(2)}, u32[]{:S(2)}) collective-permute-start(f32[128,256]{1,0:T(8,128)S(1)} %get-tuple-element.74), channel_id=1, source_target_pairs={{0,4},{1,3},{2,6},{3,1},{4,0},{5,7},{6,2},{7,5},{8,12},{9,11},{10,... | collective-permute-start | bytes 393224 | tf_op jit(solution)/shard_map/ppermute | solution.py:331
  42.8 13.7 %collective-permute-start.10 = (f32[2,2,128,128]{3,2,1,0:T(8,128)S(1)}, f32[2,2,128,128]{3,2,1,0:T(8,128)S(1)}, u32[]{:S(2)}, u32[]{:S(2)}) collective-permute-start(f32[2,2,128,128]{3,2,1,0:T(8,128)S(1)} %get-tuple-element.75), channel_id=1, source_target_pairs={{0,2},{1,3},{2,0},{3,1},{4,6},{5,7},{6,4},{7,5},{8,10},{9,11},{10,... | collective-permute-start | bytes 786440 | tf_op jit(solution)/shard_map/ppermute | solution.py:331
  43.0 12.0 %collective-permute-start.13 = (f32[128,256]{1,0:T(8,128)S(1)}, f32[128,256]{1,0:T(8,128)S(1)}, u32[]{:S(2)}, u32[]{:S(2)}) collective-permute-start(f32[128,256]{1,0:T(8,128)S(1)} %shard_map.80.a), channel_id=1, source_target_pairs={{0,8},{1,9},{2,10},{3,11},{4,12},{5,13},{6,14},{7,15},{8,0},{9,1},... | collective-permute-start | bytes 393224 | tf_op jit(solution)/shard_map/ppermute | solution.py:331
  46.8 9.7 %collective-permute-start.9 = (f32[128,256]{1,0:T(8,128)S(1)}, f32[128,256]{1,0:T(8,128)S(1)}, u32[]{:S(2)}, u32[]{:S(2)}) collective-permute-start(f32[128,256]{1,0:T(8,128)S(1)} %shard_map.75.a), channel_id=1, source_target_pairs={{0,8},{1,9},{2,10},{3,11},{4,12},{5,13},{6,14},{7,15},{8,0},{9,1},... | collective-permute-start | bytes 393224 | tf_op jit(solution)/shard_map/ppermute | solution.py:331
  55.0 6.3 %collective-permute-start.14 = (f32[128,256]{1,0:T(8,128)S(1)}, f32[128,256]{1,0:T(8,128)S(1)}, u32[]{:S(2)}, u32[]{:S(2)}) collective-permute-start(f32[128,256]{1,0:T(8,128)S(1)} %shard_map.81.a), channel_id=1, source_target_pairs={{0,4},{1,3},{2,6},{3,1},{4,0},{5,7},{6,2},{7,5},{8,12},{9,11},{10,... | collective-permute-start | bytes 393224 | tf_op jit(solution)/shard_map/ppermute | solution.py:331
  56.5 7.7 %collective-permute-start.18 = (f32[128,256]{1,0:T(8,128)S(1)}, f32[128,256]{1,0:T(8,128)S(1)}, u32[]{:S(2)}, u32[]{:S(2)}) collective-permute-start(f32[128,256]{1,0:T(8,128)S(1)} %shard_map.76.a), channel_id=1, source_target_pairs={{0,4},{1,3},{2,6},{3,1},{4,0},{5,7},{6,2},{7,5},{8,12},{9,11},{10,... | collective-permute-start | bytes 393224 | tf_op jit(solution)/shard_map/ppermute | solution.py:331
  61.4 6.4 %collective-permute-start.15 = (f32[256,256]{1,0:T(8,128)S(1)}, f32[256,256]{1,0:T(8,128)S(1)}, u32[]{:S(2)}, u32[]{:S(2)}) collective-permute-start(f32[256,256]{1,0:T(8,128)S(1)} %shard_map.82.a), channel_id=1, source_target_pairs={{0,2},{1,5},{2,0},{3,7},{4,6},{5,1},{6,4},{7,3},{8,10},{9,13},{10,... | collective-permute-start | bytes 786440 | tf_op jit(solution)/shard_map/ppermute | solution.py:331
  62.2 5.7 %collective-permute-start.16 = (f32[2,2,128,128]{3,2,1,0:T(8,128)S(1)}, f32[2,2,128,128]{3,2,1,0:T(8,128)S(1)}, u32[]{:S(2)}, u32[]{:S(2)}) collective-permute-start(f32[2,2,128,128]{3,2,1,0:T(8,128)S(1)} %get-tuple-element.84), channel_id=1, source_target_pairs={{0,4},{2,6},{4,8},{5,1},{6,10},{7,3},{8,12},{9,5},{10,14},{11,7},{... | collective-permute-start | bytes 786440 | tf_op jit(solution)/shard_map/ppermute | solution.py:331
  64.2 6.4 %collective-permute-start.19 = (f32[256,256]{1,0:T(8,128)S(1)}, f32[256,256]{1,0:T(8,128)S(1)}, u32[]{:S(2)}, u32[]{:S(2)}) collective-permute-start(f32[256,256]{1,0:T(8,128)S(1)} %shard_map.85.a), channel_id=1, source_target_pairs={{0,2},{1,5},{2,0},{3,7},{4,6},{5,1},{6,4},{7,3},{8,10},{9,13},{10,... | collective-permute-start | bytes 786440 | tf_op jit(solution)/shard_map/ppermute | solution.py:331
  67.9 4.6 %collective-permute-start.17 = (f32[512,256]{1,0:T(8,128)S(1)}, f32[512,256]{1,0:T(8,128)S(1)}, u32[]{:S(2)}, u32[]{:S(2)}) collective-permute-start(f32[512,256]{1,0:T(8,128)S(1)} %shard_map.83.refs_0_), channel_id=1, source_target_pairs={{0,1},{1,0},{2,3},{3,2},{4,5},{5,4},{6,7},{7,6},{8,9},{9,8},{10,11... | collective-permute-start | bytes 1572872 | tf_op jit(solution)/shard_map/ppermute | solution.py:331
  70.7 2.0 %collective-permute-start.20 = (f32[512,256]{1,0:T(8,128)S(1)}, f32[512,256]{1,0:T(8,128)S(1)}, u32[]{:S(2)}, u32[]{:S(2)}) collective-permute-start(f32[512,256]{1,0:T(8,128)S(1)} %shard_map.86.refs_1_), channel_id=1, source_target_pairs={{0,1},{1,0},{2,3},{3,2},{4,5},{5,4},{6,7},{7,6},{8,9},{9,8},{10,11... | collective-permute-start | bytes 1572872 | tf_op jit(solution)/shard_map/ppermute | solution.py:331
  (1 other events, 1.0 us)

commit v4 on v3

--- a/solution.py
+++ b/solution.py
@@ -77,8 +77,7 @@
 
 def mode_terms(ur, ui, probe_ref, mode, pr, pi, rows, cols):
     vr, vi = fold(dot(cols, ur), dot(cols, ui), 1)
-    g = dot(jnp.concatenate([vr, vi], 0), rows)
-    gr, gi = g[: g.shape[0] // 2], g[g.shape[0] // 2 :]
+    gr, gi = dot(vr, rows), dot(vi, rows)
     qr = probe_ref[mode, 0].astype(jnp.float32)
     qi = probe_ref[mode, 1].astype(jnp.float32)
     return (

time: 74 us -> 73.5 us (level)
  starting transfers between devices: 35.3 us -> 26.1 us
  waiting for transfers between devices: 20.9 us -> 26 us
  Pallas kernels: 13.7 us -> 16.7 us
    ppermute x21, starting transfers between devices: 35.3 us -> 26.1 us  [move(): return lax.ppermute(block, grid_axes, route(target))]
    ppermute x21, waiting for transfers between devices: 20.9 us -> 26 us  [move(): return lax.ppermute(block, grid_axes, route(target))]
    pallas_call x1, Pallas kernels: 5.49 us -> 7.66 us  [first_scans(): pl.pallas_call(functools.partial(first_kernel, blocks), out_shape=(share,...]
    pallas_call x1, Pallas kernels: 3.15 us -> 3.99 us  [second_scans(): pl.pallas_call(functools.partial(second_kernel, blocks), out_shape=(share...]
  transfers between devices with their start and end apart: 21 -> 21, of which waited for: 11 -> 13; matrix products, arithmetic and copies ran while one was open for 0% -> 0% of each run, Pallas kernels for 10% -> 11%
where the time goes in v4:
time: 73.5 us; the launch traced here: 72.5 us
  starting transfers between devices  26.1 us (36%)
  waiting for transfers between devices  26 us (35%)
  Pallas kernels  16.7 us (23%)
  local copies, waits for them, and re-layouts  2.17 us (3%)
  between operations  1.59 us (2%)
    ppermute x21, starting transfers between devices, move(): return lax.ppermute(block, grid_axes, route(target))  26.1 us
    ppermute x21, waiting for transfers between devices, move(): return lax.ppermute(block, grid_axes, route(target))  26 us
    pallas_call x1, Pallas kernels, first_scans(): pl.pallas_call(functools.partial(first_kernel, blocks), out_shape=(share,...  7.66 us
    pallas_call x1, Pallas kernels, second_scans(): pl.pallas_call(functools.partial(second_kernel, blocks), out_shape=(share...  3.99 us
    unnamed x10, local copies, waits for them, and re-layouts  2.07 us
    pallas_call x2, Pallas kernels, place_probe(): pl.pallas_call(body, out_shape=jax.ShapeDtypeStruct(shape, jnp.float32),...  2.05 us
    pallas_call x1, Pallas kernels, prepare(): pl.pallas_call(body, out_shape=(jax.ShapeDtypeStruct(probe.shape, jnp.bfl...  1.68 us
  transfers between devices with their start and end apart: 21, of which 13 were waited for; matrix products, arithmetic and copies ran while one was open for 0% of the time, Pallas kernels for 11%

profile of v4, /device:TPU:0, one launch (start us, length us, event | category | flops | bytes accessed | tf_op | source)
XLA Modules:
  0.0 72.5 jit_solution(13303644897245905352)
XLA Ops:
  0.6 1.0 %copy-done = f32[2,256,256]{2,1,0:T(8,128)S(1)} copy-done((f32[2,256,256]{2,1,0:T(8,128)S(1)}, f32[2,256,256]{2,1,0:T(8,128)}, u32[]{:S(2)}) %copy-start) | copy-done | bytes 524312
  1.8 5.1 %collective-permute-start = (f32[2,128,256]{2,1,0:T(8,128)S(1)}, f32[2,128,256]{2,1,0:T(8,128)S(1)}, u32[]{:S(2)}, u32[]{:S(2)}) collective-permute-start(f32[2,128,256]{2,1,0:T(8,128)S(1)} %get-tuple-element.45), channel_id=1, source_target_pairs={{0,4},{2,6},{4,8},{5,1},{6,10},{7,3},{8,12},{9,5},{10,14},{11,7},{... | collective-permute-start | bytes 786440 | tf_op jit(solution)/shard_map/ppermute | solution.py:330
  6.8 1.6 %collective-permute-start.1 = (f32[2,128,128]{2,1,0:T(8,128)S(1)}, f32[2,128,128]{2,1,0:T(8,128)S(1)}, u32[]{:S(2)}, u32[]{:S(2)}) collective-permute-start(f32[2,128,128]{2,1,0:T(8,128)S(1)} %get-tuple-element.46), channel_id=1, source_target_pairs={{0,2},{1,3},{2,0},{3,1},{4,6},{5,7},{6,4},{7,5},{8,10},{9,11},{10,... | collective-permute-start | bytes 393224 | tf_op jit(solution)/shard_map/ppermute | solution.py:330
  8.4 3.4 %collective-permute-start.2 = (f32[2,128,128]{2,1,0:T(8,128)S(1)}, f32[2,128,128]{2,1,0:T(8,128)S(1)}, u32[]{:S(2)}, u32[]{:S(2)}) collective-permute-start(f32[2,128,128]{2,1,0:T(8,128)S(1)} %get-tuple-element.47), channel_id=1, source_target_pairs={{0,6},{2,4},{4,10},{5,3},{6,8},{7,1},{8,14},{9,7},{10,12},{11,5},{... | collective-permute-start | bytes 393224 | tf_op jit(solution)/shard_map/ppermute | solution.py:330
  13.6 1.7 %shard_map.69 = (bf16[4,2,256,256]{3,2,1,0:T(8,128)(2,1)S(1)}, f32[3,256,256]{2,1,0:T(8,128)S(1)}, bf16[2,256,256]{2,1,0:T(8,128)(2,1)S(1)}) custom-call(bf16[4,2,256,256]{3,2,1,0:T(8,128)(2,1)} %probe_hbm.1, bf16[3,256,256]{2,1,0:T(8,128)(2,1)S(1)} %bitcast.13), custom_call_target="tpu_custom_call" | custom-call | flops 200000000 | bytes 4194304 | tf_op jit(solution)/shard_map/pallas_call | solution.py:253
  15.5 1.9 %collective-permute-done.3.other_ref = f32[2,128,512]{2,1,0:T(8,128)S(1)} collective-permute-done((f32[2,128,512]{2,1,0:T(8,128)S(1)}, f32[2,128,512]{2,1,0:T(8,128)S(1)}, u32[]{:S(2)}, u32[]{:S(2)}) %collective-permute-start.3) | collective-permute-done | bytes 524320 | tf_op jit(solution)/shard_map/ppermute | solution.py:330
  17.4 7.7 %shard_map.70 = (f32[512,256]{1,0:T(8,128)S(1)}, f32[512,256]{1,0:T(8,128)S(1)}, f32[3,2,256,256]{3,2,1,0:T(8,128)S(1)}, bf16[3,2,2,256,256]{4,3,2,1,0:T(8,128)(2,1)S(1)}, f32[3,2,256,256]{3,2,1,0:T(8,128)S(1)}) custom-call(s32[7]{0:T(128)S(1)} %stack.31.meta_ref, s32[2,3]{1,0:T(2,128)S(1)} %bitcast.14, f32[2,256,256]{2,1,0:T(8,128)S(1)} %copy-done.1, ...), custom_call_target="tpu_custom_call" | custom-call | flops 4000000000 | bytes 8388608 | tf_op jit(solution)/shard_map/pallas_call | solution.py:280
  25.1 4.0 %shard_map.71 = (f32[512,256]{1,0:T(8,128)S(1)}, f32[512,256]{1,0:T(8,128)S(1)}, f32[2,2,4,128,128]{4,3,2,1,0:T(8,128)S(1)}, f32[2,2,4,128,128]{4,3,2,1,0:T(8,128)S(1)}) custom-call(s32[7]{0:T(128)S(1)} %stack.31.meta_ref, s32[2,3]{1,0:T(2,128)S(1)} %bitcast.15, f32[2,256,256]{2,1,0:T(8,128)S(1)} %copy-done.1, ...), custom_call_target="tpu_custom_call" | custom-call | flops 2000000000 | bytes 8388608 | tf_op jit(solution)/shard_map/pallas_call | solution.py:303
  29.8 1.7 %collective-permute-start.11 = (f32[256,256]{1,0:T(8,128)S(1)}, f32[256,256]{1,0:T(8,128)S(1)}, u32[]{:S(2)}, u32[]{:S(2)}) collective-permute-start(f32[256,256]{1,0:T(8,128)S(1)} %get-tuple-element.81), channel_id=1, source_target_pairs={{0,2},{1,5},{2,0},{3,7},{4,6},{5,1},{6,4},{7,3},{8,10},{9,13},{10,... | collective-permute-start | bytes 786440 | tf_op jit(solution)/shard_map/ppermute | solution.py:330
  31.5 1.2 %collective-permute-done.6.b = f32[512,256]{1,0:T(8,128)S(1)} collective-permute-done((f32[512,256]{1,0:T(8,128)S(1)}, f32[512,256]{1,0:T(8,128)S(1)}, u32[]{:S(2)}, u32[]{:S(2)}) %collective-permute-start.6) | collective-permute-done | bytes 524320 | tf_op jit(solution)/shard_map/ppermute | solution.py:330
  32.7 1.7 %collective-permute-start.7 = (f32[256,256]{1,0:T(8,128)S(1)}, f32[256,256]{1,0:T(8,128)S(1)}, u32[]{:S(2)}, u32[]{:S(2)}) collective-permute-start(f32[256,256]{1,0:T(8,128)S(1)} %get-tuple-element.72), channel_id=1, source_target_pairs={{0,2},{1,5},{2,0},{3,7},{4,6},{5,1},{6,4},{7,3},{8,10},{9,13},{10,... | collective-permute-start | bytes 786440 | tf_op jit(solution)/shard_map/ppermute | solution.py:330
  34.4 1.8 %collective-permute-done.11.b = f32[256,256]{1,0:T(8,128)S(1)} collective-permute-done((f32[256,256]{1,0:T(8,128)S(1)}, f32[256,256]{1,0:T(8,128)S(1)}, u32[]{:S(2)}, u32[]{:S(2)}) %collective-permute-start.11) | collective-permute-done | bytes 262176 | tf_op jit(solution)/shard_map/ppermute | solution.py:330
  36.2 2.5 %collective-permute-start.12 = (f32[128,256]{1,0:T(8,128)S(1)}, f32[128,256]{1,0:T(8,128)S(1)}, u32[]{:S(2)}, u32[]{:S(2)}) collective-permute-start(f32[128,256]{1,0:T(8,128)S(1)} %get-tuple-element.83), channel_id=1, source_target_pairs={{0,4},{1,3},{2,6},{3,1},{4,0},{5,7},{6,2},{7,5},{8,12},{9,11},{10,... | collective-permute-start | bytes 393224 | tf_op jit(solution)/shard_map/ppermute | solution.py:330
  39.4 3.1 %collective-permute-start.8 = (f32[128,256]{1,0:T(8,128)S(1)}, f32[128,256]{1,0:T(8,128)S(1)}, u32[]{:S(2)}, u32[]{:S(2)}) collective-permute-start(f32[128,256]{1,0:T(8,128)S(1)} %get-tuple-element.74), channel_id=1, source_target_pairs={{0,4},{1,3},{2,6},{3,1},{4,0},{5,7},{6,2},{7,5},{8,12},{9,11},{10,... | collective-permute-start | bytes 393224 | tf_op jit(solution)/shard_map/ppermute | solution.py:330
  42.7 1.6 %collective-permute-start.13 = (f32[128,256]{1,0:T(8,128)S(1)}, f32[128,256]{1,0:T(8,128)S(1)}, u32[]{:S(2)}, u32[]{:S(2)}) collective-permute-start(f32[128,256]{1,0:T(8,128)S(1)} %shard_map.80.a), channel_id=1, source_target_pairs={{0,8},{1,9},{2,10},{3,11},{4,12},{5,13},{6,14},{7,15},{8,0},{9,1},... | collective-permute-start | bytes 393224 | tf_op jit(solution)/shard_map/ppermute | solution.py:330
  44.3 2.6 %collective-permute-done.8.b = f32[128,256]{1,0:T(8,128)S(1)} collective-permute-done((f32[128,256]{1,0:T(8,128)S(1)}, f32[128,256]{1,0:T(8,128)S(1)}, u32[]{:S(2)}, u32[]{:S(2)}) %collective-permute-start.8) | collective-permute-done | bytes 131104 | tf_op jit(solution)/shard_map/ppermute | solution.py:330
  47.0 7.5 %collective-permute-done.13.b = f32[128,256]{1,0:T(8,128)S(1)} collective-permute-done((f32[128,256]{1,0:T(8,128)S(1)}, f32[128,256]{1,0:T(8,128)S(1)}, u32[]{:S(2)}, u32[]{:S(2)}) %collective-permute-start.13) | collective-permute-done | bytes 131104 | tf_op jit(solution)/shard_map/ppermute | solution.py:330
  54.6 1.3 %collective-permute-done.9.b = f32[128,256]{1,0:T(8,128)S(1)} collective-permute-done((f32[128,256]{1,0:T(8,128)S(1)}, f32[128,256]{1,0:T(8,128)S(1)}, u32[]{:S(2)}, u32[]{:S(2)}) %collective-permute-start.9) | collective-permute-done | bytes 131104 | tf_op jit(solution)/shard_map/ppermute | solution.py:330
  56.7 3.5 %collective-permute-done.14.b = f32[128,256]{1,0:T(8,128)S(1)} collective-permute-done((f32[128,256]{1,0:T(8,128)S(1)}, f32[128,256]{1,0:T(8,128)S(1)}, u32[]{:S(2)}, u32[]{:S(2)}) %collective-permute-start.14) | collective-permute-done | bytes 131104 | tf_op jit(solution)/shard_map/ppermute | solution.py:330
  60.2 1.0 %collective-permute-start.15 = (f32[256,256]{1,0:T(8,128)S(1)}, f32[256,256]{1,0:T(8,128)S(1)}, u32[]{:S(2)}, u32[]{:S(2)}) collective-permute-start(f32[256,256]{1,0:T(8,128)S(1)} %shard_map.82.a), channel_id=1, source_target_pairs={{0,2},{1,5},{2,0},{3,7},{4,6},{5,1},{6,4},{7,3},{8,10},{9,13},{10,... | collective-permute-start | bytes 786440 | tf_op jit(solution)/shard_map/ppermute | solution.py:330
  61.3 1.6 %collective-permute-start.16 = (f32[2,2,128,128]{3,2,1,0:T(8,128)S(1)}, f32[2,2,128,128]{3,2,1,0:T(8,128)S(1)}, u32[]{:S(2)}, u32[]{:S(2)}) collective-permute-start(f32[2,2,128,128]{3,2,1,0:T(8,128)S(1)} %get-tuple-element.84), channel_id=1, source_target_pairs={{0,4},{2,6},{4,8},{5,1},{6,10},{7,3},{8,12},{9,5},{10,14},{11,7},{... | collective-permute-start | bytes 786440 | tf_op jit(solution)/shard_map/ppermute | solution.py:330
  63.0 1.1 %collective-permute-start.19 = (f32[256,256]{1,0:T(8,128)S(1)}, f32[256,256]{1,0:T(8,128)S(1)}, u32[]{:S(2)}, u32[]{:S(2)}) collective-permute-start(f32[256,256]{1,0:T(8,128)S(1)} %shard_map.85.a), channel_id=1, source_target_pairs={{0,2},{1,5},{2,0},{3,7},{4,6},{5,1},{6,4},{7,3},{8,10},{9,13},{10,... | collective-permute-start | bytes 786440 | tf_op jit(solution)/shard_map/ppermute | solution.py:330
  64.1 2.6 %collective-permute-done.15.b = f32[256,256]{1,0:T(8,128)S(1)} collective-permute-done((f32[256,256]{1,0:T(8,128)S(1)}, f32[256,256]{1,0:T(8,128)S(1)}, u32[]{:S(2)}, u32[]{:S(2)}) %collective-permute-start.15) | collective-permute-done | bytes 262176 | tf_op jit(solution)/shard_map/ppermute | solution.py:330
  66.9 2.6 %collective-permute-done.19.b = f32[256,256]{1,0:T(8,128)S(1)} collective-permute-done((f32[256,256]{1,0:T(8,128)S(1)}, f32[256,256]{1,0:T(8,128)S(1)}, u32[]{:S(2)}, u32[]{:S(2)}) %collective-permute-start.19) | collective-permute-done | bytes 262176 | tf_op jit(solution)/shard_map/ppermute | solution.py:330
  (51 shorter events, 7.3 us)
Async XLA Ops:
  0.6 1.0 %copy-start = (f32[2,256,256]{2,1,0:T(8,128)S(1)}, f32[2,256,256]{2,1,0:T(8,128)}, u32[]{:S(2)}) copy-start(f32[2,256,256]{2,1,0:T(8,128)} %tile_ref.5) | copy-start | bytes 1572868
  1.7 15.7 %copy-start.1 = (f32[2,256,256]{2,1,0:T(8,128)S(1)}, f32[2,256,256]{2,1,0:T(8,128)}, u32[]{:S(2)}) copy-start(f32[2,256,256]{2,1,0:T(8,128)} %tile_ref.5) | copy-start | bytes 1572868
  1.7 15.7 %copy-start.3 = (s32[1,1,3,2]{2,3,1,0:T(2,128)S(1)}, s32[1,1,3,2]{2,3,1,0:T(2,128)}, u32[]{:S(2)}) copy-start(s32[1,1,3,2]{2,3,1,0:T(2,128)} %param.8) | copy-start | bytes 76
  1.8 13.6 %collective-permute-start = (f32[2,128,256]{2,1,0:T(8,128)S(1)}, f32[2,128,256]{2,1,0:T(8,128)S(1)}, u32[]{:S(2)}, u32[]{:S(2)}) collective-permute-start(f32[2,128,256]{2,1,0:T(8,128)S(1)} %get-tuple-element.45), channel_id=1, source_target_pairs={{0,4},{2,6},{4,8},{5,1},{6,10},{7,3},{8,12},{9,5},{10,14},{11,7},{... | collective-permute-start | bytes 786440 | tf_op jit(solution)/shard_map/ppermute | solution.py:330
  6.8 8.5 %collective-permute-start.1 = (f32[2,128,128]{2,1,0:T(8,128)S(1)}, f32[2,128,128]{2,1,0:T(8,128)S(1)}, u32[]{:S(2)}, u32[]{:S(2)}) collective-permute-start(f32[2,128,128]{2,1,0:T(8,128)S(1)} %get-tuple-element.46), channel_id=1, source_target_pairs={{0,2},{1,3},{2,0},{3,1},{4,6},{5,7},{6,4},{7,5},{8,10},{9,11},{10,... | collective-permute-start | bytes 393224 | tf_op jit(solution)/shard_map/ppermute | solution.py:330
  8.4 6.9 %collective-permute-start.2 = (f32[2,128,128]{2,1,0:T(8,128)S(1)}, f32[2,128,128]{2,1,0:T(8,128)S(1)}, u32[]{:S(2)}, u32[]{:S(2)}) collective-permute-start(f32[2,128,128]{2,1,0:T(8,128)S(1)} %get-tuple-element.47), channel_id=1, source_target_pairs={{0,6},{2,4},{4,10},{5,3},{6,8},{7,1},{8,14},{9,7},{10,12},{11,5},{... | collective-permute-start | bytes 393224 | tf_op jit(solution)/shard_map/ppermute | solution.py:330
  15.4 2.0 %collective-permute-start.3 = (f32[2,128,512]{2,1,0:T(8,128)S(1)}, f32[2,128,512]{2,1,0:T(8,128)S(1)}, u32[]{:S(2)}, u32[]{:S(2)}) collective-permute-start(f32[2,128,512]{2,1,0:T(8,128)S(1)} %constant_dynamic-update-slice_fusion.mine_ref), channel_id=1, source_target_pairs={{0,1},{1,0},{2,3},{3,2},{4,5},{5,4},{6,7},{7,6},{8,9},{9,8},{10,11... | collective-permute-start | bytes 1572872 | tf_op jit(solution)/shard_map/ppermute | solution.py:330
  25.1 4.1 %collective-permute-start.4 = (f32[512,256]{1,0:T(8,128)S(1)}, f32[512,256]{1,0:T(8,128)S(1)}, u32[]{:S(2)}, u32[]{:S(2)}) collective-permute-start(f32[512,256]{1,0:T(8,128)S(1)} %get-tuple-element.58), channel_id=1, source_target_pairs={{0,1},{1,0},{2,3},{3,2},{4,5},{5,4},{6,7},{7,6},{8,9},{9,8},{10,11... | collective-permute-start | bytes 1572872 | tf_op jit(solution)/shard_map/ppermute | solution.py:330
  29.1 13.4 %collective-permute-start.5 = (f32[2,2,4,128,128]{4,3,2,1,0:T(8,128)S(1)}, f32[2,2,4,128,128]{4,3,2,1,0:T(8,128)S(1)}, u32[]{:S(2)}, u32[]{:S(2)}) collective-permute-start(f32[2,2,4,128,128]{4,3,2,1,0:T(8,128)S(1)} %get-tuple-element.67), channel_id=1, source_target_pairs={{0,1},{1,0},{2,3},{3,2},{4,5},{5,4},{6,7},{7,6},{8,9},{9,8},{10,11... | collective-permute-start | bytes 3145736 | tf_op jit(solution)/shard_map/ppermute | solution.py:330
  29.2 3.4 %collective-permute-start.6 = (f32[512,256]{1,0:T(8,128)S(1)}, f32[512,256]{1,0:T(8,128)S(1)}, u32[]{:S(2)}, u32[]{:S(2)}) collective-permute-start(f32[512,256]{1,0:T(8,128)S(1)} %get-tuple-element.70), channel_id=1, source_target_pairs={{0,1},{1,0},{2,3},{3,2},{4,5},{5,4},{6,7},{7,6},{8,9},{9,8},{10,11... | collective-permute-start | bytes 1572872 | tf_op jit(solution)/shard_map/ppermute | solution.py:330
  29.8 6.4 %collective-permute-start.11 = (f32[256,256]{1,0:T(8,128)S(1)}, f32[256,256]{1,0:T(8,128)S(1)}, u32[]{:S(2)}, u32[]{:S(2)}) collective-permute-start(f32[256,256]{1,0:T(8,128)S(1)} %get-tuple-element.81), channel_id=1, source_target_pairs={{0,2},{1,5},{2,0},{3,7},{4,6},{5,1},{6,4},{7,3},{8,10},{9,13},{10,... | collective-permute-start | bytes 786440 | tf_op jit(solution)/shard_map/ppermute | solution.py:330
  32.7 6.7 %collective-permute-start.7 = (f32[256,256]{1,0:T(8,128)S(1)}, f32[256,256]{1,0:T(8,128)S(1)}, u32[]{:S(2)}, u32[]{:S(2)}) collective-permute-start(f32[256,256]{1,0:T(8,128)S(1)} %get-tuple-element.72), channel_id=1, source_target_pairs={{0,2},{1,5},{2,0},{3,7},{4,6},{5,1},{6,4},{7,3},{8,10},{9,13},{10,... | collective-permute-start | bytes 786440 | tf_op jit(solution)/shard_map/ppermute | solution.py:330
  36.2 6.5 %collective-permute-start.12 = (f32[128,256]{1,0:T(8,128)S(1)}, f32[128,256]{1,0:T(8,128)S(1)}, u32[]{:S(2)}, u32[]{:S(2)}) collective-permute-start(f32[128,256]{1,0:T(8,128)S(1)} %get-tuple-element.83), channel_id=1, source_target_pairs={{0,4},{1,3},{2,6},{3,1},{4,0},{5,7},{6,2},{7,5},{8,12},{9,11},{10,... | collective-permute-start | bytes 393224 | tf_op jit(solution)/shard_map/ppermute | solution.py:330
  39.4 7.5 %collective-permute-start.8 = (f32[128,256]{1,0:T(8,128)S(1)}, f32[128,256]{1,0:T(8,128)S(1)}, u32[]{:S(2)}, u32[]{:S(2)}) collective-permute-start(f32[128,256]{1,0:T(8,128)S(1)} %get-tuple-element.74), channel_id=1, source_target_pairs={{0,4},{1,3},{2,6},{3,1},{4,0},{5,7},{6,2},{7,5},{8,12},{9,11},{10,... | collective-permute-start | bytes 393224 | tf_op jit(solution)/shard_map/ppermute | solution.py:330
  42.6 13.3 %collective-permute-start.10 = (f32[2,2,128,128]{3,2,1,0:T(8,128)S(1)}, f32[2,2,128,128]{3,2,1,0:T(8,128)S(1)}, u32[]{:S(2)}, u32[]{:S(2)}) collective-permute-start(f32[2,2,128,128]{3,2,1,0:T(8,128)S(1)} %get-tuple-element.75), channel_id=1, source_target_pairs={{0,2},{1,3},{2,0},{3,1},{4,6},{5,7},{6,4},{7,5},{8,10},{9,11},{10,... | collective-permute-start | bytes 786440 | tf_op jit(solution)/shard_map/ppermute | solution.py:330
  42.7 11.7 %collective-permute-start.13 = (f32[128,256]{1,0:T(8,128)S(1)}, f32[128,256]{1,0:T(8,128)S(1)}, u32[]{:S(2)}, u32[]{:S(2)}) collective-permute-start(f32[128,256]{1,0:T(8,128)S(1)} %shard_map.80.a), channel_id=1, source_target_pairs={{0,8},{1,9},{2,10},{3,11},{4,12},{5,13},{6,14},{7,15},{8,0},{9,1},... | collective-permute-start | bytes 393224 | tf_op jit(solution)/shard_map/ppermute | solution.py:330
  46.9 8.9 %collective-permute-start.9 = (f32[128,256]{1,0:T(8,128)S(1)}, f32[128,256]{1,0:T(8,128)S(1)}, u32[]{:S(2)}, u32[]{:S(2)}) collective-permute-start(f32[128,256]{1,0:T(8,128)S(1)} %shard_map.75.a), channel_id=1, source_target_pairs={{0,8},{1,9},{2,10},{3,11},{4,12},{5,13},{6,14},{7,15},{8,0},{9,1},... | collective-permute-start | bytes 393224 | tf_op jit(solution)/shard_map/ppermute | solution.py:330
  54.5 5.7 %collective-permute-start.14 = (f32[128,256]{1,0:T(8,128)S(1)}, f32[128,256]{1,0:T(8,128)S(1)}, u32[]{:S(2)}, u32[]{:S(2)}) collective-permute-start(f32[128,256]{1,0:T(8,128)S(1)} %shard_map.81.a), channel_id=1, source_target_pairs={{0,4},{1,3},{2,6},{3,1},{4,0},{5,7},{6,2},{7,5},{8,12},{9,11},{10,... | collective-permute-start | bytes 393224 | tf_op jit(solution)/shard_map/ppermute | solution.py:330
  55.9 7.1 %collective-permute-start.18 = (f32[128,256]{1,0:T(8,128)S(1)}, f32[128,256]{1,0:T(8,128)S(1)}, u32[]{:S(2)}, u32[]{:S(2)}) collective-permute-start(f32[128,256]{1,0:T(8,128)S(1)} %shard_map.76.a), channel_id=1, source_target_pairs={{0,4},{1,3},{2,6},{3,1},{4,0},{5,7},{6,2},{7,5},{8,12},{9,11},{10,... | collective-permute-start | bytes 393224 | tf_op jit(solution)/shard_map/ppermute | solution.py:330
  60.2 6.4 %collective-permute-start.15 = (f32[256,256]{1,0:T(8,128)S(1)}, f32[256,256]{1,0:T(8,128)S(1)}, u32[]{:S(2)}, u32[]{:S(2)}) collective-permute-start(f32[256,256]{1,0:T(8,128)S(1)} %shard_map.82.a), channel_id=1, source_target_pairs={{0,2},{1,5},{2,0},{3,7},{4,6},{5,1},{6,4},{7,3},{8,10},{9,13},{10,... | collective-permute-start | bytes 786440 | tf_op jit(solution)/shard_map/ppermute | solution.py:330
  61.3 5.5 %collective-permute-start.16 = (f32[2,2,128,128]{3,2,1,0:T(8,128)S(1)}, f32[2,2,128,128]{3,2,1,0:T(8,128)S(1)}, u32[]{:S(2)}, u32[]{:S(2)}) collective-permute-start(f32[2,2,128,128]{3,2,1,0:T(8,128)S(1)} %get-tuple-element.84), channel_id=1, source_target_pairs={{0,4},{2,6},{4,8},{5,1},{6,10},{7,3},{8,12},{9,5},{10,14},{11,7},{... | collective-permute-start | bytes 786440 | tf_op jit(solution)/shard_map/ppermute | solution.py:330
  63.0 6.4 %collective-permute-start.19 = (f32[256,256]{1,0:T(8,128)S(1)}, f32[256,256]{1,0:T(8,128)S(1)}, u32[]{:S(2)}, u32[]{:S(2)}) collective-permute-start(f32[256,256]{1,0:T(8,128)S(1)} %shard_map.85.a), channel_id=1, source_target_pairs={{0,2},{1,5},{2,0},{3,7},{4,6},{5,1},{6,4},{7,3},{8,10},{9,13},{10,... | collective-permute-start | bytes 786440 | tf_op jit(solution)/shard_map/ppermute | solution.py:330
  66.9 4.5 %collective-permute-start.17 = (f32[512,256]{1,0:T(8,128)S(1)}, f32[512,256]{1,0:T(8,128)S(1)}, u32[]{:S(2)}, u32[]{:S(2)}) collective-permute-start(f32[512,256]{1,0:T(8,128)S(1)} %shard_map.83.refs_0_), channel_id=1, source_target_pairs={{0,1},{1,0},{2,3},{3,2},{4,5},{5,4},{6,7},{7,6},{8,9},{9,8},{10,11... | collective-permute-start | bytes 1572872 | tf_op jit(solution)/shard_map/ppermute | solution.py:330
  69.5 2.0 %collective-permute-start.20 = (f32[512,256]{1,0:T(8,128)S(1)}, f32[512,256]{1,0:T(8,128)S(1)}, u32[]{:S(2)}, u32[]{:S(2)}) collective-permute-start(f32[512,256]{1,0:T(8,128)S(1)} %shard_map.86.refs_1_), channel_id=1, source_target_pairs={{0,1},{1,0},{2,3},{3,2},{4,5},{5,4},{6,7},{7,6},{8,9},{9,8},{10,11... | collective-permute-start | bytes 1572872 | tf_op jit(solution)/shard_map/ppermute | solution.py:330
  (1 other events, 1.0 us)

commit v5 on v4

--- a/solution.py
+++ b/solution.py
@@ -586,7 +586,7 @@
     below = move(down_part, lambda z, x, c: (down(z, c), x, c))
     for order in early[::-1]:
         parts = [stack(p, move(p, flip(order))) for p in parts]
-    parts[0], below = lax.optimization_barrier((parts[0], below))
+    parts[1], below = lax.optimization_barrier((parts[1], below))
     new_field = fold_finish(main, below)
     theirs = [swap_cores(p) for p in parts]
     new_probe = place_probe(parts, early, blocks, probe.shape, False)

time: 73.5 us -> 74.1 us (level)
  starting transfers between devices: 26.1 us -> 29 us
  waiting for transfers between devices: 26 us -> 24.4 us
    ppermute x21, starting transfers between devices: 26.1 us -> 29 us  [move(): return lax.ppermute(block, grid_axes, route(target))]
    ppermute x21, waiting for transfers between devices: 26 us -> 24.4 us  [move(): return lax.ppermute(block, grid_axes, route(target))]
  transfers between devices with their start and end apart: 21 -> 21, of which waited for: 13 -> 12; matrix products, arithmetic and copies ran while one was open for 0% -> 0% of each run, Pallas kernels for 11% -> 11%
where the time goes in v5:
time: 74.1 us; the launch traced here: 73.8 us
  starting transfers between devices  29 us (39%)
  waiting for transfers between devices  24.4 us (33%)
  Pallas kernels  16.7 us (23%)
  local copies, waits for them, and re-layouts  2.17 us (3%)
  between operations  1.57 us (2%)
    ppermute x21, starting transfers between devices, move(): return lax.ppermute(block, grid_axes, route(target))  29 us
    ppermute x21, waiting for transfers between devices, move(): return lax.ppermute(block, grid_axes, route(target))  24.4 us
    pallas_call x1, Pallas kernels, first_scans(): pl.pallas_call(functools.partial(first_kernel, blocks), out_shape=(share,...  7.68 us
    pallas_call x1, Pallas kernels, second_scans(): pl.pallas_call(functools.partial(second_kernel, blocks), out_shape=(share...  3.99 us
    pallas_call x2, Pallas kernels, place_probe(): pl.pallas_call(body, out_shape=jax.ShapeDtypeStruct(shape, jnp.float32),...  2.08 us
    unnamed x10, local copies, waits for them, and re-layouts  2.07 us
    pallas_call x1, Pallas kernels, prepare(): pl.pallas_call(body, out_shape=(jax.ShapeDtypeStruct(probe.shape, jnp.bfl...  1.68 us
  transfers between devices with their start and end apart: 21, of which 12 were waited for; matrix products, arithmetic and copies ran while one was open for 0% of the time, Pallas kernels for 11%

profile of v5, /device:TPU:0, one launch (start us, length us, event | category | flops | bytes accessed | tf_op | source)
XLA Modules:
  0.0 73.8 jit_solution(3460458266080432634)
XLA Ops:
  1.8 5.1 %collective-permute-start = (f32[2,128,256]{2,1,0:T(8,128)S(1)}, f32[2,128,256]{2,1,0:T(8,128)S(1)}, u32[]{:S(2)}, u32[]{:S(2)}) collective-permute-start(f32[2,128,256]{2,1,0:T(8,128)S(1)} %get-tuple-element.45), channel_id=1, source_target_pairs={{0,4},{2,6},{4,8},{5,1},{6,10},{7,3},{8,12},{9,5},{10,14},{11,7},{... | collective-permute-start | bytes 786440 | tf_op jit(solution)/shard_map/ppermute | solution.py:330
  6.8 1.6 %collective-permute-start.1 = (f32[2,128,128]{2,1,0:T(8,128)S(1)}, f32[2,128,128]{2,1,0:T(8,128)S(1)}, u32[]{:S(2)}, u32[]{:S(2)}) collective-permute-start(f32[2,128,128]{2,1,0:T(8,128)S(1)} %get-tuple-element.46), channel_id=1, source_target_pairs={{0,2},{1,3},{2,0},{3,1},{4,6},{5,7},{6,4},{7,5},{8,10},{9,11},{10,... | collective-permute-start | bytes 393224 | tf_op jit(solution)/shard_map/ppermute | solution.py:330
  8.4 3.4 %collective-permute-start.2 = (f32[2,128,128]{2,1,0:T(8,128)S(1)}, f32[2,128,128]{2,1,0:T(8,128)S(1)}, u32[]{:S(2)}, u32[]{:S(2)}) collective-permute-start(f32[2,128,128]{2,1,0:T(8,128)S(1)} %get-tuple-element.47), channel_id=1, source_target_pairs={{0,6},{2,4},{4,10},{5,3},{6,8},{7,1},{8,14},{9,7},{10,12},{11,5},{... | collective-permute-start | bytes 393224 | tf_op jit(solution)/shard_map/ppermute | solution.py:330
  13.6 1.7 %shard_map.69 = (bf16[4,2,256,256]{3,2,1,0:T(8,128)(2,1)S(1)}, f32[3,256,256]{2,1,0:T(8,128)S(1)}, bf16[2,256,256]{2,1,0:T(8,128)(2,1)S(1)}) custom-call(bf16[4,2,256,256]{3,2,1,0:T(8,128)(2,1)} %probe_hbm.1, bf16[3,256,256]{2,1,0:T(8,128)(2,1)S(1)} %bitcast.13), custom_call_target="tpu_custom_call" | custom-call | flops 200000000 | bytes 4194304 | tf_op jit(solution)/shard_map/pallas_call | solution.py:253
  15.5 1.9 %collective-permute-done.3.other_ref = f32[2,128,512]{2,1,0:T(8,128)S(1)} collective-permute-done((f32[2,128,512]{2,1,0:T(8,128)S(1)}, f32[2,128,512]{2,1,0:T(8,128)S(1)}, u32[]{:S(2)}, u32[]{:S(2)}) %collective-permute-start.3) | collective-permute-done | bytes 524320 | tf_op jit(solution)/shard_map/ppermute | solution.py:330
  17.4 7.7 %shard_map.70 = (f32[512,256]{1,0:T(8,128)S(1)}, f32[512,256]{1,0:T(8,128)S(1)}, f32[3,2,256,256]{3,2,1,0:T(8,128)S(1)}, bf16[3,2,2,256,256]{4,3,2,1,0:T(8,128)(2,1)S(1)}, f32[3,2,256,256]{3,2,1,0:T(8,128)S(1)}) custom-call(s32[7]{0:T(128)S(1)} %stack.31.meta_ref, s32[2,3]{1,0:T(2,128)S(1)} %bitcast.14, f32[2,256,256]{2,1,0:T(8,128)S(1)} %copy-done.1, ...), custom_call_target="tpu_custom_call" | custom-call | flops 4000000000 | bytes 8388608 | tf_op jit(solution)/shard_map/pallas_call | solution.py:280
  25.1 4.0 %shard_map.71 = (f32[512,256]{1,0:T(8,128)S(1)}, f32[512,256]{1,0:T(8,128)S(1)}, f32[2,2,4,128,128]{4,3,2,1,0:T(8,128)S(1)}, f32[2,2,4,128,128]{4,3,2,1,0:T(8,128)S(1)}) custom-call(s32[7]{0:T(128)S(1)} %stack.31.meta_ref, s32[2,3]{1,0:T(2,128)S(1)} %bitcast.15, f32[2,256,256]{2,1,0:T(8,128)S(1)} %copy-done.1, ...), custom_call_target="tpu_custom_call" | custom-call | flops 2000000000 | bytes 8388608 | tf_op jit(solution)/shard_map/pallas_call | solution.py:303
  29.8 1.7 %collective-permute-start.14 = (f32[256,256]{1,0:T(8,128)S(1)}, f32[256,256]{1,0:T(8,128)S(1)}, u32[]{:S(2)}, u32[]{:S(2)}) collective-permute-start(f32[256,256]{1,0:T(8,128)S(1)} %get-tuple-element.84), channel_id=1, source_target_pairs={{0,2},{1,5},{2,0},{3,7},{4,6},{5,1},{6,4},{7,3},{8,10},{9,13},{10,... | collective-permute-start | bytes 786440 | tf_op jit(solution)/shard_map/ppermute | solution.py:330
  31.4 1.2 %collective-permute-done.6.b = f32[512,256]{1,0:T(8,128)S(1)} collective-permute-done((f32[512,256]{1,0:T(8,128)S(1)}, f32[512,256]{1,0:T(8,128)S(1)}, u32[]{:S(2)}, u32[]{:S(2)}) %collective-permute-start.6) | collective-permute-done | bytes 524320 | tf_op jit(solution)/shard_map/ppermute | solution.py:330
  32.7 1.7 %collective-permute-start.7 = (f32[256,256]{1,0:T(8,128)S(1)}, f32[256,256]{1,0:T(8,128)S(1)}, u32[]{:S(2)}, u32[]{:S(2)}) collective-permute-start(f32[256,256]{1,0:T(8,128)S(1)} %get-tuple-element.72), channel_id=1, source_target_pairs={{0,2},{1,5},{2,0},{3,7},{4,6},{5,1},{6,4},{7,3},{8,10},{9,13},{10,... | collective-permute-start | bytes 786440 | tf_op jit(solution)/shard_map/ppermute | solution.py:330
  34.4 1.8 %collective-permute-done.14.b = f32[256,256]{1,0:T(8,128)S(1)} collective-permute-done((f32[256,256]{1,0:T(8,128)S(1)}, f32[256,256]{1,0:T(8,128)S(1)}, u32[]{:S(2)}, u32[]{:S(2)}) %collective-permute-start.14) | collective-permute-done | bytes 262176 | tf_op jit(solution)/shard_map/ppermute | solution.py:330
  36.2 2.4 %collective-permute-start.15 = (f32[128,256]{1,0:T(8,128)S(1)}, f32[128,256]{1,0:T(8,128)S(1)}, u32[]{:S(2)}, u32[]{:S(2)}) collective-permute-start(f32[128,256]{1,0:T(8,128)S(1)} %get-tuple-element.86), channel_id=1, source_target_pairs={{0,4},{1,3},{2,6},{3,1},{4,0},{5,7},{6,2},{7,5},{8,12},{9,11},{10,... | collective-permute-start | bytes 393224 | tf_op jit(solution)/shard_map/ppermute | solution.py:330
  39.4 3.1 %collective-permute-start.8 = (f32[128,256]{1,0:T(8,128)S(1)}, f32[128,256]{1,0:T(8,128)S(1)}, u32[]{:S(2)}, u32[]{:S(2)}) collective-permute-start(f32[128,256]{1,0:T(8,128)S(1)} %get-tuple-element.74), channel_id=1, source_target_pairs={{0,4},{1,3},{2,6},{3,1},{4,0},{5,7},{6,2},{7,5},{8,12},{9,11},{10,... | collective-permute-start | bytes 393224 | tf_op jit(solution)/shard_map/ppermute | solution.py:330
  43.4 1.5 %collective-permute-start.16 = (f32[128,256]{1,0:T(8,128)S(1)}, f32[128,256]{1,0:T(8,128)S(1)}, u32[]{:S(2)}, u32[]{:S(2)}) collective-permute-start(f32[128,256]{1,0:T(8,128)S(1)} %shard_map.83.a), channel_id=1, source_target_pairs={{0,8},{1,9},{2,10},{3,11},{4,12},{5,13},{6,14},{7,15},{8,0},{9,1},... | collective-permute-start | bytes 393224 | tf_op jit(solution)/shard_map/ppermute | solution.py:330
  44.9 1.6 %collective-permute-done.8.b = f32[128,256]{1,0:T(8,128)S(1)} collective-permute-done((f32[128,256]{1,0:T(8,128)S(1)}, f32[128,256]{1,0:T(8,128)S(1)}, u32[]{:S(2)}, u32[]{:S(2)}) %collective-permute-start.8) | collective-permute-done | bytes 131104 | tf_op jit(solution)/shard_map/ppermute | solution.py:330
  46.5 3.3 %collective-permute-start.9 = (f32[128,256]{1,0:T(8,128)S(1)}, f32[128,256]{1,0:T(8,128)S(1)}, u32[]{:S(2)}, u32[]{:S(2)}) collective-permute-start(f32[128,256]{1,0:T(8,128)S(1)} %shard_map.75.a), channel_id=1, source_target_pairs={{0,8},{1,9},{2,10},{3,11},{4,12},{5,13},{6,14},{7,15},{8,0},{9,1},... | collective-permute-start | bytes 393224 | tf_op jit(solution)/shard_map/ppermute | solution.py:330
  49.8 5.2 %collective-permute-done.16.b = f32[128,256]{1,0:T(8,128)S(1)} collective-permute-done((f32[128,256]{1,0:T(8,128)S(1)}, f32[128,256]{1,0:T(8,128)S(1)}, u32[]{:S(2)}, u32[]{:S(2)}) %collective-permute-start.16) | collective-permute-done | bytes 131104 | tf_op jit(solution)/shard_map/ppermute | solution.py:330
  55.1 1.3 %collective-permute-done.9.b = f32[128,256]{1,0:T(8,128)S(1)} collective-permute-done((f32[128,256]{1,0:T(8,128)S(1)}, f32[128,256]{1,0:T(8,128)S(1)}, u32[]{:S(2)}, u32[]{:S(2)}) %collective-permute-start.9) | collective-permute-done | bytes 131104 | tf_op jit(solution)/shard_map/ppermute | solution.py:330
  57.3 4.2 %collective-permute-done.17.b = f32[128,256]{1,0:T(8,128)S(1)} collective-permute-done((f32[128,256]{1,0:T(8,128)S(1)}, f32[128,256]{1,0:T(8,128)S(1)}, u32[]{:S(2)}, u32[]{:S(2)}) %collective-permute-start.17) | collective-permute-done | bytes 131104 | tf_op jit(solution)/shard_map/ppermute | solution.py:330
  62.1 2.2 %collective-permute-done.11.b = f32[128,256]{1,0:T(8,128)S(1)} collective-permute-done((f32[128,256]{1,0:T(8,128)S(1)}, f32[128,256]{1,0:T(8,128)S(1)}, u32[]{:S(2)}, u32[]{:S(2)}) %collective-permute-start.11) | collective-permute-done | bytes 131104 | tf_op jit(solution)/shard_map/ppermute | solution.py:330
  64.9 1.7 %collective-permute-start.13 = (f32[2,2,128,128]{3,2,1,0:T(8,128)S(1)}, f32[2,2,128,128]{3,2,1,0:T(8,128)S(1)}, u32[]{:S(2)}, u32[]{:S(2)}) collective-permute-start(f32[2,2,128,128]{3,2,1,0:T(8,128)S(1)} %get-tuple-element.79), channel_id=1, source_target_pairs={{0,4},{2,6},{4,8},{5,1},{6,10},{7,3},{8,12},{9,5},{10,14},{11,7},{... | collective-permute-start | bytes 786440 | tf_op jit(solution)/shard_map/ppermute | solution.py:330
  66.7 1.3 %collective-permute-done.18.b = f32[256,256]{1,0:T(8,128)S(1)} collective-permute-done((f32[256,256]{1,0:T(8,128)S(1)}, f32[256,256]{1,0:T(8,128)S(1)}, u32[]{:S(2)}, u32[]{:S(2)}) %collective-permute-start.18) | collective-permute-done | bytes 262176 | tf_op jit(solution)/shard_map/ppermute | solution.py:330
  68.1 2.7 %collective-permute-done.12.b = f32[256,256]{1,0:T(8,128)S(1)} collective-permute-done((f32[256,256]{1,0:T(8,128)S(1)}, f32[256,256]{1,0:T(8,128)S(1)}, u32[]{:S(2)}, u32[]{:S(2)}) %collective-permute-start.12) | collective-permute-done | bytes 262176 | tf_op jit(solution)/shard_map/ppermute | solution.py:330
  70.9 1.1 %shard_map.87.refs_2_ = f32[4,2,256,256]{3,2,1,0:T(8,128)} custom-call(f32[512,256]{1,0:T(8,128)S(1)} %shard_map.86.refs_0_, f32[512,256]{1,0:T(8,128)S(1)} %shard_map.79.refs_1_), custom_call_target="tpu_custom_call" | custom-call | flops 1000000 | bytes 2097152 | tf_op jit(solution)/shard_map/pallas_call | solution.py:529
  (51 shorter events, 8.9 us)
Async XLA Ops:
  0.6 1.0 %copy-start = (f32[2,256,256]{2,1,0:T(8,128)S(1)}, f32[2,256,256]{2,1,0:T(8,128)}, u32[]{:S(2)}) copy-start(f32[2,256,256]{2,1,0:T(8,128)} %tile_ref.5) | copy-start | bytes 1572868
  1.7 15.7 %copy-start.1 = (f32[2,256,256]{2,1,0:T(8,128)S(1)}, f32[2,256,256]{2,1,0:T(8,128)}, u32[]{:S(2)}) copy-start(f32[2,256,256]{2,1,0:T(8,128)} %tile_ref.5) | copy-start | bytes 1572868
  1.7 15.7 %copy-start.3 = (s32[1,1,3,2]{2,3,1,0:T(2,128)S(1)}, s32[1,1,3,2]{2,3,1,0:T(2,128)}, u32[]{:S(2)}) copy-start(s32[1,1,3,2]{2,3,1,0:T(2,128)} %param.8) | copy-start | bytes 76
  1.8 13.6 %collective-permute-start = (f32[2,128,256]{2,1,0:T(8,128)S(1)}, f32[2,128,256]{2,1,0:T(8,128)S(1)}, u32[]{:S(2)}, u32[]{:S(2)}) collective-permute-start(f32[2,128,256]{2,1,0:T(8,128)S(1)} %get-tuple-element.45), channel_id=1, source_target_pairs={{0,4},{2,6},{4,8},{5,1},{6,10},{7,3},{8,12},{9,5},{10,14},{11,7},{... | collective-permute-start | bytes 786440 | tf_op jit(solution)/shard_map/ppermute | solution.py:330
  6.8 8.5 %collective-permute-start.1 = (f32[2,128,128]{2,1,0:T(8,128)S(1)}, f32[2,128,128]{2,1,0:T(8,128)S(1)}, u32[]{:S(2)}, u32[]{:S(2)}) collective-permute-start(f32[2,128,128]{2,1,0:T(8,128)S(1)} %get-tuple-element.46), channel_id=1, source_target_pairs={{0,2},{1,3},{2,0},{3,1},{4,6},{5,7},{6,4},{7,5},{8,10},{9,11},{10,... | collective-permute-start | bytes 393224 | tf_op jit(solution)/shard_map/ppermute | solution.py:330
  8.4 6.9 %collective-permute-start.2 = (f32[2,128,128]{2,1,0:T(8,128)S(1)}, f32[2,128,128]{2,1,0:T(8,128)S(1)}, u32[]{:S(2)}, u32[]{:S(2)}) collective-permute-start(f32[2,128,128]{2,1,0:T(8,128)S(1)} %get-tuple-element.47), channel_id=1, source_target_pairs={{0,6},{2,4},{4,10},{5,3},{6,8},{7,1},{8,14},{9,7},{10,12},{11,5},{... | collective-permute-start | bytes 393224 | tf_op jit(solution)/shard_map/ppermute | solution.py:330
  15.4 2.0 %collective-permute-start.3 = (f32[2,128,512]{2,1,0:T(8,128)S(1)}, f32[2,128,512]{2,1,0:T(8,128)S(1)}, u32[]{:S(2)}, u32[]{:S(2)}) collective-permute-start(f32[2,128,512]{2,1,0:T(8,128)S(1)} %constant_dynamic-update-slice_fusion.mine_ref), channel_id=1, source_target_pairs={{0,1},{1,0},{2,3},{3,2},{4,5},{5,4},{6,7},{7,6},{8,9},{9,8},{10,11... | collective-permute-start | bytes 1572872 | tf_op jit(solution)/shard_map/ppermute | solution.py:330
  25.1 4.1 %collective-permute-start.4 = (f32[512,256]{1,0:T(8,128)S(1)}, f32[512,256]{1,0:T(8,128)S(1)}, u32[]{:S(2)}, u32[]{:S(2)}) collective-permute-start(f32[512,256]{1,0:T(8,128)S(1)} %get-tuple-element.58), channel_id=1, source_target_pairs={{0,1},{1,0},{2,3},{3,2},{4,5},{5,4},{6,7},{7,6},{8,9},{9,8},{10,11... | collective-permute-start | bytes 1572872 | tf_op jit(solution)/shard_map/ppermute | solution.py:330
  29.1 13.4 %collective-permute-start.5 = (f32[2,2,4,128,128]{4,3,2,1,0:T(8,128)S(1)}, f32[2,2,4,128,128]{4,3,2,1,0:T(8,128)S(1)}, u32[]{:S(2)}, u32[]{:S(2)}) collective-permute-start(f32[2,2,4,128,128]{4,3,2,1,0:T(8,128)S(1)} %get-tuple-element.67), channel_id=1, source_target_pairs={{0,1},{1,0},{2,3},{3,2},{4,5},{5,4},{6,7},{7,6},{8,9},{9,8},{10,11... | collective-permute-start | bytes 3145736 | tf_op jit(solution)/shard_map/ppermute | solution.py:330
  29.2 3.4 %collective-permute-start.6 = (f32[512,256]{1,0:T(8,128)S(1)}, f32[512,256]{1,0:T(8,128)S(1)}, u32[]{:S(2)}, u32[]{:S(2)}) collective-permute-start(f32[512,256]{1,0:T(8,128)S(1)} %get-tuple-element.70), channel_id=1, source_target_pairs={{0,1},{1,0},{2,3},{3,2},{4,5},{5,4},{6,7},{7,6},{8,9},{9,8},{10,11... | collective-permute-start | bytes 1572872 | tf_op jit(solution)/shard_map/ppermute | solution.py:330
  29.8 6.4 %collective-permute-start.14 = (f32[256,256]{1,0:T(8,128)S(1)}, f32[256,256]{1,0:T(8,128)S(1)}, u32[]{:S(2)}, u32[]{:S(2)}) collective-permute-start(f32[256,256]{1,0:T(8,128)S(1)} %get-tuple-element.84), channel_id=1, source_target_pairs={{0,2},{1,5},{2,0},{3,7},{4,6},{5,1},{6,4},{7,3},{8,10},{9,13},{10,... | collective-permute-start | bytes 786440 | tf_op jit(solution)/shard_map/ppermute | solution.py:330
  32.7 6.7 %collective-permute-start.7 = (f32[256,256]{1,0:T(8,128)S(1)}, f32[256,256]{1,0:T(8,128)S(1)}, u32[]{:S(2)}, u32[]{:S(2)}) collective-permute-start(f32[256,256]{1,0:T(8,128)S(1)} %get-tuple-element.72), channel_id=1, source_target_pairs={{0,2},{1,5},{2,0},{3,7},{4,6},{5,1},{6,4},{7,3},{8,10},{9,13},{10,... | collective-permute-start | bytes 786440 | tf_op jit(solution)/shard_map/ppermute | solution.py:330
  36.2 7.1 %collective-permute-start.15 = (f32[128,256]{1,0:T(8,128)S(1)}, f32[128,256]{1,0:T(8,128)S(1)}, u32[]{:S(2)}, u32[]{:S(2)}) collective-permute-start(f32[128,256]{1,0:T(8,128)S(1)} %get-tuple-element.86), channel_id=1, source_target_pairs={{0,4},{1,3},{2,6},{3,1},{4,0},{5,7},{6,2},{7,5},{8,12},{9,11},{10,... | collective-permute-start | bytes 393224 | tf_op jit(solution)/shard_map/ppermute | solution.py:330
  39.4 7.1 %collective-permute-start.8 = (f32[128,256]{1,0:T(8,128)S(1)}, f32[128,256]{1,0:T(8,128)S(1)}, u32[]{:S(2)}, u32[]{:S(2)}) collective-permute-start(f32[128,256]{1,0:T(8,128)S(1)} %get-tuple-element.74), channel_id=1, source_target_pairs={{0,4},{1,3},{2,6},{3,1},{4,0},{5,7},{6,2},{7,5},{8,12},{9,11},{10,... | collective-permute-start | bytes 393224 | tf_op jit(solution)/shard_map/ppermute | solution.py:330
  42.6 13.9 %collective-permute-start.10 = (f32[2,2,128,128]{3,2,1,0:T(8,128)S(1)}, f32[2,2,128,128]{3,2,1,0:T(8,128)S(1)}, u32[]{:S(2)}, u32[]{:S(2)}) collective-permute-start(f32[2,2,128,128]{3,2,1,0:T(8,128)S(1)} %get-tuple-element.75), channel_id=1, source_target_pairs={{0,2},{1,3},{2,0},{3,1},{4,6},{5,7},{6,4},{7,5},{8,10},{9,11},{10,... | collective-permute-start | bytes 786440 | tf_op jit(solution)/shard_map/ppermute | solution.py:330
  43.4 11.7 %collective-permute-start.16 = (f32[128,256]{1,0:T(8,128)S(1)}, f32[128,256]{1,0:T(8,128)S(1)}, u32[]{:S(2)}, u32[]{:S(2)}) collective-permute-start(f32[128,256]{1,0:T(8,128)S(1)} %shard_map.83.a), channel_id=1, source_target_pairs={{0,8},{1,9},{2,10},{3,11},{4,12},{5,13},{6,14},{7,15},{8,0},{9,1},... | collective-permute-start | bytes 393224 | tf_op jit(solution)/shard_map/ppermute | solution.py:330
  46.5 9.9 %collective-permute-start.9 = (f32[128,256]{1,0:T(8,128)S(1)}, f32[128,256]{1,0:T(8,128)S(1)}, u32[]{:S(2)}, u32[]{:S(2)}) collective-permute-start(f32[128,256]{1,0:T(8,128)S(1)} %shard_map.75.a), channel_id=1, source_target_pairs={{0,8},{1,9},{2,10},{3,11},{4,12},{5,13},{6,14},{7,15},{8,0},{9,1},... | collective-permute-start | bytes 393224 | tf_op jit(solution)/shard_map/ppermute | solution.py:330
  55.1 6.4 %collective-permute-start.17 = (f32[128,256]{1,0:T(8,128)S(1)}, f32[128,256]{1,0:T(8,128)S(1)}, u32[]{:S(2)}, u32[]{:S(2)}) collective-permute-start(f32[128,256]{1,0:T(8,128)S(1)} %shard_map.84.a), channel_id=1, source_target_pairs={{0,4},{1,3},{2,6},{3,1},{4,0},{5,7},{6,2},{7,5},{8,12},{9,11},{10,... | collective-permute-start | bytes 393224 | tf_op jit(solution)/shard_map/ppermute | solution.py:330
  56.5 7.8 %collective-permute-start.11 = (f32[128,256]{1,0:T(8,128)S(1)}, f32[128,256]{1,0:T(8,128)S(1)}, u32[]{:S(2)}, u32[]{:S(2)}) collective-permute-start(f32[128,256]{1,0:T(8,128)S(1)} %shard_map.76.a), channel_id=1, source_target_pairs={{0,4},{1,3},{2,6},{3,1},{4,0},{5,7},{6,2},{7,5},{8,12},{9,11},{10,... | collective-permute-start | bytes 393224 | tf_op jit(solution)/shard_map/ppermute | solution.py:330
  61.5 6.4 %collective-permute-start.18 = (f32[256,256]{1,0:T(8,128)S(1)}, f32[256,256]{1,0:T(8,128)S(1)}, u32[]{:S(2)}, u32[]{:S(2)}) collective-permute-start(f32[256,256]{1,0:T(8,128)S(1)} %shard_map.85.a), channel_id=1, source_target_pairs={{0,2},{1,5},{2,0},{3,7},{4,6},{5,1},{6,4},{7,3},{8,10},{9,13},{10,... | collective-permute-start | bytes 786440 | tf_op jit(solution)/shard_map/ppermute | solution.py:330
  64.3 6.4 %collective-permute-start.12 = (f32[256,256]{1,0:T(8,128)S(1)}, f32[256,256]{1,0:T(8,128)S(1)}, u32[]{:S(2)}, u32[]{:S(2)}) collective-permute-start(f32[256,256]{1,0:T(8,128)S(1)} %shard_map.78.a), channel_id=1, source_target_pairs={{0,2},{1,5},{2,0},{3,7},{4,6},{5,1},{6,4},{7,3},{8,10},{9,13},{10,... | collective-permute-start | bytes 786440 | tf_op jit(solution)/shard_map/ppermute | solution.py:330
  64.9 5.9 %collective-permute-start.13 = (f32[2,2,128,128]{3,2,1,0:T(8,128)S(1)}, f32[2,2,128,128]{3,2,1,0:T(8,128)S(1)}, u32[]{:S(2)}, u32[]{:S(2)}) collective-permute-start(f32[2,2,128,128]{3,2,1,0:T(8,128)S(1)} %get-tuple-element.79), channel_id=1, source_target_pairs={{0,4},{2,6},{4,8},{5,1},{6,10},{7,3},{8,12},{9,5},{10,14},{11,7},{... | collective-permute-start | bytes 786440 | tf_op jit(solution)/shard_map/ppermute | solution.py:330
  68.0 4.7 %collective-permute-start.19 = (f32[512,256]{1,0:T(8,128)S(1)}, f32[512,256]{1,0:T(8,128)S(1)}, u32[]{:S(2)}, u32[]{:S(2)}) collective-permute-start(f32[512,256]{1,0:T(8,128)S(1)} %shard_map.86.refs_0_), channel_id=1, source_target_pairs={{0,1},{1,0},{2,3},{3,2},{4,5},{5,4},{6,7},{7,6},{8,9},{9,8},{10,11... | collective-permute-start | bytes 1572872 | tf_op jit(solution)/shard_map/ppermute | solution.py:330
  70.8 2.0 %collective-permute-start.20 = (f32[512,256]{1,0:T(8,128)S(1)}, f32[512,256]{1,0:T(8,128)S(1)}, u32[]{:S(2)}, u32[]{:S(2)}) collective-permute-start(f32[512,256]{1,0:T(8,128)S(1)} %shard_map.79.refs_1_), channel_id=1, source_target_pairs={{0,1},{1,0},{2,3},{3,2},{4,5},{5,4},{6,7},{7,6},{8,9},{9,8},{10,11... | collective-permute-start | bytes 1572872 | tf_op jit(solution)/shard_map/ppermute | solution.py:330
  (1 other events, 1.0 us)
